TPU v7x, 512 devices: a whole 4x8x8 slice. The times are simulated.
512 devices in a mesh: segment: 8 (over x, core), dev: 64 (over z, y).
Axes of the slice: x: 4, y: 8, z: 8, core: 2. Of those that a mesh axis runs over, the one named last changes fastest.
Arguments:
- queries: bfloat16 [512, 8192], P(('segment', 'dev')), may hold values from -64 to 64
- page_ids: int32 [512, 4, 32], P(('segment', 'dev')), may hold values from 0 to 1023, as said below
- key_pages: bfloat16 [8192, 64, 128], P(('segment', 'dev')), may hold values from -6 to 6
- value_pages: bfloat16 [8192, 64, 128], P(('segment', 'dev')), may hold values from -6 to 6
- out_weight: bfloat16 [65536, 16384], P(('segment', 'dev')), may hold values from -0.1875 to 0.1875
Outputs:
- block_out: bfloat16 [512, 16384], P(('segment', 'dev'))
Inputs may be any that keep to these rules, and one draw needn't show every extreme that they name: `page_ids`: within the rows of one device (aligned blocks of 1 row), at most 4 of the entries name pages of one device (id // 16); in every section one such device, the same for all of its row blocks, is named exactly 4 times from each block. The 32 ids of one row and key head are distinct.
All inputs are finite; a program needn't handle non-finite values.
Results may differ from a plain program's by a relative error of at most 0.006.
Values may be sent and summed in bfloat16 or wider, within the bound.
No kernel may reach another device: no remote copies, remote signals or barrier semaphores. Data moves between devices by JAX's collectives and lax.ppermute only.
A program may use at most 64 MiB of HBM per device.

v0:
```python
import math

import jax
import jax.numpy as jnp
from jax import lax
from jax.sharding import PartitionSpec as P


def from_behind(value, axis, steps):
    count = lax.axis_size(axis)
    pairs = [(source, (source + steps) % count) for source in range(count)]
    return lax.ppermute(value, axis, pairs)


def request_layout(page_ids, pool_size, devices, capacity):
    owner_ids = (page_ids // pool_size).reshape(-1)
    slot_ids = (page_ids % pool_size).reshape(-1)
    onehot = (owner_ids[:, None] == jnp.arange(devices, dtype=jnp.int32)[None, :]).astype(jnp.int32)
    before = jnp.cumsum(onehot, axis=0) - onehot
    rank_ids = jnp.sum(before * onehot, axis=1)
    target = owner_ids * capacity + rank_ids
    slot_table = jnp.zeros((devices * capacity,), jnp.int32).at[target].set(slot_ids)
    return (target, slot_table.reshape(devices, capacity))


def page_partials(query_part, key_part, value_part, score_scale):
    scores = (
        jnp.einsum("...gd,...td->...gt", query_part, key_part, preferred_element_type=jnp.float32)
        * score_scale
    )
    page_max = jnp.max(scores, axis=-1)
    weights = jnp.exp(scores - page_max[..., None]).astype(jnp.bfloat16)
    weight_sum = jnp.sum(weights.astype(jnp.float32), axis=-1)
    partial_value = jnp.einsum(
        "...gt,...td->...gd", weights, value_part, preferred_element_type=jnp.float32
    )
    return (partial_value, page_max, weight_sum)


def local(queries, page_ids, key_pages, value_pages, out_weight):
    devices = lax.axis_size("dev")
    row_count = queries.shape[0]
    kv_heads = page_ids.shape[1]
    chosen = page_ids.shape[2]
    pool_size = key_pages.shape[0]
    page_tokens = key_pages.shape[1]
    head_dim = key_pages.shape[2]
    group_size = queries.shape[1] // (kv_heads * head_dim)
    capacity = 2 * row_count * kv_heads * chosen // devices
    score_scale = 1.0 / math.sqrt(head_dim)
    target, slot_table = request_layout(page_ids, pool_size, devices, capacity)
    grouped = queries.reshape(row_count, kv_heads, 1, group_size, head_dim)
    per_request = jnp.broadcast_to(grouped, (row_count, kv_heads, chosen, group_size, head_dim))
    per_request = per_request.reshape(-1, group_size, head_dim)
    asked_slots = lax.all_to_all(slot_table, "dev", split_axis=0, concat_axis=0, tiled=True)
    fetched_keys, fetched_values = (
        lax.all_to_all(key_pages[asked_slots], "dev", split_axis=0, concat_axis=0, tiled=True),
        lax.all_to_all(value_pages[asked_slots], "dev", split_axis=0, concat_axis=0, tiled=True),
    )
    request_keys = fetched_keys.reshape(devices * capacity, page_tokens, head_dim)[target]
    request_values = fetched_values.reshape(devices * capacity, page_tokens, head_dim)[target]
    partial_value, page_max, weight_sum = page_partials(
        per_request, request_keys, request_values, score_scale
    )
    request_shape = (row_count, kv_heads, chosen, group_size)
    page_max = page_max.reshape(request_shape)
    weight_sum = weight_sum.reshape(request_shape)
    partial_value = partial_value.reshape(request_shape + (head_dim,))
    highest = jnp.max(page_max, axis=2, keepdims=True)
    factor = jnp.exp(page_max - highest)
    numerator = jnp.sum(factor[..., None] * partial_value, axis=2)
    denominator = jnp.sum(factor * weight_sum, axis=2)
    attended = (numerator / denominator[..., None]).astype(jnp.bfloat16)
    attended = attended.reshape(row_count, devices, -1)
    by_heads = lax.all_to_all(attended, "dev", split_axis=1, concat_axis=0, tiled=True)
    by_heads = by_heads.reshape(row_count * devices, -1)
    projected = lax.psum_scatter(
        jnp.dot(by_heads, out_weight, preferred_element_type=jnp.float32),
        "dev",
        scatter_dimension=0,
        tiled=True,
    ).astype(jnp.bfloat16)
    return from_behind(projected, "segment", 1)


def solution(mesh):
    placed = (
        P(("segment", "dev"), None),
        P(("segment", "dev"), None, None),
        P(("segment", "dev"), None, None),
        P(("segment", "dev"), None, None),
        P(("segment", "dev"), None),
    )
    return jax.shard_map(
        local, mesh=mesh, in_specs=placed, out_specs=P(("segment", "dev"), None), check_vma=False
    )
```

profile of v0, /device:TPU:1, one launch (start us, length us, event | category | flops | bytes accessed | tf_op | source)
XLA Modules:
  0.0 664.7 jit_solution(18260836763687210046)
XLA Ops:
  0.0 0.0 copy-start
  0.0 0.7 broadcast_multiply_fusion
  0.7 0.1 eq.17
  0.8 0.1 fusion.3
  0.9 0.2 reduce_window_sum.11
  1.1 0.2 select_reduce_fusion
  1.3 0.1 mul.54
  1.3 0.1 reshape.241
  1.4 1.0 scatter_custom_fusion
  2.4 0.1 all_to_all.21
  2.5 27.8 %all_to_all.31 = s32[64,1,4]{2,1,0:T(1,128)S(1)} all-to-all(s32[64,1,4]{2,1,0:T(1,128)S(1)} %bitcast.42), channel_id=1, replica_groups=mesh['segment'=8,'dev'=64] {'dev'}, dimensions={0} | all-to-all | bytes 2048 | tf_op jit(solution)/shard_map/all_to_all | solution.py:55
  30.3 0.1 reshape.207
  30.4 0.0 copy-done
  30.5 3.1 gather_fusion
  33.5 0.0 copy-start.1
  33.5 5.8 all-to-all-start.1
  39.3 0.0 copy-done.1
  39.3 3.1 gather_fusion.2
  42.4 100.4 %all-to-all-done.1 = bf16[64,4,64,128]{3,2,1,0:T(8,128)(2,1)} async-done(((bf16[64,4,64,128]{3,2,1,0:T(8,128)(2,1)}), bf16[64,4,64,128]{3,2,1,0:T(8,128)(2,1)}, u32[]{:S(2)}, u32[]{:S(2)}) %all-to-all-start.1) | async-done | bytes 4194336 | tf_op jit(solution)/shard_map/all_to_all | solution.py:57
  142.8 0.0 copy-start.2
  142.8 37.4 %all-to-all-start.2 = ((bf16[64,4,64,128]{3,2,1,0:T(8,128)(2,1)}), bf16[64,4,64,128]{3,2,1,0:T(8,128)(2,1)}, u32[]{:S(2)}, u32[]{:S(2)}) async-start(bf16[64,4,64,128]{3,2,1,0:T(8,128)(2,1)} %bitcast.35), calls=%async_computation.2 | async-start | bytes 8388608 | tf_op jit(solution)/shard_map/all_to_all | solution.py:58
  180.2 0.0 copy-done.2
  180.2 0.1 reduce.3
  180.3 3.1 gather_fusion.1
  183.5 0.1 broadcast_in_dim.10
  183.6 1.3 fusion.11
  184.9 0.7 convert_reduce_fusion
  185.6 0.1 div.35
  185.7 95.0 %all-to-all-done.2 = bf16[64,4,64,128]{3,2,1,0:T(8,128)(2,1)} async-done(((bf16[64,4,64,128]{3,2,1,0:T(8,128)(2,1)}), bf16[64,4,64,128]{3,2,1,0:T(8,128)(2,1)}, u32[]{:S(2)}, u32[]{:S(2)}) %all-to-all-start.2) | async-done | bytes 4194336 | tf_op jit(solution)/shard_map/all_to_all | solution.py:58
  280.7 3.1 gather_fusion.3
  283.9 0.7 fusion.1
  284.6 0.3 multiply_reduce_fusion
  285.0 0.8 divide_convert_fusion
  285.7 29.6 %all-to-all-start.3 = ((bf16[1,64,128]{2,0,1:T(2,128)(2,1)}), bf16[1,64,128]{2,0,1:T(2,128)(2,1)S(1)}, u32[]{:S(2)}, u32[]{:S(2)}) async-start(bf16[1,64,128]{2,0,1:T(2,128)(2,1)} %divide_convert_fusion), calls=%async_computation.3 | async-start | bytes 65536 | tf_op jit(solution)/shard_map/all_to_all | solution.py:75
  315.3 1.3 dynamic-slice
  316.6 9.5 %all-to-all-done.3 = bf16[1,64,128]{2,0,1:T(2,128)(2,1)S(1)} async-done(((bf16[1,64,128]{2,0,1:T(2,128)(2,1)}), bf16[1,64,128]{2,0,1:T(2,128)(2,1)S(1)}, u32[]{:S(2)}, u32[]{:S(2)}) %all-to-all-start.3) | async-done | bytes 16416 | tf_op jit(solution)/shard_map/all_to_all | solution.py:75
  326.1 4.8 fusion.4
  330.9 272.3 %all-reduce.2 = bf16[64,16384]{1,0:T(8,128)(2,1)S(1)} all-reduce(f32[64,16384]{1,0:T(8,128)} %fusion.4), channel_id=2, replica_groups=mesh['segment'=8,'dev'=64] {'dev'}, use_global_device_ids=true, to_apply=%region_8.9.clone | all-reduce | flops 1048576 | bytes 6291456
  603.2 0.7 dynamic-slice_convert_fusion
  603.9 58.8 %collective-permute-start = (bf16[1,16384]{1,0:T(2,128)(2,1)S(1)}, bf16[1,16384]{1,0:T(2,128)(2,1)S(1)}, u32[]{:S(2)}, u32[]{:S(2)}) collective-permute-start(bf16[1,16384]{1,0:T(2,128)(2,1)S(1)} %dynamic-slice_convert_fusion), channel_id=1, source_target_pairs={{0,64},{64,128},{128,192},{192,256},{256,320},{320,384},{384,448},... | collective-permute-start | bytes 98312 | tf_op jit(solution)/shard_map/ppermute | solution.py:12
  662.7 1.3 collective-permute-done
  664.1 0.6 copy.16
  (7 shorter events, 0.1 us)
Async XLA Ops:
  0.0 30.4 %copy-start = (bf16[16,64,128]{2,1,0:T(8,128)(2,1)S(1)}, bf16[16,64,128]{2,1,0:T(8,128)(2,1)}, u32[]{:S(2)}) copy-start(bf16[16,64,128]{2,1,0:T(8,128)(2,1)} %param.7) | copy-start | bytes 786436
  33.5 5.8 copy-start.1
  33.5 109.3 %all-to-all-start.1 = ((bf16[64,4,64,128]{3,2,1,0:T(8,128)(2,1)}), bf16[64,4,64,128]{3,2,1,0:T(8,128)(2,1)}, u32[]{:S(2)}, u32[]{:S(2)}) async-start(bf16[64,4,64,128]{3,2,1,0:T(8,128)(2,1)} %bitcast.36), calls=%async_computation.1 | async-start | bytes 8388608 | tf_op jit(solution)/shard_map/all_to_all | solution.py:57
  142.8 37.4 %copy-start.2 = (bf16[1,8192]{1,0:T(2,128)(2,1)S(1)}, bf16[1,8192]{1,0:T(2,128)(2,1)}, u32[]{:S(2)}) copy-start(bf16[1,8192]{1,0:T(2,128)(2,1)} %param.5) | copy-start | bytes 49156
  142.8 137.9 %all-to-all-start.2 = ((bf16[64,4,64,128]{3,2,1,0:T(8,128)(2,1)}), bf16[64,4,64,128]{3,2,1,0:T(8,128)(2,1)}, u32[]{:S(2)}, u32[]{:S(2)}) async-start(bf16[64,4,64,128]{3,2,1,0:T(8,128)(2,1)} %bitcast.35), calls=%async_computation.2 | async-start | bytes 8388608 | tf_op jit(solution)/shard_map/all_to_all | solution.py:58
  285.7 40.4 %all-to-all-start.3 = ((bf16[1,64,128]{2,0,1:T(2,128)(2,1)}), bf16[1,64,128]{2,0,1:T(2,128)(2,1)S(1)}, u32[]{:S(2)}, u32[]{:S(2)}) async-start(bf16[1,64,128]{2,0,1:T(2,128)(2,1)} %divide_convert_fusion), calls=%async_computation.3 | async-start | bytes 65536 | tf_op jit(solution)/shard_map/all_to_all | solution.py:75
  603.9 60.1 %collective-permute-start = (bf16[1,16384]{1,0:T(2,128)(2,1)S(1)}, bf16[1,16384]{1,0:T(2,128)(2,1)S(1)}, u32[]{:S(2)}, u32[]{:S(2)}) collective-permute-start(bf16[1,16384]{1,0:T(2,128)(2,1)S(1)} %dynamic-slice_convert_fusion), channel_id=1, source_target_pairs={{0,64},{64,128},{128,192},{192,256},{256,320},{320,384},{384,448},... | collective-permute-start | bytes 98312 | tf_op jit(solution)/shard_map/ppermute | solution.py:12
where the time goes:
time: 665 us
  blocking collectives  300 us (45%)
  waiting for transfers between devices  206 us (31%)
  starting transfers between devices  132 us (20%)
  local copies, waits for them, and re-layouts  16.6 us (2%)
  matrix products  6.83 us (1%)
    unnamed x1, blocking collectives  272 us
    all_to_all x1, waiting for transfers between devices, local(): lax.all_to_all(key_pages[asked_slots], 'dev', split_axis=0, concat_axis=0...  100 us
    all_to_all x1, waiting for transfers between devices, local(): lax.all_to_all(value_pages[asked_slots], 'dev', split_axis=0, concat_axis...  95 us
    ppermute x1, starting transfers between devices, from_behind(): return lax.ppermute(value, axis, pairs)  58.8 us
    all_to_all x1, starting transfers between devices, local(): lax.all_to_all(value_pages[asked_slots], 'dev', split_axis=0, concat_axis...  37.4 us
    all_to_all x1, starting transfers between devices, local(): lax.all_to_all(attended, 'dev', split_axis=1, concat_axis=0, tiled=True)  29.6 us
    all_to_all x1, blocking collectives, local(): lax.all_to_all(slot_table, 'dev', split_axis=0, concat_axis=0, tiled=True)  27.8 us
  transfers between devices with their start and end apart: 4, of which 4 were waited for; matrix products, arithmetic and copies ran while one was open for 1% of the time, Pallas kernels for 0%

commit v1 on v0

v1 whole, which is shorter than its diff:
```python
import math

import jax
import jax.numpy as jnp
from jax import lax
from jax.experimental import pallas as pl
from jax.experimental.pallas import tpu as pltpu
from jax.sharding import PartitionSpec as P

BF = jnp.bfloat16
F32 = jnp.float32
HEADS = 64
GROUP = 16
KVH = 4
HD = 128
ROWS = 64
POOL = 16
TOKENS = 1024
SLAB = 72
BLOCK = 2048
LOG2E = math.log2(math.e)
SCALE = 1.0 / math.sqrt(HD)
FAR = float(2**20)
FLOOR = -8192.0


def iota(shape, dim):
    return lax.broadcasted_iota(jnp.int32, shape, dim)


def dot(a, b):
    return lax.dot_general(a, b, (((1,), (0,)), ((), ())), preferred_element_type=F32)


def dot_nt(a, b):
    return lax.dot_general(a, b, (((1,), (1,)), ((), ())), preferred_element_type=F32)


def one_if(condition):
    return jnp.where(condition, 1.0, 0.0).astype(BF)


def attend_kernel(me_ref, q_ref, k_ref, v_ref, out_ref, qs, kaug, vt, bias):
    me = me_ref[0].astype(F32)
    i, j = iota((256, 256), 0), iota((256, 256), 1)
    swap = one_if((j % 16) * 16 + j // 16 == i)
    for h in range(KVH):
        for c in range(4):
            part = q_ref[c * 16 : (c + 1) * 16, h * 16 : (h + 1) * 16, :]
            turned = dot(swap, part.reshape(256, HD)).astype(BF)
            for g in range(GROUP):
                row = (h * GROUP + g) * ROWS + c * 16
                qs[row : row + 16, :] = turned[g * 16 : (g + 1) * 16, :]
    i, j = iota((HD, HD), 0), iota((HD, HD), 1)
    vt[0:HD, :] = dot_nt(one_if(i == j), v_ref[...]).astype(BF)
    vt[HD : HD + 16, :] = jnp.ones((16, TOKENS), BF)
    token, lane = iota((TOKENS, HD), 0), iota((TOKENS, HD), 1)
    for h in range(KVH):
        kaug[h, :, 0:HD] = k_ref[...]
        kaug[h, :, HD : 2 * HD] = one_if(lane == h * POOL + token // 64)
    ids = q_ref[:, HEADS:SLAB, :].astype(F32).reshape(ROWS * 8, HD).astype(BF)
    i, j = iota((ROWS, ROWS * 8), 0), iota((ROWS, ROWS * 8), 1)
    owner = dot(one_if(j == i * 8), ids)
    slot = dot(one_if(j == i * 8 + 1), ids)
    slot = jnp.where(owner == me, slot, -1.0)
    i, j = iota((HD, HD), 0), iota((HD, HD), 1)
    count = jnp.zeros((ROWS, HD), F32)
    for page in range(POOL):
        count += dot(one_if(slot == float(page)), one_if(j == (i // 32) * POOL + page))
    bias[...] = jnp.where(count > 0.5, 0.0, -FAR).astype(BF)

    low = iota((1, HD), 1) < 64
    row8 = iota((8, HD), 0)

    def step(n, carry):
        h = n // 4
        q = qs[pl.ds(pl.multiple_of(n * 256, 256), 256), :]
        b = bias[...]
        qa = jnp.concatenate([q, jnp.concatenate([b, b, b, b], axis=0)], axis=1)
        s = dot_nt(kaug[h], qa)
        top = jnp.max(s, axis=0, keepdims=True) * SCALE
        point = jnp.maximum(top.astype(BF).astype(F32), FLOOR)
        p = jnp.exp2(s * (SCALE * LOG2E) - point * LOG2E).astype(BF)
        o = dot(vt[...], p)
        for pair in range(2):
            lanes = slice(pair * 128, (pair + 1) * 128)
            lo, hi = o[0:64, lanes], o[64:128, lanes]
            lo_turned, hi_turned = pltpu.roll(lo, 64, 1), pltpu.roll(hi, 64, 1)
            total = o[HD : HD + 1, lanes]
            total_hi = total.astype(BF).astype(F32)
            stats = jnp.where(
                row8 == 0,
                point[:, lanes],
                jnp.where(row8 == 1, total_hi, total - total_hi),
            )
            stats_turned = pltpu.roll(stats, 64, 1)
            head = n * 4 + pair * 2
            out_ref[head, 0:64, :] = jnp.where(low, lo, hi_turned).astype(BF)
            out_ref[head, 64:SLAB, :] = jnp.where(low, stats, stats_turned).astype(BF)
            out_ref[head + 1, 0:64, :] = jnp.where(low, lo_turned, hi).astype(BF)
            out_ref[head + 1, 64:SLAB, :] = jnp.where(low, stats_turned, stats).astype(BF)
        return carry

    lax.fori_loop(0, 16, step, 0)


def project_kernel(r_ref, w_ref, out_ref, att, tmp):
    @pl.when(pl.program_id(0) == 0)
    def _():
        stats = r_ref[:, 64:SLAB, :].astype(F32)
        top = jnp.max(stats, axis=0)
        factor = jnp.exp2((stats - top[None]) * LOG2E)
        den = jnp.zeros((1, HD), F32)
        acc = jnp.zeros((64, HD), F32)
        for src in range(ROWS):
            f = factor[src, 0:1, :]
            den += f * (stats[src, 1:2, :] + stats[src, 2:3, :])
            acc += f * r_ref[src, 0:64, :].astype(F32)
        both = acc / den
        tall = jnp.concatenate([both, pltpu.roll(both, 64, 1)], axis=0)
        att[...] = tall.T[0:ROWS, :].astype(BF)

    x = dot(att[...], w_ref[...])
    for cb in range(BLOCK // 128):
        tmp[pl.ds(cb, ROWS, stride=BLOCK // 128), :] = x[:, cb * 128 : (cb + 1) * 128]
    out_ref[...] = tmp[...].reshape(ROWS, BLOCK // 128, 128).astype(BF)


def attend(me, got, keys, values):
    return pl.pallas_call(
        attend_kernel,
        out_shape=jax.ShapeDtypeStruct((HEADS, SLAB, HD), BF),
        in_specs=[pl.BlockSpec(memory_space=pltpu.SMEM)] + [pl.BlockSpec(memory_space=pltpu.VMEM)] * 3,
        out_specs=pl.BlockSpec(memory_space=pltpu.VMEM),
        scratch_shapes=[
            pltpu.VMEM((HEADS * ROWS, HD), BF),
            pltpu.VMEM((KVH, TOKENS, 2 * HD), BF),
            pltpu.VMEM((HD + 16, TOKENS), BF),
            pltpu.VMEM((ROWS, HD), BF),
        ],
        compiler_params=pltpu.CompilerParams(vmem_limit_bytes=32 * 2**20),
        name="attend",
    )(me, got, keys, values)


def project(merged, weight):
    width = weight.shape[1]
    return pl.pallas_call(
        project_kernel,
        out_shape=jax.ShapeDtypeStruct((ROWS, width // 128, 128), BF),
        grid=(width // BLOCK,),
        in_specs=[
            pl.BlockSpec((ROWS, SLAB, HD), lambda n: (0, 0, 0)),
            pl.BlockSpec((HD, BLOCK), lambda n: (0, n)),
        ],
        out_specs=pl.BlockSpec((ROWS, BLOCK // 128, 128), lambda n: (0, n, 0)),
        scratch_shapes=[pltpu.VMEM((ROWS, HD), BF), pltpu.VMEM((ROWS * BLOCK // 128, 128), F32)],
        compiler_params=pltpu.CompilerParams(vmem_limit_bytes=32 * 2**20),
        name="project",
    )(merged, weight)


def exchange(value):
    return lax.all_to_all(value, "dev", split_axis=0, concat_axis=0, tiled=True)


def local(queries, page_ids, key_pages, value_pages, out_weight):
    count = lax.axis_size("segment")
    ids = page_ids.reshape(1, KVH * page_ids.shape[2])
    payload = jnp.concatenate(
        [
            queries.reshape(HEADS, HD),
            (ids // POOL).astype(BF),
            (ids % POOL).astype(BF),
            jnp.zeros((SLAB - HEADS - 2, HD), BF),
        ],
        axis=0,
    )
    got = exchange(jnp.broadcast_to(payload[None], (ROWS, SLAB, HD)))
    me = lax.axis_index("dev").astype(jnp.int32).reshape(1)
    partial = attend(me, got, key_pages.reshape(TOKENS, HD), value_pages.reshape(TOKENS, HD))
    sums = project(exchange(partial), out_weight)
    parts = exchange(sums)
    projected = jnp.sum(parts.astype(F32), axis=0).astype(BF)
    handed = lax.ppermute(projected, "segment", [(s, (s + 1) % count) for s in range(count)])
    return handed.reshape(1, -1)


def solution(mesh):
    placed = (
        P(("segment", "dev"), None),
        P(("segment", "dev"), None, None),
        P(("segment", "dev"), None, None),
        P(("segment", "dev"), None, None),
        P(("segment", "dev"), None),
    )
    return jax.shard_map(
        local, mesh=mesh, in_specs=placed, out_specs=P(("segment", "dev"), None), check_vma=False
    )
```

time: 665 us -> 173 us (0.26)
  blocking collectives: 300 us -> 93.6 us
  waiting for transfers between devices: 206 us -> 30.9 us
  starting transfers between devices: 132 us -> 23.6 us
  Pallas kernels: 0 us -> 20.6 us
  local copies, waits for them, and re-layouts: 16.6 us -> 2.69 us
  matrix products: 6.83 us -> 0 us
    unnamed x1 -> x0, blocking collectives: 272 us -> none
    all_to_all x3 -> x1, waiting for transfers between devices: 205 us -> 29.9 us  [exchange(): return lax.all_to_all(value, 'dev', split_axis=0, concat_axis=0, tiled=True)]
    all_to_all x1 -> x2, blocking collectives: 27.8 us -> 93.6 us  [exchange(): return lax.all_to_all(value, 'dev', split_axis=0, concat_axis=0, tiled=True)]
    all_to_all x3 -> x1, starting transfers between devices: 72.8 us -> 17.3 us  [exchange(): return lax.all_to_all(value, 'dev', split_axis=0, concat_axis=0, tiled=True)]
    ppermute x1, starting transfers between devices: 58.8 us -> 6.36 us  [local(): lax.ppermute(projected, 'segment', [(s, (s + 1) % count) for s in range(c...]
    pallas_call x0 -> x2, Pallas kernels: none -> 20.6 us  [the longest x1 17.1 us: attend(): pl.pallas_call(attend_kernel, out_shape=jax.ShapeDtypeStruct((HEADS, SLAB...]
    gather x4 -> x0, local copies, waits for them, and re-layouts: 12.4 us -> none  [the longest x1 3.14 us: local(): fetched_keys.reshape(devices * capacity, page_tokens, head_dim)[target]]
    dot_general x3 -> x0, matrix products: 6.83 us -> none  [the longest x1 4.82 us: local(): jnp.dot(by_heads, out_weight, preferred_element_type=jnp.float32)]
  transfers between devices with their start and end apart: 4 -> 2, of which waited for: 4 -> 2; matrix products, arithmetic and copies ran while one was open for 1% -> 0% of each run, Pallas kernels for 0% -> 0%
where the time goes in v1:
time: 173 us
  blocking collectives  93.6 us (54%)
  waiting for transfers between devices  30.9 us (18%)
  starting transfers between devices  23.6 us (14%)
  Pallas kernels  20.6 us (12%)
  local copies, waits for them, and re-layouts  2.69 us (2%)
    all_to_all x2, blocking collectives, exchange(): return lax.all_to_all(value, 'dev', split_axis=0, concat_axis=0, tiled=True)  93.6 us
    all_to_all x1, waiting for transfers between devices, exchange(): return lax.all_to_all(value, 'dev', split_axis=0, concat_axis=0, tiled=True)  29.9 us
    all_to_all x1, starting transfers between devices, exchange(): return lax.all_to_all(value, 'dev', split_axis=0, concat_axis=0, tiled=True)  17.3 us
    pallas_call x1, Pallas kernels, attend(): pl.pallas_call(attend_kernel, out_shape=jax.ShapeDtypeStruct((HEADS, SLAB...  17.1 us
    ppermute x1, starting transfers between devices, local(): lax.ppermute(projected, 'segment', [(s, (s + 1) % count) for s in range(c...  6.36 us
    pallas_call x1, Pallas kernels, project(): pl.pallas_call(project_kernel, out_shape=jax.ShapeDtypeStruct((ROWS, widt...  3.48 us
  transfers between devices with their start and end apart: 2, of which 2 were waited for; matrix products, arithmetic and copies ran while one was open for 0% of the time, Pallas kernels for 0%

profile of v1, /device:TPU:1, one launch (start us, length us, event | category | flops | bytes accessed | tf_op | source)
XLA Modules:
  0.0 172.8 jit_solution(1743752142909213227)
XLA Ops:
  0.0 0.8 reshape.169
  0.8 0.1 pad.3.clone
  0.9 0.8 reduce.1
  1.7 0.1 maximum_maximum_fusion
  1.8 1.2 broadcast_in_dim.10
  3.0 0.0 copy-start.1
  3.0 0.0 copy-start.2
  3.0 17.3 %all-to-all-start = ((bf16[64,72,128]{2,1,0:T(8,128)(2,1)}), bf16[64,72,128]{2,1,0:T(8,128)(2,1)S(1)}, u32[]{:S(2)}, u32[]{:S(2)}) async-start(bf16[64,72,128]{2,1,0:T(8,128)(2,1)} %broadcast_in_dim.10), calls=%async_computation | async-start | bytes 2359296 | tf_op jit(solution)/shard_map/all_to_all | solution.py:164
  20.2 29.9 %all-to-all-done.q_ref = bf16[64,72,128]{2,1,0:T(8,128)(2,1)S(1)} async-done(((bf16[64,72,128]{2,1,0:T(8,128)(2,1)}), bf16[64,72,128]{2,1,0:T(8,128)(2,1)S(1)}, u32[]{:S(2)}, u32[]{:S(2)}) %all-to-all-start) | async-done | bytes 1179680 | tf_op jit(solution)/shard_map/all_to_all | solution.py:164
  50.1 0.0 copy-done.1
  50.2 0.0 copy-done.2
  50.2 0.0 copy-start
  50.2 17.1 %attend.1 = bf16[64,72,128]{2,1,0:T(8,128)(2,1)S(1)} custom-call(s32[1]{0:T(128)} %bitcast.me_ref, bf16[64,72,128]{2,1,0:T(8,128)(2,1)S(1)} %all-to-all-done.q_ref, bf16[1024,128]{1,0:T(8,128)(2,1)S(1)} %bitcast.9, bf16[1024,128]{1,0:T(8,128)(2,1)S(1)} %bitcast.10), custom_call_target="tpu_custom_call" | custom-call | tf_op jit(solution)/shard_map/attend/pallas_call | solution.py:130
  67.3 37.0 %all_to_all.15.r_ref = bf16[64,72,128]{2,1,0:T(8,128)(2,1)S(1)} all-to-all(bf16[64,72,128]{2,1,0:T(8,128)(2,1)S(1)} %attend.1), channel_id=1, replica_groups=mesh['segment'=8,'dev'=64] {'dev'}, dimensions={0} | all-to-all | bytes 2359296 | tf_op jit(solution)/shard_map/all_to_all | solution.py:164
  104.3 0.0 copy-done
  104.3 3.5 %project.1 = bf16[64,128,128]{2,1,0:T(8,128)(2,1)S(1)} custom-call(bf16[64,72,128]{2,1,0:T(8,128)(2,1)S(1)} %all_to_all.15.r_ref, bf16[128,16384]{1,0:T(8,128)(2,1)S(1)} %copy-done), custom_call_target="tpu_custom_call" | custom-call | tf_op jit(solution)/shard_map/project/pallas_call | solution.py:148
  107.8 56.6 %all_to_all.16 = bf16[64,128,128]{2,1,0:T(8,128)(2,1)S(1)} all-to-all(bf16[64,128,128]{2,1,0:T(8,128)(2,1)S(1)} %project.1), channel_id=1, replica_groups=mesh['segment'=8,'dev'=64] {'dev'}, dimensions={0} | all-to-all | bytes 4194304 | tf_op jit(solution)/shard_map/all_to_all | solution.py:164
  164.4 0.3 reduce_sum.12
  164.7 6.4 %collective-permute-start = (bf16[128,128]{1,0:T(8,128)(2,1)S(1)}, bf16[128,128]{1,0:T(8,128)(2,1)S(1)}, u32[]{:S(2)}, u32[]{:S(2)}) collective-permute-start(bf16[128,128]{1,0:T(8,128)(2,1)S(1)} %reduce_sum.12), channel_id=1, source_target_pairs={{0,64},{64,128},{128,192},{192,256},{256,320},{320,384},{384,448},... | collective-permute-start | bytes 98312 | tf_op jit(solution)/shard_map/ppermute | solution.py:185
  171.1 1.0 collective-permute-done
  172.1 0.7 copy.8
  (2 shorter events, 0.0 us)
Async XLA Ops:
  3.0 47.2 %copy-start.1 = (bf16[16,64,128]{2,1,0:T(8,128)(2,1)S(1)}, bf16[16,64,128]{2,1,0:T(8,128)(2,1)}, u32[]{:S(2)}) copy-start(bf16[16,64,128]{2,1,0:T(8,128)(2,1)} %param.7) | copy-start | bytes 786436
  3.0 47.2 %copy-start.2 = (bf16[16,64,128]{2,1,0:T(8,128)(2,1)S(1)}, bf16[16,64,128]{2,1,0:T(8,128)(2,1)}, u32[]{:S(2)}) copy-start(bf16[16,64,128]{2,1,0:T(8,128)(2,1)} %param.8) | copy-start | bytes 786436
  3.0 47.2 %all-to-all-start = ((bf16[64,72,128]{2,1,0:T(8,128)(2,1)}), bf16[64,72,128]{2,1,0:T(8,128)(2,1)S(1)}, u32[]{:S(2)}, u32[]{:S(2)}) async-start(bf16[64,72,128]{2,1,0:T(8,128)(2,1)} %broadcast_in_dim.10), calls=%async_computation | async-start | bytes 2359296 | tf_op jit(solution)/shard_map/all_to_all | solution.py:164
  50.2 54.2 %copy-start = (bf16[128,16384]{1,0:T(8,128)(2,1)S(1)}, bf16[128,16384]{1,0:T(8,128)(2,1)}, u32[]{:S(2)}) copy-start(bf16[128,16384]{1,0:T(8,128)(2,1)} %w_ref.1) | copy-start | bytes 12582916
  164.7 7.4 %collective-permute-start = (bf16[128,128]{1,0:T(8,128)(2,1)S(1)}, bf16[128,128]{1,0:T(8,128)(2,1)S(1)}, u32[]{:S(2)}, u32[]{:S(2)}) collective-permute-start(bf16[128,128]{1,0:T(8,128)(2,1)S(1)} %reduce_sum.12), channel_id=1, source_target_pairs={{0,64},{64,128},{128,192},{192,256},{256,320},{320,384},{384,448},... | collective-permute-start | bytes 98312 | tf_op jit(solution)/shard_map/ppermute | solution.py:185

commit v2 on v1

--- a/solution.py
+++ b/solution.py
@@ -18,6 +18,7 @@
 TOKENS = 1024
 SLAB = 72
 BLOCK = 2048
+CHUNK = 1024
 LOG2E = math.log2(math.e)
 SCALE = 1.0 / math.sqrt(HD)
 FAR = float(2**20)
@@ -51,9 +52,8 @@
             for g in range(GROUP):
                 row = (h * GROUP + g) * ROWS + c * 16
                 qs[row : row + 16, :] = turned[g * 16 : (g + 1) * 16, :]
-    i, j = iota((HD, HD), 0), iota((HD, HD), 1)
-    vt[0:HD, :] = dot_nt(one_if(i == j), v_ref[...]).astype(BF)
-    vt[HD : HD + 16, :] = jnp.ones((16, TOKENS), BF)
+    vt[:, 0:HD] = v_ref[...]
+    vt[:, HD : 2 * HD] = one_if(iota((TOKENS, HD), 1) == 0)
     token, lane = iota((TOKENS, HD), 0), iota((TOKENS, HD), 1)
     for h in range(KVH):
         kaug[h, :, 0:HD] = k_ref[...]
@@ -71,37 +71,38 @@
 
     low = iota((1, HD), 1) < 64
     row8 = iota((8, HD), 0)
+    lane = iota((CHUNK, HD), 1)
+    per = CHUNK // ROWS
 
     def step(n, carry):
-        h = n // 4
-        q = qs[pl.ds(pl.multiple_of(n * 256, 256), 256), :]
+        h = n * per // GROUP
+        q = qs[pl.ds(pl.multiple_of(n * CHUNK, CHUNK), CHUNK), :]
         b = bias[...]
-        qa = jnp.concatenate([q, jnp.concatenate([b, b, b, b], axis=0)], axis=1)
-        s = dot_nt(kaug[h], qa)
-        top = jnp.max(s, axis=0, keepdims=True) * SCALE
+        qa = jnp.concatenate([q, jnp.concatenate([b] * per, axis=0)], axis=1)
+        s = dot_nt(qa, kaug[h])
+        top = jnp.max(s, axis=1, keepdims=True) * SCALE
         point = jnp.maximum(top.astype(BF).astype(F32), FLOOR)
         p = jnp.exp2(s * (SCALE * LOG2E) - point * LOG2E).astype(BF)
-        o = dot(vt[...], p)
-        for pair in range(2):
+        o = dot(p, vt[...])
+        total = o[:, HD : HD + 1]
+        total_hi = total.astype(BF).astype(F32)
+        stats = jnp.where(lane == 0, point, jnp.where(lane == 1, total_hi, total - total_hi))
+        ot = o[:, 0:HD].T
+        st = stats.T
+        for pair in range(per // 2):
             lanes = slice(pair * 128, (pair + 1) * 128)
-            lo, hi = o[0:64, lanes], o[64:128, lanes]
+            lo, hi = ot[0:64, lanes], ot[64:128, lanes]
             lo_turned, hi_turned = pltpu.roll(lo, 64, 1), pltpu.roll(hi, 64, 1)
-            total = o[HD : HD + 1, lanes]
-            total_hi = total.astype(BF).astype(F32)
-            stats = jnp.where(
-                row8 == 0,
-                point[:, lanes],
-                jnp.where(row8 == 1, total_hi, total - total_hi),
-            )
+            stats = st[0:8, lanes]
             stats_turned = pltpu.roll(stats, 64, 1)
-            head = n * 4 + pair * 2
+            head = n * per + pair * 2
             out_ref[head, 0:64, :] = jnp.where(low, lo, hi_turned).astype(BF)
             out_ref[head, 64:SLAB, :] = jnp.where(low, stats, stats_turned).astype(BF)
             out_ref[head + 1, 0:64, :] = jnp.where(low, lo_turned, hi).astype(BF)
             out_ref[head + 1, 64:SLAB, :] = jnp.where(low, stats_turned, stats).astype(BF)
         return carry
 
-    lax.fori_loop(0, 16, step, 0)
+    lax.fori_loop(0, HEADS * ROWS // CHUNK, step, 0)
 
 
 def project_kernel(r_ref, w_ref, out_ref, att, tmp):
@@ -129,13 +130,13 @@
 def attend(me, got, keys, values):
     return pl.pallas_call(
         attend_kernel,
-        out_shape=jax.ShapeDtypeStruct((HEADS, SLAB, HD), BF),
+        out_shape=pltpu.HBM((HEADS, SLAB, HD), BF),
         in_specs=[pl.BlockSpec(memory_space=pltpu.SMEM)] + [pl.BlockSpec(memory_space=pltpu.VMEM)] * 3,
         out_specs=pl.BlockSpec(memory_space=pltpu.VMEM),
         scratch_shapes=[
             pltpu.VMEM((HEADS * ROWS, HD), BF),
             pltpu.VMEM((KVH, TOKENS, 2 * HD), BF),
-            pltpu.VMEM((HD + 16, TOKENS), BF),
+            pltpu.VMEM((TOKENS, 2 * HD), BF),
             pltpu.VMEM((ROWS, HD), BF),
         ],
         compiler_params=pltpu.CompilerParams(vmem_limit_bytes=32 * 2**20),
@@ -147,7 +148,7 @@
     width = weight.shape[1]
     return pl.pallas_call(
         project_kernel,
-        out_shape=jax.ShapeDtypeStruct((ROWS, width // 128, 128), BF),
+        out_shape=pltpu.HBM((ROWS, width // 128, 128), BF),
         grid=(width // BLOCK,),
         in_specs=[
             pl.BlockSpec((ROWS, SLAB, HD), lambda n: (0, 0, 0)),

time: 173 us -> 173 us (level)
  no operation moved by 1% of the time
where the time goes in v2:
time: 173 us
  blocking collectives  94 us (54%)
  waiting for transfers between devices  30.9 us (18%)
  starting transfers between devices  23.6 us (14%)
  Pallas kernels  20.1 us (12%)
  local copies, waits for them, and re-layouts  2.69 us (2%)
    all_to_all x2, blocking collectives, exchange(): return lax.all_to_all(value, 'dev', split_axis=0, concat_axis=0, tiled=True)  94 us
    all_to_all x1, waiting for transfers between devices, exchange(): return lax.all_to_all(value, 'dev', split_axis=0, concat_axis=0, tiled=True)  29.9 us
    all_to_all x1, starting transfers between devices, exchange(): return lax.all_to_all(value, 'dev', split_axis=0, concat_axis=0, tiled=True)  17.3 us
    pallas_call x1, Pallas kernels, attend(): pl.pallas_call(attend_kernel, out_shape=pltpu.HBM((HEADS, SLAB, HD), BF),...  15 us
    ppermute x1, starting transfers between devices, local(): lax.ppermute(projected, 'segment', [(s, (s + 1) % count) for s in range(c...  6.3 us
    pallas_call x1, Pallas kernels, project(): pl.pallas_call(project_kernel, out_shape=pltpu.HBM((ROWS, width // 128, 1...  5.11 us
  transfers between devices with their start and end apart: 2, of which 2 were waited for; matrix products, arithmetic and copies ran while one was open for 0% of the time, Pallas kernels for 0%

profile of v2, /device:TPU:1, one launch (start us, length us, event | category | flops | bytes accessed | tf_op | source)
XLA Modules:
  0.0 172.7 jit_solution(8154415079631761212)
XLA Ops:
  0.0 0.8 reshape.169
  0.8 0.1 pad.3.clone
  0.9 0.8 reduce.1
  1.7 0.1 maximum_maximum_fusion
  1.8 1.2 broadcast_in_dim.10
  3.0 0.0 copy-start.1
  3.0 0.0 copy-start.2
  3.0 17.3 %all-to-all-start = ((bf16[64,72,128]{2,1,0:T(8,128)(2,1)}), bf16[64,72,128]{2,1,0:T(8,128)(2,1)S(1)}, u32[]{:S(2)}, u32[]{:S(2)}) async-start(bf16[64,72,128]{2,1,0:T(8,128)(2,1)} %broadcast_in_dim.10), calls=%async_computation | async-start | bytes 2359296 | tf_op jit(solution)/shard_map/all_to_all | solution.py:165
  20.2 29.9 %all-to-all-done.q_ref = bf16[64,72,128]{2,1,0:T(8,128)(2,1)S(1)} async-done(((bf16[64,72,128]{2,1,0:T(8,128)(2,1)}), bf16[64,72,128]{2,1,0:T(8,128)(2,1)S(1)}, u32[]{:S(2)}, u32[]{:S(2)}) %all-to-all-start) | async-done | bytes 1179680 | tf_op jit(solution)/shard_map/all_to_all | solution.py:165
  50.1 0.0 copy-done.1
  50.2 0.0 copy-done.2
  50.2 0.0 copy-start
  50.2 15.0 %attend.1 = bf16[64,72,128]{2,1,0:T(8,128)(2,1)} custom-call(s32[1]{0:T(128)} %bitcast.me_ref, bf16[64,72,128]{2,1,0:T(8,128)(2,1)S(1)} %all-to-all-done.q_ref, bf16[1024,128]{1,0:T(8,128)(2,1)S(1)} %bitcast.9, bf16[1024,128]{1,0:T(8,128)(2,1)S(1)} %bitcast.10), custom_call_target="tpu_custom_call" | custom-call | tf_op jit(solution)/shard_map/attend/pallas_call | solution.py:131
  65.2 37.2 %all_to_all.15.r_ref = bf16[64,72,128]{2,1,0:T(8,128)(2,1)S(1)} all-to-all(bf16[64,72,128]{2,1,0:T(8,128)(2,1)} %attend.1), channel_id=1, replica_groups=mesh['segment'=8,'dev'=64] {'dev'}, dimensions={0} | all-to-all | bytes 2359296 | tf_op jit(solution)/shard_map/all_to_all | solution.py:165
  102.4 0.0 copy-done
  102.4 5.1 %project.1 = bf16[64,128,128]{2,1,0:T(8,128)(2,1)} custom-call(bf16[64,72,128]{2,1,0:T(8,128)(2,1)S(1)} %all_to_all.15.r_ref, bf16[128,16384]{1,0:T(8,128)(2,1)S(1)} %copy-done), custom_call_target="tpu_custom_call" | custom-call | tf_op jit(solution)/shard_map/project/pallas_call | solution.py:149
  107.5 56.8 %all_to_all.16 = bf16[64,128,128]{2,1,0:T(8,128)(2,1)S(1)} all-to-all(bf16[64,128,128]{2,1,0:T(8,128)(2,1)} %project.1), channel_id=1, replica_groups=mesh['segment'=8,'dev'=64] {'dev'}, dimensions={0} | all-to-all | bytes 4194304 | tf_op jit(solution)/shard_map/all_to_all | solution.py:165
  164.3 0.3 reduce_sum.12
  164.6 6.3 %collective-permute-start = (bf16[128,128]{1,0:T(8,128)(2,1)S(1)}, bf16[128,128]{1,0:T(8,128)(2,1)S(1)}, u32[]{:S(2)}, u32[]{:S(2)}) collective-permute-start(bf16[128,128]{1,0:T(8,128)(2,1)S(1)} %reduce_sum.12), channel_id=1, source_target_pairs={{0,64},{64,128},{128,192},{192,256},{256,320},{320,384},{384,448},... | collective-permute-start | bytes 98312 | tf_op jit(solution)/shard_map/ppermute | solution.py:186
  170.9 1.0 collective-permute-done
  172.0 0.7 copy.8
  (2 shorter events, 0.0 us)
Async XLA Ops:
  3.0 47.2 %copy-start.1 = (bf16[16,64,128]{2,1,0:T(8,128)(2,1)S(1)}, bf16[16,64,128]{2,1,0:T(8,128)(2,1)}, u32[]{:S(2)}) copy-start(bf16[16,64,128]{2,1,0:T(8,128)(2,1)} %param.7) | copy-start | bytes 786436
  3.0 47.2 %copy-start.2 = (bf16[16,64,128]{2,1,0:T(8,128)(2,1)S(1)}, bf16[16,64,128]{2,1,0:T(8,128)(2,1)}, u32[]{:S(2)}) copy-start(bf16[16,64,128]{2,1,0:T(8,128)(2,1)} %param.8) | copy-start | bytes 786436
  3.0 47.2 %all-to-all-start = ((bf16[64,72,128]{2,1,0:T(8,128)(2,1)}), bf16[64,72,128]{2,1,0:T(8,128)(2,1)S(1)}, u32[]{:S(2)}, u32[]{:S(2)}) async-start(bf16[64,72,128]{2,1,0:T(8,128)(2,1)} %broadcast_in_dim.10), calls=%async_computation | async-start | bytes 2359296 | tf_op jit(solution)/shard_map/all_to_all | solution.py:165
  50.2 52.2 %copy-start = (bf16[128,16384]{1,0:T(8,128)(2,1)S(1)}, bf16[128,16384]{1,0:T(8,128)(2,1)}, u32[]{:S(2)}) copy-start(bf16[128,16384]{1,0:T(8,128)(2,1)} %w_ref.1) | copy-start | bytes 12582916
  164.6 7.3 %collective-permute-start = (bf16[128,128]{1,0:T(8,128)(2,1)S(1)}, bf16[128,128]{1,0:T(8,128)(2,1)S(1)}, u32[]{:S(2)}, u32[]{:S(2)}) collective-permute-start(bf16[128,128]{1,0:T(8,128)(2,1)S(1)} %reduce_sum.12), channel_id=1, source_target_pairs={{0,64},{64,128},{128,192},{192,256},{256,320},{320,384},{384,448},... | collective-permute-start | bytes 98312 | tf_op jit(solution)/shard_map/ppermute | solution.py:186

commit v3 on v2

v3 whole, which is shorter than its diff:
```python
import math

import jax
import jax.numpy as jnp
from jax import lax
from jax.experimental import pallas as pl
from jax.experimental.pallas import tpu as pltpu
from jax.sharding import PartitionSpec as P

BF = jnp.bfloat16
F32 = jnp.float32
HEADS = 64
GROUP = 16
KVH = 4
HD = 128
ROWS = 64
POOL = 16
TOKENS = 1024
SLAB = 72
PAGE = 64
SEL = 32
LINE = 8
BLOCK = 4096
CHUNK = 1024
LOG2E = math.log2(math.e)
SCALE = 1.0 / math.sqrt(HD)
FAR = float(2**20)
FLOOR = -8192.0


def iota(shape, dim):
    return lax.broadcasted_iota(jnp.int32, shape, dim)


def dot(a, b):
    return lax.dot_general(a, b, (((1,), (0,)), ((), ())), preferred_element_type=F32)


def dot_nt(a, b):
    return lax.dot_general(a, b, (((1,), (1,)), ((), ())), preferred_element_type=F32)


def one_if(condition):
    return jnp.where(condition, 1.0, 0.0).astype(BF)


def prepare_kernel(q_ref, id_ref, out_ref, tmp):
    for head in range(HEADS):
        tmp[head : head + 1, :] = q_ref[:, head * HD : (head + 1) * HD].astype(F32)
    ids = id_ref[...]
    tmp[HEADS:SLAB, :] = jnp.full((SLAB - HEADS, HD), -1.0, F32)
    tmp[HEADS : HEADS + KVH, 0:SEL] = (ids // POOL).astype(F32)
    tmp[HEADS + KVH : SLAB, 0:SEL] = (ids % POOL).astype(F32)
    slab = tmp[...].astype(BF)
    for copy in range(LINE):
        out_ref[copy, :, :] = slab


def attend_kernel(where_ref, q_ref, k_ref, v_ref, out_ref, qs, bias):
    me = where_ref[0].astype(F32)
    odd = where_ref[1]
    i, j = iota((256, 256), 0), iota((256, 256), 1)
    swap = one_if((j % 16) * 16 + j // 16 == i)
    for h in range(KVH):
        for c in range(4):
            part = q_ref[c * 16 : (c + 1) * 16, h * 16 : (h + 1) * 16, :]
            turned = dot(swap, part.reshape(256, HD)).astype(BF)
            for g in range(GROUP):
                row = (h * GROUP + g) * ROWS + c * 16
                qs[row : row + 16, :] = turned[g * 16 : (g + 1) * 16, :]
    ids = q_ref[:, HEADS:SLAB, :].astype(F32).reshape(ROWS * 8, HD).astype(BF)
    i, j = iota((KVH * ROWS, ROWS * 8), 0), iota((KVH * ROWS, ROWS * 8), 1)
    first = (i % ROWS) * 8 + i // ROWS
    owner = dot(one_if(j == first), ids)
    slot = dot(one_if(j == first + KVH), ids)
    slot = jnp.where(owner == me, slot, -1.0)
    j = iota((HD, HD), 1)
    count = jnp.zeros((KVH * ROWS, HD), F32)
    for page in range(POOL):
        count += dot(one_if(slot == float(page)), one_if(j == page))
    bias[...] = jnp.where(count > 0.5, 0.0, -FAR).astype(BF)

    low = iota((1, HD), 1) < 64
    lane = iota((CHUNK, HD), 1)
    per = CHUNK // ROWS
    page_of = one_if(iota((TOKENS, HD), 1) == iota((TOKENS, HD), 0) // PAGE)
    first_lane = one_if(iota((TOKENS, HD), 1) == 0)

    def step(n, carry):
        h = n * per // GROUP
        q = qs[pl.ds(pl.multiple_of(n * CHUNK, CHUNK), CHUNK), :]
        b = bias[pl.ds(pl.multiple_of(h * ROWS, ROWS), ROWS), :]
        qa = jnp.concatenate([q, jnp.concatenate([b] * per, axis=0)], axis=1)
        s = dot_nt(qa, jnp.concatenate([k_ref[...], page_of], axis=1))
        top = jnp.max(s, axis=1, keepdims=True) * SCALE
        point = jnp.maximum(top.astype(BF).astype(F32), FLOOR)
        p = jnp.exp2(s * (SCALE * LOG2E) - point * LOG2E).astype(BF)
        o = dot(p, jnp.concatenate([v_ref[...], first_lane], axis=1))
        total = o[:, HD : HD + 1]
        total_hi = total.astype(BF).astype(F32)
        stats = jnp.where(lane == 0, point, jnp.where(lane == 1, total_hi, total - total_hi))
        ot = o[:, 0:HD].T
        st = stats.T
        for pair in range(per // 2):
            lanes = slice(pair * 128, (pair + 1) * 128)
            lo, hi = ot[0:64, lanes], ot[64:128, lanes]
            lo_turned, hi_turned = pltpu.roll(lo, 64, 1), pltpu.roll(hi, 64, 1)
            stats = st[0:8, lanes]
            stats_turned = pltpu.roll(stats, 64, 1)
            head = n * per + pair * 2
            swapped = (head % LINE) * LINE + head // LINE
            even_at = jnp.where(odd == 1, head, swapped)
            odd_at = jnp.where(odd == 1, head + 1, swapped + LINE)
            out_ref[even_at, 0:64, :] = jnp.where(low, lo, hi_turned).astype(BF)
            out_ref[even_at, 64:SLAB, :] = jnp.where(low, stats, stats_turned).astype(BF)
            out_ref[odd_at, 0:64, :] = jnp.where(low, lo_turned, hi).astype(BF)
            out_ref[odd_at, 64:SLAB, :] = jnp.where(low, stats_turned, stats).astype(BF)
        return carry

    lax.fori_loop(0, HEADS * ROWS // CHUNK, step, 0)


def merged(slab_of):
    stats = [slab_of(src, slice(64, SLAB)).astype(F32) for src in range(LINE)]
    points = [s[0:1, :] for s in stats]
    top = points[0]
    for point in points[1:]:
        top = jnp.maximum(top, point)
    total = jnp.zeros((1, HD), F32)
    acc = jnp.zeros((64, HD), F32)
    for src in range(LINE):
        f = jnp.exp2((points[src] - top) * LOG2E)
        total += f * (stats[src][1:2, :] + stats[src][2:3, :])
        acc += f * slab_of(src, slice(0, 64)).astype(F32)
    return top, total, acc


def merge_kernel(r_ref, out_ref):
    row8 = iota((8, HD), 0)
    for head in range(LINE):
        top, total, acc = merged(lambda src, rows: r_ref[src, head, rows, :])
        total_hi = total.astype(BF).astype(F32)
        stats = jnp.where(row8 == 0, top, jnp.where(row8 == 1, total_hi, total - total_hi))
        out_ref[head, 0:64, :] = acc.astype(BF)
        out_ref[head, 64:SLAB, :] = stats.astype(BF)


def project_kernel(r_ref, w_ref, out_ref, att):
    @pl.when(pl.program_id(0) == 0)
    def _():
        top, total, acc = merged(lambda src, rows: r_ref[src, rows, :])
        both = acc / total
        tall = jnp.concatenate([both, pltpu.roll(both, 64, 1)], axis=0)
        att[...] = tall.T[0:ROWS, :].astype(BF)

    out_ref[...] = dot(att[...], w_ref[...]).astype(BF)


def add_kernel(x_ref, out_ref, tmp):
    tiles = tmp.shape[0] // LINE
    for tile in range(tiles):
        total = x_ref[0, :, tile * 128 : (tile + 1) * 128].astype(F32)
        for src in range(1, LINE):
            total += x_ref[src, :, tile * 128 : (tile + 1) * 128].astype(F32)
        tmp[pl.ds(tile, LINE, stride=tiles), :] = total
    out_ref[...] = tmp[...].reshape(LINE, tiles, 128).astype(BF)


VMEM = pl.BlockSpec(memory_space=pltpu.VMEM)
SMEM = pl.BlockSpec(memory_space=pltpu.SMEM)
PARAMS = pltpu.CompilerParams(vmem_limit_bytes=40 * 2**20)


def prepare(queries, ids):
    return pl.pallas_call(
        prepare_kernel,
        out_shape=jax.ShapeDtypeStruct((LINE, SLAB, HD), BF),
        in_specs=[VMEM, VMEM],
        out_specs=VMEM,
        scratch_shapes=[pltpu.VMEM((SLAB, HD), F32)],
        compiler_params=PARAMS,
        name="prepare",
    )(queries, ids)


def attend(place, got, keys, values):
    return pl.pallas_call(
        attend_kernel,
        out_shape=jax.ShapeDtypeStruct((HEADS, SLAB, HD), BF),
        in_specs=[SMEM, VMEM, VMEM, VMEM],
        out_specs=VMEM,
        scratch_shapes=[pltpu.VMEM((HEADS * ROWS, HD), BF), pltpu.VMEM((KVH * ROWS, HD), BF)],
        compiler_params=PARAMS,
        name="attend",
    )(place, got, keys, values)


def merge(parts):
    return pl.pallas_call(
        merge_kernel,
        out_shape=jax.ShapeDtypeStruct((LINE, SLAB, HD), BF),
        in_specs=[VMEM],
        out_specs=VMEM,
        compiler_params=PARAMS,
        name="merge",
    )(parts)


def project(parts, weight):
    width = weight.shape[1]
    return pl.pallas_call(
        project_kernel,
        out_shape=jax.ShapeDtypeStruct((ROWS, width), BF),
        grid=(width // BLOCK,),
        in_specs=[
            pl.BlockSpec((LINE, SLAB, HD), lambda n: (0, 0, 0)),
            pl.BlockSpec((HD, BLOCK), lambda n: (0, n)),
        ],
        out_specs=pl.BlockSpec((ROWS, BLOCK), lambda n: (0, n)),
        scratch_shapes=[pltpu.VMEM((ROWS, HD), BF)],
        compiler_params=PARAMS,
        name="project",
    )(parts, weight)


def add(parts):
    width = parts.shape[2]
    return pl.pallas_call(
        add_kernel,
        out_shape=jax.ShapeDtypeStruct((LINE, width // 128, 128), BF),
        in_specs=[VMEM],
        out_specs=VMEM,
        scratch_shapes=[pltpu.VMEM((LINE * width // 128, 128), F32)],
        compiler_params=PARAMS,
        name="add",
    )(parts)


def lines(sections, first):
    groups = []
    for section in range(sections):
        base = section * LINE * LINE
        along_y = (section % 2 == 0) == first
        for other in range(LINE):
            step, start = (1, other * LINE) if along_y else (LINE, other)
            groups.append([base + start + step * k for k in range(LINE)])
    return groups


def exchange(value, groups):
    return lax.all_to_all(
        value, ("segment", "dev"), split_axis=0, concat_axis=0, axis_index_groups=groups, tiled=True
    )


def local(queries, page_ids, key_pages, value_pages, out_weight):
    count = lax.axis_size("segment")
    one, other = lines(count, True), lines(count, False)
    place = jnp.stack([lax.axis_index("dev"), lax.axis_index("segment") % 2]).astype(jnp.int32)
    near = exchange(prepare(queries, page_ids.reshape(KVH, SEL)), one)
    got = exchange(jnp.broadcast_to(near[None], (LINE, LINE, SLAB, HD)), other)
    partial = attend(
        place,
        got.reshape(ROWS, SLAB, HD),
        key_pages.reshape(TOKENS, HD),
        value_pages.reshape(TOKENS, HD),
    )
    joined = merge(exchange(partial.reshape(LINE, LINE, SLAB, HD), one))
    sums = project(exchange(joined, other), out_weight)
    added = add(exchange(sums.reshape(LINE, LINE, -1), other))
    parts = exchange(added, one)
    projected = jnp.sum(parts.astype(F32), axis=0).astype(BF)
    handed = lax.ppermute(projected, "segment", [(s, (s + 1) % count) for s in range(count)])
    return handed.reshape(1, -1)


def solution(mesh):
    placed = (
        P(("segment", "dev"), None),
        P(("segment", "dev"), None, None),
        P(("segment", "dev"), None, None),
        P(("segment", "dev"), None, None),
        P(("segment", "dev"), None),
    )
    return jax.shard_map(
        local, mesh=mesh, in_specs=placed, out_specs=P(("segment", "dev"), None), check_vma=False
    )
```

time: 173 us -> 151 us (0.87)
  waiting for transfers between devices: 30.9 us -> 20.5 us
  starting transfers between devices: 23.6 us -> 15.6 us
  Pallas kernels: 20.1 us -> 16.9 us
    all_to_all x1, waiting for transfers between devices: 29.9 us -> 19.4 us  [exchange(): lax.all_to_all(value, ('segment', 'dev'), split_axis=0, concat_axis=0, ax...]
    all_to_all x1, starting transfers between devices: 17.3 us -> 6.95 us  [exchange(): lax.all_to_all(value, ('segment', 'dev'), split_axis=0, concat_axis=0, ax...]
    pallas_call x2 -> x5, Pallas kernels: 20.1 us -> 16.9 us  [the longest x1 14.3 us: attend(): pl.pallas_call(attend_kernel, out_shape=jax.ShapeDtypeStruct((HEADS, SLAB...]
    ppermute x1, starting transfers between devices: 6.3 us -> 8.64 us  [local(): lax.ppermute(projected, 'segment', [(s, (s + 1) % count) for s in range(c...]
    all_to_all x2 -> x5, blocking collectives: 94 us -> 94.3 us  [exchange(): lax.all_to_all(value, ('segment', 'dev'), split_axis=0, concat_axis=0, ax...]
where the time goes in v3:
time: 151 us
  blocking collectives  94.3 us (62%)
  waiting for transfers between devices  20.5 us (14%)
  Pallas kernels  16.9 us (11%)
  starting transfers between devices  15.6 us (10%)
  local copies, waits for them, and re-layouts  3.29 us (2%)
    all_to_all x5, blocking collectives, exchange(): lax.all_to_all(value, ('segment', 'dev'), split_axis=0, concat_axis=0, ax...  94.3 us
    all_to_all x1, waiting for transfers between devices, exchange(): lax.all_to_all(value, ('segment', 'dev'), split_axis=0, concat_axis=0, ax...  19.4 us
    pallas_call x1, Pallas kernels, attend(): pl.pallas_call(attend_kernel, out_shape=jax.ShapeDtypeStruct((HEADS, SLAB...  14.3 us
    ppermute x1, starting transfers between devices, local(): lax.ppermute(projected, 'segment', [(s, (s + 1) % count) for s in range(c...  8.64 us
    all_to_all x1, starting transfers between devices, exchange(): lax.all_to_all(value, ('segment', 'dev'), split_axis=0, concat_axis=0, ax...  6.95 us
  transfers between devices with their start and end apart: 2, of which 2 were waited for; matrix products, arithmetic and copies ran while one was open for 0% of the time, Pallas kernels for 0%

profile of v3, /device:TPU:1, one launch (start us, length us, event | category | flops | bytes accessed | tf_op | source)
XLA Modules:
  0.0 150.7 jit_solution(12710246928426084841)
XLA Ops:
  0.0 0.0 copy-start.3
  0.0 0.8 copy-done.3
  0.8 0.0 copy-start.4
  0.8 0.7 copy-done.4
  1.5 18.8 %all_to_all.30 = bf16[8,72,128]{2,1,0:T(8,128)(2,1)S(1)} all-to-all(bf16[8,72,128]{2,1,0:T(8,128)(2,1)S(1)} %prepare.1), channel_id=1, replica_groups={{0,1,2,3,4,5,6,7},{8,9,10,11,12,13,14,15},{16,17,18,19,20,21,22,23},{24..., dimensions={0} | all-to-all | bytes 294912 | tf_op jit(solution)/shard_map/all_to_all | solution.py:251
  20.2 1.2 broadcast_in_dim.2
  21.4 0.0 copy-start.1
  21.4 0.0 copy-start.2
  21.4 7.0 %all-to-all-start.1 = ((bf16[8,8,72,128]{3,2,1,0:T(8,128)(2,1)}), bf16[8,8,72,128]{3,2,1,0:T(8,128)(2,1)S(1)}, u32[]{:S(2)}, u32[]{:S(2)}) async-start(bf16[8,8,72,128]{3,2,1,0:T(8,128)(2,1)} %broadcast_in_dim.2), calls=%async_computation.1 | async-start | bytes 2359296 | tf_op jit(solution)/shard_map/all_to_all | solution.py:251
  28.4 0.1 pad_add_fusion.where_ref
  28.4 19.4 %all-to-all-done.1 = bf16[8,8,72,128]{3,2,1,0:T(8,128)(2,1)S(1)} async-done(((bf16[8,8,72,128]{3,2,1,0:T(8,128)(2,1)}), bf16[8,8,72,128]{3,2,1,0:T(8,128)(2,1)S(1)}, u32[]{:S(2)}, u32[]{:S(2)}) %all-to-all-start.1) | async-done | bytes 1179680 | tf_op jit(solution)/shard_map/all_to_all | solution.py:251
  47.9 0.0 copy-done.1
  47.9 0.0 copy-done.2
  47.9 0.0 copy-start
  47.9 14.3 %attend.1 = bf16[64,72,128]{2,1,0:T(8,128)(2,1)S(1)} custom-call(s32[2]{0:T(128)S(1)} %pad_add_fusion.where_ref, bf16[64,72,128]{2,1,0:T(8,128)(2,1)S(1)} %bitcast.14, bf16[1024,128]{1,0:T(8,128)(2,1)S(1)} %bitcast.16, bf16[1024,128]{1,0:T(8,128)(2,1)S(1)} %bitcast.17), custom_call_target="tpu_custom_call" | custom-call | tf_op jit(solution)/shard_map/attend/pallas_call | solution.py:187
  62.2 21.6 %all_to_all.31.r_ref = bf16[8,8,72,128]{3,2,1,0:T(8,128)(2,1)S(1)} all-to-all(bf16[8,8,72,128]{3,2,1,0:T(8,128)(2,1)S(1)} %bitcast.15), channel_id=1, replica_groups={{0,1,2,3,4,5,6,7},{8,9,10,11,12,13,14,15},{16,17,18,19,20,21,22,23},{24..., dimensions={0} | all-to-all | bytes 2359296 | tf_op jit(solution)/shard_map/all_to_all | solution.py:251
  83.7 0.4 merge.1
  84.1 10.5 %all_to_all.32.r_ref = bf16[8,72,128]{2,1,0:T(8,128)(2,1)S(1)} all-to-all(bf16[8,72,128]{2,1,0:T(8,128)(2,1)S(1)} %merge.1), channel_id=1, replica_groups={{0,8,16,24,32,40,48,56},{1,9,17,25,33,41,49,57},{2,10,18,26,34,42,50,58..., dimensions={0} | all-to-all | bytes 294912 | tf_op jit(solution)/shard_map/all_to_all | solution.py:251
  94.6 0.0 copy-done
  94.6 1.8 %project.1 = bf16[64,16384]{1,0:T(8,128)(2,1)S(1)} custom-call(bf16[8,72,128]{2,1,0:T(8,128)(2,1)S(1)} %all_to_all.32.r_ref, bf16[128,16384]{1,0:T(8,128)(2,1)S(1)} %copy-done), custom_call_target="tpu_custom_call" | custom-call | tf_op jit(solution)/shard_map/project/pallas_call | solution.py:211
  96.4 31.7 %all_to_all.33.x_ref = bf16[8,8,16384]{2,1,0:T(8,128)(2,1)S(1)} all-to-all(bf16[8,8,16384]{2,1,0:T(8,128)(2,1)S(1)} %bitcast.13), channel_id=1, replica_groups={{0,8,16,24,32,40,48,56},{1,9,17,25,33,41,49,57},{2,10,18,26,34,42,50,58..., dimensions={0} | all-to-all | bytes 4194304 | tf_op jit(solution)/shard_map/all_to_all | solution.py:251
  128.2 0.4 add.8
  128.5 11.7 %all_to_all.34 = bf16[8,128,128]{2,1,0:T(8,128)(2,1)S(1)} all-to-all(bf16[8,128,128]{2,1,0:T(8,128)(2,1)S(1)} %add.8), channel_id=1, replica_groups={{0,1,2,3,4,5,6,7},{8,9,10,11,12,13,14,15},{16,17,18,19,20,21,22,23},{24..., dimensions={0} | all-to-all | bytes 524288 | tf_op jit(solution)/shard_map/all_to_all | solution.py:251
  140.3 8.6 %collective-permute-start = (bf16[128,128]{1,0:T(8,128)(2,1)S(1)}, bf16[128,128]{1,0:T(8,128)(2,1)S(1)}, u32[]{:S(2)}, u32[]{:S(2)}) collective-permute-start(bf16[128,128]{1,0:T(8,128)(2,1)S(1)} %reduce_sum.12), channel_id=1, source_target_pairs={{0,64},{64,128},{128,192},{192,256},{256,320},{320,384},{384,448},... | collective-permute-start | bytes 98312 | tf_op jit(solution)/shard_map/ppermute | solution.py:273
  149.0 1.0 collective-permute-done
  150.0 0.7 copy.8
  (2 shorter events, 0.1 us)
Async XLA Ops:
  0.0 0.8 copy-start.3
  0.8 0.7 copy-start.4
  21.4 26.5 %copy-start.1 = (bf16[16,64,128]{2,1,0:T(8,128)(2,1)S(1)}, bf16[16,64,128]{2,1,0:T(8,128)(2,1)}, u32[]{:S(2)}) copy-start(bf16[16,64,128]{2,1,0:T(8,128)(2,1)} %param.7) | copy-start | bytes 786436
  21.4 26.5 %copy-start.2 = (bf16[16,64,128]{2,1,0:T(8,128)(2,1)S(1)}, bf16[16,64,128]{2,1,0:T(8,128)(2,1)}, u32[]{:S(2)}) copy-start(bf16[16,64,128]{2,1,0:T(8,128)(2,1)} %param.8) | copy-start | bytes 786436
  21.4 26.5 %all-to-all-start.1 = ((bf16[8,8,72,128]{3,2,1,0:T(8,128)(2,1)}), bf16[8,8,72,128]{3,2,1,0:T(8,128)(2,1)S(1)}, u32[]{:S(2)}, u32[]{:S(2)}) async-start(bf16[8,8,72,128]{3,2,1,0:T(8,128)(2,1)} %broadcast_in_dim.2), calls=%async_computation.1 | async-start | bytes 2359296 | tf_op jit(solution)/shard_map/all_to_all | solution.py:251
  47.9 46.7 %copy-start = (bf16[128,16384]{1,0:T(8,128)(2,1)S(1)}, bf16[128,16384]{1,0:T(8,128)(2,1)}, u32[]{:S(2)}) copy-start(bf16[128,16384]{1,0:T(8,128)(2,1)} %w_ref.1) | copy-start | bytes 12582916
  140.3 9.7 %collective-permute-start = (bf16[128,128]{1,0:T(8,128)(2,1)S(1)}, bf16[128,128]{1,0:T(8,128)(2,1)S(1)}, u32[]{:S(2)}, u32[]{:S(2)}) collective-permute-start(bf16[128,128]{1,0:T(8,128)(2,1)S(1)} %reduce_sum.12), channel_id=1, source_target_pairs={{0,64},{64,128},{128,192},{192,256},{256,320},{320,384},{384,448},... | collective-permute-start | bytes 98312 | tf_op jit(solution)/shard_map/ppermute | solution.py:273

commit v4 on v3

v4 whole, which is shorter than its diff:
```python
import functools
import math

import jax
import jax.numpy as jnp
from jax import lax
from jax.experimental import pallas as pl
from jax.experimental.pallas import tpu as pltpu
from jax.sharding import PartitionSpec as P

BF = jnp.bfloat16
F32 = jnp.float32
HEADS = 64
GROUP = 16
KVH = 4
HD = 128
ROWS = 64
POOL = 16
TOKENS = 1024
SLAB = 72
PAGE = 64
SEL = 32
LINE = 8
SHARE = 4
SPAN = LINE // SHARE
OWN = ROWS // SHARE
BLOCK = 4096
CHUNK = 512
LOG2E = math.log2(math.e)
SCALE = 1.0 / math.sqrt(HD)
FAR = float(2**20)
FLOOR = -8192.0


def iota(shape, dim):
    return lax.broadcasted_iota(jnp.int32, shape, dim)


def dot(a, b):
    return lax.dot_general(a, b, (((1,), (0,)), ((), ())), preferred_element_type=F32)


def dot_nt(a, b):
    return lax.dot_general(a, b, (((1,), (1,)), ((), ())), preferred_element_type=F32)


def one_if(condition):
    return jnp.where(condition, 1.0, 0.0).astype(BF)


def prepare_kernel(q_hbm, id_hbm, out_ref, q_ref, id_ref, tmp, sems):
    q_copy = pltpu.make_async_copy(q_hbm, q_ref, sems.at[0])
    id_copy = pltpu.make_async_copy(id_hbm, id_ref, sems.at[1])
    q_copy.start()
    id_copy.start()
    q_copy.wait()
    id_copy.wait()
    for head in range(HEADS):
        tmp[head : head + 1, :] = q_ref[:, head * HD : (head + 1) * HD].astype(F32)
    ids = id_ref[...]
    tmp[HEADS:SLAB, :] = jnp.full((SLAB - HEADS, HD), -1.0, F32)
    tmp[HEADS : HEADS + KVH, 0:SEL] = (ids // POOL).astype(F32)
    tmp[HEADS + KVH : SLAB, 0:SEL] = (ids % POOL).astype(F32)
    slab = tmp[...].astype(BF)
    for copy in range(SPAN):
        out_ref[copy, :, :] = slab


def spread_kernel(x_ref, out_ref):
    for copy in range(LINE):
        out_ref[copy, :, :, :] = x_ref[...]


def attend_kernel(place_ref, q_ref, *refs):
    kv_refs = refs[:SHARE]
    out_ref, qa, point, acc, s_even, s_odd = refs[SHARE:]
    odd = place_ref[SHARE]
    ids = q_ref[:, HEADS:SLAB, :].astype(F32).reshape(OWN * 8, HD).astype(BF)
    i, j = iota((KVH * OWN, OWN * 8), 0), iota((KVH * OWN, OWN * 8), 1)
    first = (i % OWN) * 8 + i // OWN
    owner = dot(one_if(j == first), ids)
    slot = dot(one_if(j == first + KVH), ids)
    code = jnp.full((KVH * OWN, HD), -1.0, F32)
    for block in range(SHARE):
        code = jnp.where(owner == place_ref[block].astype(F32), slot + float(block * POOL), code)
    lane = iota((KVH * OWN, HD), 1).astype(F32)
    bias = jnp.full((KVH * OWN, HD), -FAR, F32)
    for j in range(SEL):
        bias = jnp.where(code[:, j : j + 1] == lane, 0.0, bias)
    bias = bias.astype(BF)
    i, j = iota((256, 256), 0), iota((256, 256), 1)
    swap = one_if((j % 16) * 16 + j // 16 == i)
    for h in range(KVH):
        for c in range(OWN // 16):
            part = q_ref[c * 16 : (c + 1) * 16, h * 16 : (h + 1) * 16, :]
            turned = dot(swap, part.reshape(256, HD)).astype(BF)
            for g in range(GROUP):
                head = h * GROUP + g
                at = jnp.where(odd == 1, head, (head % LINE) * LINE + head // LINE)
                row = pl.multiple_of(at * OWN + c * 16, 16)
                qa[pl.ds(row, 16), 0:HD] = turned[g * 16 : (g + 1) * 16, :]
                qa[pl.ds(row, 16), HD : 2 * HD] = bias[h * OWN + c * 16 : h * OWN + (c + 1) * 16, :]

    point[...] = jnp.full(point.shape, FLOOR, F32)
    acc[...] = jnp.zeros(acc.shape, F32)
    first_lane = one_if(iota((TOKENS, HD), 1) == 0)
    token_page, page_lane = iota((TOKENS, HD), 0) // PAGE, iota((TOKENS, HD), 1)

    def score(block, n):
        keys = jnp.concatenate(
            [kv_refs[block][0], one_if(page_lane == token_page + block * POOL)], axis=1
        )
        return dot_nt(qa[n * CHUNK : (n + 1) * CHUNK, :], keys)

    def finish(block, n, s_ref):
        here = slice(n * CHUNK, (n + 1) * CHUNK)
        s = s_ref[...]
        top = jnp.max(s, axis=1, keepdims=True) * SCALE
        old = point[here, :]
        new = jnp.maximum(jnp.broadcast_to(top.astype(BF).astype(F32), old.shape), old)
        point[here, :] = new
        p = jnp.exp2(s * (SCALE * LOG2E) - new[:, 0:1] * LOG2E).astype(BF)
        o = dot(p, jnp.concatenate([kv_refs[block][1], first_lane], axis=1))
        fade = jnp.exp2((old - new) * LOG2E)
        acc[here, :] = acc[here, :] * jnp.concatenate([fade, fade], axis=1) + o

    chunks = HEADS * OWN // CHUNK
    steps = [(block, n) for block in range(SHARE) for n in range(chunks)]
    slots = (s_even, s_odd)
    slots[0][...] = score(*steps[0])
    for k, step in enumerate(steps):
        if k + 1 < len(steps):
            slots[(k + 1) % 2][...] = score(*steps[k + 1])
        finish(*step, slots[k % 2])

    lane = iota((OWN, HD), 1)
    for j in range(LINE):
        stats = jnp.zeros((OWN, HD), F32)
        for i in range(LINE):
            here = slice((j * LINE + i) * OWN, (j * LINE + i + 1) * OWN)
            total = acc[here, HD : HD + 1]
            total_hi = total.astype(BF).astype(F32)
            stats = jnp.where(lane == i * 8, point[here, :], stats)
            stats = jnp.where(lane == i * 8 + 1, total_hi, stats)
            stats = jnp.where(lane == i * 8 + 2, total - total_hi, stats)
            out_ref[j, i * OWN : (i + 1) * OWN, :] = acc[here, 0:HD].astype(BF)
        out_ref[j, LINE * OWN : (LINE + 1) * OWN, :] = stats.astype(BF)


def merge_kernel(r_ref, out_ref):
    kind = iota((OWN, HD), 1) % 8
    stats_of_all = []
    for rows in range(SHARE):
        sources = [span * SHARE + rows for span in range(SPAN)]
        stats = [r_ref[src, LINE * OWN : (LINE + 1) * OWN, :].astype(F32) for src in sources]
        top = functools.reduce(jnp.maximum, stats)
        factors = [jnp.exp2((s - top) * LOG2E) for s in stats]
        total = sum(
            f * (pltpu.roll(s, HD - 1, 1) + pltpu.roll(s, HD - 2, 1))
            for f, s in zip(factors, stats)
        )
        total_hi = total.astype(BF).astype(F32)
        total_lo = pltpu.roll(total - total_hi, 2, 1)
        joint = jnp.where(kind == 1, pltpu.roll(total_hi, 1, 1), jnp.where(kind == 2, total_lo, 0.0))
        stats_of_all.append(jnp.where(kind == 0, top, joint))
        for head in range(LINE):
            acc = sum(
                f[:, head * 8 : head * 8 + 1] * r_ref[src, head * OWN : (head + 1) * OWN, :].astype(F32)
                for f, src in zip(factors, sources)
            )
            out_ref[head, rows * OWN : (rows + 1) * OWN, :] = acc.astype(BF)
    tall = jnp.concatenate(stats_of_all + [jnp.zeros((HD - ROWS, HD), F32)], axis=0).T
    for head in range(LINE):
        out_ref[head, ROWS:SLAB, :] = tall[head * 8 : (head + 1) * 8, :].astype(BF)


def project_kernel(r_ref, w_ref, out_ref, att):
    @pl.when(pl.program_id(0) == 0)
    def _():
        stats = [r_ref[src, ROWS:SLAB, :].astype(F32).T[0:ROWS, :] for src in range(LINE)]
        top = functools.reduce(jnp.maximum, [s[:, 0:1] for s in stats])
        factors = [jnp.exp2((s[:, 0:1] - top) * LOG2E) for s in stats]
        total = sum(f * (s[:, 1:2] + s[:, 2:3]) for f, s in zip(factors, stats))
        acc = sum(f * r_ref[src, 0:ROWS, :].astype(F32) for src, f in enumerate(factors))
        both = (acc / total).astype(BF)
        i, j = iota((ROWS, ROWS), 0), iota((ROWS, ROWS), 1)
        came_from = (i % SHARE) * OWN + (i // LINE) * SPAN + (i % LINE) // SHARE
        att[...] = dot(one_if(j == came_from), both).astype(BF)

    out_ref[...] = dot(att[...], w_ref[...]).astype(BF)


def add_kernel(x_ref, out_ref, tmp):
    tiles = tmp.shape[0] // LINE
    for tile in range(tiles):
        total = x_ref[0, :, tile * 128 : (tile + 1) * 128].astype(F32)
        for src in range(1, LINE):
            total += x_ref[src, :, tile * 128 : (tile + 1) * 128].astype(F32)
        tmp[pl.ds(tile, LINE, stride=tiles), :] = total
    out_ref[...] = tmp[...].reshape(LINE, tiles, 128).astype(BF)


VMEM = pl.BlockSpec(memory_space=pltpu.VMEM)
SMEM = pl.BlockSpec(memory_space=pltpu.SMEM)
PARAMS = pltpu.CompilerParams(vmem_limit_bytes=24 * 2**20)


def prepare(queries, ids):
    return pl.pallas_call(
        prepare_kernel,
        out_shape=jax.ShapeDtypeStruct((SPAN, SLAB, HD), BF),
        in_specs=[pl.BlockSpec(memory_space=pltpu.HBM)] * 2,
        out_specs=VMEM,
        scratch_shapes=[
            pltpu.VMEM(queries.shape, BF),
            pltpu.VMEM(ids.shape, jnp.int32),
            pltpu.VMEM((SLAB, HD), F32),
            pltpu.SemaphoreType.DMA((2,)),
        ],
        compiler_params=PARAMS,
        name="prepare",
    )(queries, ids)


def spread(value):
    return pl.pallas_call(
        spread_kernel,
        out_shape=jax.ShapeDtypeStruct((LINE,) + value.shape, BF),
        in_specs=[VMEM],
        out_specs=VMEM,
        compiler_params=PARAMS,
        name="spread",
    )(value)


def attend(place, got, pages):
    return pl.pallas_call(
        attend_kernel,
        out_shape=jax.ShapeDtypeStruct((LINE, (LINE + 1) * OWN, HD), BF),
        in_specs=[SMEM] + [VMEM] * (1 + SHARE),
        out_specs=VMEM,
        scratch_shapes=[
            pltpu.VMEM((HEADS * OWN, 2 * HD), BF),
            pltpu.VMEM((HEADS * OWN, HD), F32),
            pltpu.VMEM((HEADS * OWN, 2 * HD), F32),
            pltpu.VMEM((CHUNK, TOKENS), F32),
            pltpu.VMEM((CHUNK, TOKENS), F32),
        ],
        compiler_params=PARAMS,
        name="attend",
    )(place, got, *pages)


def merge(parts):
    return pl.pallas_call(
        merge_kernel,
        out_shape=jax.ShapeDtypeStruct((LINE, SLAB, HD), BF),
        in_specs=[VMEM],
        out_specs=VMEM,
        compiler_params=PARAMS,
        name="merge",
    )(parts)


def project(parts, weight):
    width = weight.shape[1]
    return pl.pallas_call(
        project_kernel,
        out_shape=jax.ShapeDtypeStruct((ROWS, width), BF),
        grid=(width // BLOCK,),
        in_specs=[
            pl.BlockSpec((LINE, SLAB, HD), lambda n: (0, 0, 0)),
            pl.BlockSpec((HD, BLOCK), lambda n: (0, n)),
        ],
        out_specs=pl.BlockSpec((ROWS, BLOCK), lambda n: (0, n)),
        scratch_shapes=[pltpu.VMEM((ROWS, HD), BF)],
        compiler_params=PARAMS,
        name="project",
    )(parts, weight)


def add(parts):
    width = parts.shape[2]
    return pl.pallas_call(
        add_kernel,
        out_shape=jax.ShapeDtypeStruct((LINE, width // 128, 128), BF),
        in_specs=[VMEM],
        out_specs=VMEM,
        scratch_shapes=[pltpu.VMEM((LINE * width // 128, 128), F32)],
        compiler_params=PARAMS,
        name="add",
    )(parts)


def lines(sections, first):
    groups = []
    for section in range(sections):
        base = section * LINE * LINE
        along_y = (section % 2 == 0) == first
        for other in range(LINE):
            step, start = (1, other * LINE) if along_y else (LINE, other)
            groups.append([base + start + step * k for k in range(LINE)])
    return groups


def exchange(value, groups):
    return lax.all_to_all(
        value, ("segment", "dev"), split_axis=0, concat_axis=0, axis_index_groups=groups, tiled=True
    )


def local(queries, page_ids, key_pages, value_pages, out_weight):
    count = lax.axis_size("segment")
    one, other = lines(count, True), lines(count, False)
    spread_over = [line[rows::SHARE] for line in one for rows in range(SHARE)]
    odd = lax.axis_index("segment") % 2
    me = lax.axis_index("dev")
    stride = jnp.where(odd == 1, LINE, 1)
    along = (me // stride) % LINE
    place = [me + ((along ^ block) - along) * stride for block in range(SHARE)]
    place = jnp.stack(place + [odd]).astype(jnp.int32)
    pages = jnp.stack([key_pages.reshape(TOKENS, HD), value_pages.reshape(TOKENS, HD)])
    shared = [pages]
    for block in range(1, SHARE):
        pairs = [(line[k], line[k ^ block]) for line in one for k in range(LINE)]
        shared.append(lax.ppermute(pages, ("segment", "dev"), pairs))
    near = exchange(prepare(queries, page_ids.reshape(KVH, SEL)), spread_over)
    got = exchange(spread(near), other)
    partial = attend(place, got.reshape(OWN, SLAB, HD), shared)
    joined = merge(exchange(partial, one))
    sums = project(exchange(joined, other), out_weight)
    added = add(exchange(sums.reshape(LINE, LINE, -1), other))
    parts = exchange(added, one)
    projected = jnp.sum(parts.astype(F32), axis=0).astype(BF)
    handed = lax.ppermute(projected, "segment", [(s, (s + 1) % count) for s in range(count)])
    return handed.reshape(1, -1)


def solution(mesh):
    placed = (
        P(("segment", "dev"), None),
        P(("segment", "dev"), None, None),
        P(("segment", "dev"), None, None),
        P(("segment", "dev"), None, None),
        P(("segment", "dev"), None),
    )
    return jax.shard_map(
        local, mesh=mesh, in_specs=placed, out_specs=P(("segment", "dev"), None), check_vma=False
    )
```

time: 151 us -> 141 us (0.934)
  blocking collectives: 94.3 us -> 74.1 us
  starting transfers between devices: 15.6 us -> 34.5 us
  waiting for transfers between devices: 20.5 us -> 15.1 us
  Pallas kernels: 16.9 us -> 11.5 us
    all_to_all x5 -> x4, blocking collectives: 94.3 us -> 74.1 us  [exchange(): lax.all_to_all(value, ('segment', 'dev'), split_axis=0, concat_axis=0, ax...]
    all_to_all x1 -> x2, waiting for transfers between devices: 19.4 us -> 0.01 us  [exchange(): lax.all_to_all(value, ('segment', 'dev'), split_axis=0, concat_axis=0, ax...]
    ppermute x0 -> x3, waiting for transfers between devices: none -> 14.1 us  [local(): shared.append(lax.ppermute(pages, ('segment', 'dev'), pairs))]
    all_to_all x1 -> x2, starting transfers between devices: 6.95 us -> 17.7 us  [exchange(): lax.all_to_all(value, ('segment', 'dev'), split_axis=0, concat_axis=0, ax...]
    ppermute x0 -> x3, starting transfers between devices: none -> 9.27 us  [local(): shared.append(lax.ppermute(pages, ('segment', 'dev'), pairs))]
    pallas_call x2 -> x3, Pallas kernels: 14.3 us -> 8.47 us  [the longest x1 7.02 us: attend(): pl.pallas_call(attend_kernel, out_shape=jax.ShapeDtypeStruct((LINE, (LINE...]
    unnamed x11 -> x7, local copies, waits for them, and re-layouts: 2.13 us -> 4.31 us
  transfers between devices with their start and end apart: 2 -> 6, of which waited for: 2 -> 2; matrix products, arithmetic and copies ran while one was open for 0% -> 1% of each run, Pallas kernels for 0% -> 1%
where the time goes in v4:
time: 141 us
  blocking collectives  74.1 us (53%)
  starting transfers between devices  34.5 us (24%)
  waiting for transfers between devices  15.1 us (11%)
  Pallas kernels  11.5 us (8%)
  local copies, waits for them, and re-layouts  4.39 us (3%)
    all_to_all x4, blocking collectives, exchange(): lax.all_to_all(value, ('segment', 'dev'), split_axis=0, concat_axis=0, ax...  74.1 us
    all_to_all x2, starting transfers between devices, exchange(): lax.all_to_all(value, ('segment', 'dev'), split_axis=0, concat_axis=0, ax...  17.7 us
    ppermute x3, waiting for transfers between devices, local(): shared.append(lax.ppermute(pages, ('segment', 'dev'), pairs))  14.1 us
    ppermute x3, starting transfers between devices, local(): shared.append(lax.ppermute(pages, ('segment', 'dev'), pairs))  9.27 us
    ppermute x1, starting transfers between devices, local(): lax.ppermute(projected, 'segment', [(s, (s + 1) % count) for s in range(c...  7.58 us
    pallas_call x1, Pallas kernels, attend(): pl.pallas_call(attend_kernel, out_shape=jax.ShapeDtypeStruct((LINE, (LINE...  7.02 us
    unnamed x7, local copies, waits for them, and re-layouts  4.31 us
  transfers between devices with their start and end apart: 6, of which 2 were waited for; matrix products, arithmetic and copies ran while one was open for 1% of the time, Pallas kernels for 1%

profile of v4, /device:TPU:1, one launch (start us, length us, event | category | flops | bytes accessed | tf_op | source)
XLA Modules:
  0.0 140.8 jit_solution(11162234017074104304)
XLA Ops:
  0.0 0.0 copy-start.1
  0.0 0.8 copy-done.1
  0.8 0.0 copy-start.2
  0.8 0.7 copy-done.2
  1.4 0.7 prepare.1
  2.1 10.8 %all-to-all-start = ((bf16[2,72,128]{2,1,0:T(8,128)(2,1)}), bf16[2,72,128]{2,1,0:T(8,128)(2,1)S(1)}, u32[]{:S(2)}, u32[]{:S(2)}) async-start(bf16[2,72,128]{2,1,0:T(8,128)(2,1)} %prepare.1), calls=%async_computation | async-start | bytes 73728 | tf_op jit(solution)/shard_map/all_to_all | solution.py:307
  13.0 1.1 pad_maximum_fusion.refs_0_
  14.1 4.9 %collective-permute-start.2 = (bf16[2,1024,128]{2,1,0:T(8,128)(2,1)S(1)}, bf16[2,1024,128]{2,1,0:T(8,128)(2,1)S(1)}, u32[]{:S(2)}, u32[]{:S(2)}) collective-permute-start(bf16[2,1024,128]{2,1,0:T(8,128)(2,1)S(1)} %pad_maximum_fusion.refs_0_), channel_id=1, source_target_pairs={{0,3},{1,2},{2,1},{3,0},{4,7},{5,6},{6,5},{7,4},{8,11},{9,10},{10,... | collective-permute-start | bytes 1572872 | tf_op jit(solution)/shard_map/ppermute | solution.py:326
  19.0 1.9 %collective-permute-start.1 = (bf16[2,1024,128]{2,1,0:T(8,128)(2,1)S(1)}, bf16[2,1024,128]{2,1,0:T(8,128)(2,1)S(1)}, u32[]{:S(2)}, u32[]{:S(2)}) collective-permute-start(bf16[2,1024,128]{2,1,0:T(8,128)(2,1)S(1)} %pad_maximum_fusion.refs_0_), channel_id=1, source_target_pairs={{0,2},{1,3},{2,0},{3,1},{4,6},{5,7},{6,4},{7,5},{8,10},{9,11},{10,... | collective-permute-start | bytes 1572872 | tf_op jit(solution)/shard_map/ppermute | solution.py:326
  20.9 2.4 %collective-permute-start = (bf16[2,1024,128]{2,1,0:T(8,128)(2,1)S(1)}, bf16[2,1024,128]{2,1,0:T(8,128)(2,1)S(1)}, u32[]{:S(2)}, u32[]{:S(2)}) collective-permute-start(bf16[2,1024,128]{2,1,0:T(8,128)(2,1)S(1)} %pad_maximum_fusion.refs_0_), channel_id=1, source_target_pairs={{0,1},{1,0},{2,3},{3,2},{4,5},{5,4},{6,7},{7,6},{8,9},{9,8},{10,11... | collective-permute-start | bytes 1572872 | tf_op jit(solution)/shard_map/ppermute | solution.py:326
  23.4 0.0 all-to-all-done.x_ref
  23.4 0.8 spread.1
  24.1 6.8 %all-to-all-start.1 = ((bf16[8,2,72,128]{3,2,1,0:T(8,128)(2,1)}), bf16[8,2,72,128]{3,2,1,0:T(8,128)(2,1)S(1)}, u32[]{:S(2)}, u32[]{:S(2)}) async-start(bf16[8,2,72,128]{3,2,1,0:T(8,128)(2,1)} %spread.1), calls=%async_computation.1 | async-start | bytes 589824 | tf_op jit(solution)/shard_map/all_to_all | solution.py:307
  30.9 0.1 stack.26.place_ref
  31.0 0.0 collective-permute-done.2.refs_3_
  31.0 14.1 %collective-permute-done.1.refs_2_ = bf16[2,1024,128]{2,1,0:T(8,128)(2,1)S(1)} collective-permute-done((bf16[2,1024,128]{2,1,0:T(8,128)(2,1)S(1)}, bf16[2,1024,128]{2,1,0:T(8,128)(2,1)S(1)}, u32[]{:S(2)}, u32[]{:S(2)}) %collective-permute-start.1) | collective-permute-done | bytes 524320 | tf_op jit(solution)/shard_map/ppermute | solution.py:326
  45.1 0.0 collective-permute-done.refs_1_
  45.1 0.0 all-to-all-done.1
  45.1 7.0 %attend.1 = bf16[8,144,128]{2,1,0:T(8,128)(2,1)S(1)} custom-call(s32[5]{0:T(128)S(1)} %stack.26.place_ref, bf16[16,72,128]{2,1,0:T(8,128)(2,1)S(1)} %bitcast.16, bf16[2,1024,128]{2,1,0:T(8,128)(2,1)S(1)} %pad_maximum_fusion.refs_0_, bf16[2,1024,128]{2,1,0:T(8,128)(2,1)S(1)} %collective-permute-done.refs_1_, ...), custom_call_target="tpu_custom_call" | custom-call | tf_op jit(solution)/shard_map/attend/pallas_call | solution.py:237
  52.2 16.2 %all_to_all.30.r_ref = bf16[8,144,128]{2,1,0:T(8,128)(2,1)S(1)} all-to-all(bf16[8,144,128]{2,1,0:T(8,128)(2,1)S(1)} %attend.1), channel_id=1, replica_groups={{0,1,2,3,4,5,6,7},{8,9,10,11,12,13,14,15},{16,17,18,19,20,21,22,23},{24..., dimensions={0} | all-to-all | bytes 589824 | tf_op jit(solution)/shard_map/all_to_all | solution.py:307
  68.4 0.5 merge.1
  68.9 14.7 %all_to_all.31.r_ref = bf16[8,72,128]{2,1,0:T(8,128)(2,1)S(1)} all-to-all(bf16[8,72,128]{2,1,0:T(8,128)(2,1)S(1)} %merge.1), channel_id=1, replica_groups={{0,8,16,24,32,40,48,56},{1,9,17,25,33,41,49,57},{2,10,18,26,34,42,50,58..., dimensions={0} | all-to-all | bytes 294912 | tf_op jit(solution)/shard_map/all_to_all | solution.py:307
  83.6 0.0 copy-start
  83.6 2.2 %copy-done = bf16[128,16384]{1,0:T(8,128)(2,1)S(1)} copy-done((bf16[128,16384]{1,0:T(8,128)(2,1)S(1)}, bf16[128,16384]{1,0:T(8,128)(2,1)}, u32[]{:S(2)}) %copy-start) | copy-done | bytes 4194328
  85.8 2.2 %project.1 = bf16[64,16384]{1,0:T(8,128)(2,1)S(1)} custom-call(bf16[8,72,128]{2,1,0:T(8,128)(2,1)S(1)} %all_to_all.31.r_ref, bf16[128,16384]{1,0:T(8,128)(2,1)S(1)} %copy-done), custom_call_target="tpu_custom_call" | custom-call | tf_op jit(solution)/shard_map/project/pallas_call | solution.py:267
  88.0 31.4 %all_to_all.32.x_ref = bf16[8,8,16384]{2,1,0:T(8,128)(2,1)S(1)} all-to-all(bf16[8,8,16384]{2,1,0:T(8,128)(2,1)S(1)} %bitcast.15), channel_id=1, replica_groups={{0,8,16,24,32,40,48,56},{1,9,17,25,33,41,49,57},{2,10,18,26,34,42,50,58..., dimensions={0} | all-to-all | bytes 4194304 | tf_op jit(solution)/shard_map/all_to_all | solution.py:307
  119.4 0.4 add.23
  119.8 11.7 %all_to_all.33 = bf16[8,128,128]{2,1,0:T(8,128)(2,1)S(1)} all-to-all(bf16[8,128,128]{2,1,0:T(8,128)(2,1)S(1)} %add.23), channel_id=1, replica_groups={{0,1,2,3,4,5,6,7},{8,9,10,11,12,13,14,15},{16,17,18,19,20,21,22,23},{24..., dimensions={0} | all-to-all | bytes 524288 | tf_op jit(solution)/shard_map/all_to_all | solution.py:307
  131.6 7.6 %collective-permute-start.3 = (bf16[128,128]{1,0:T(8,128)(2,1)S(1)}, bf16[128,128]{1,0:T(8,128)(2,1)S(1)}, u32[]{:S(2)}, u32[]{:S(2)}) collective-permute-start(bf16[128,128]{1,0:T(8,128)(2,1)S(1)} %reduce_sum.12), channel_id=1, source_target_pairs={{0,64},{64,128},{128,192},{192,256},{256,320},{320,384},{384,448},... | collective-permute-start | bytes 98312 | tf_op jit(solution)/shard_map/ppermute | solution.py:335
  139.1 1.0 collective-permute-done.3
  140.2 0.7 copy.8
  (1 shorter events, 0.0 us)
Async XLA Ops:
  0.0 0.8 copy-start.1
  0.8 0.7 copy-start.2
  2.1 21.2 %all-to-all-start = ((bf16[2,72,128]{2,1,0:T(8,128)(2,1)}), bf16[2,72,128]{2,1,0:T(8,128)(2,1)S(1)}, u32[]{:S(2)}, u32[]{:S(2)}) async-start(bf16[2,72,128]{2,1,0:T(8,128)(2,1)} %prepare.1), calls=%async_computation | async-start | bytes 73728 | tf_op jit(solution)/shard_map/all_to_all | solution.py:307
  14.1 17.0 %collective-permute-start.2 = (bf16[2,1024,128]{2,1,0:T(8,128)(2,1)S(1)}, bf16[2,1024,128]{2,1,0:T(8,128)(2,1)S(1)}, u32[]{:S(2)}, u32[]{:S(2)}) collective-permute-start(bf16[2,1024,128]{2,1,0:T(8,128)(2,1)S(1)} %pad_maximum_fusion.refs_0_), channel_id=1, source_target_pairs={{0,3},{1,2},{2,1},{3,0},{4,7},{5,6},{6,5},{7,4},{8,11},{9,10},{10,... | collective-permute-start | bytes 1572872 | tf_op jit(solution)/shard_map/ppermute | solution.py:326
  19.0 26.2 %collective-permute-start.1 = (bf16[2,1024,128]{2,1,0:T(8,128)(2,1)S(1)}, bf16[2,1024,128]{2,1,0:T(8,128)(2,1)S(1)}, u32[]{:S(2)}, u32[]{:S(2)}) collective-permute-start(bf16[2,1024,128]{2,1,0:T(8,128)(2,1)S(1)} %pad_maximum_fusion.refs_0_), channel_id=1, source_target_pairs={{0,2},{1,3},{2,0},{3,1},{4,6},{5,7},{6,4},{7,5},{8,10},{9,11},{10,... | collective-permute-start | bytes 1572872 | tf_op jit(solution)/shard_map/ppermute | solution.py:326
  20.9 24.2 %collective-permute-start = (bf16[2,1024,128]{2,1,0:T(8,128)(2,1)S(1)}, bf16[2,1024,128]{2,1,0:T(8,128)(2,1)S(1)}, u32[]{:S(2)}, u32[]{:S(2)}) collective-permute-start(bf16[2,1024,128]{2,1,0:T(8,128)(2,1)S(1)} %pad_maximum_fusion.refs_0_), channel_id=1, source_target_pairs={{0,1},{1,0},{2,3},{3,2},{4,5},{5,4},{6,7},{7,6},{8,9},{9,8},{10,11... | collective-permute-start | bytes 1572872 | tf_op jit(solution)/shard_map/ppermute | solution.py:326
  24.1 21.0 %all-to-all-start.1 = ((bf16[8,2,72,128]{3,2,1,0:T(8,128)(2,1)}), bf16[8,2,72,128]{3,2,1,0:T(8,128)(2,1)S(1)}, u32[]{:S(2)}, u32[]{:S(2)}) async-start(bf16[8,2,72,128]{3,2,1,0:T(8,128)(2,1)} %spread.1), calls=%async_computation.1 | async-start | bytes 589824 | tf_op jit(solution)/shard_map/all_to_all | solution.py:307
  83.6 2.2 %copy-start = (bf16[128,16384]{1,0:T(8,128)(2,1)S(1)}, bf16[128,16384]{1,0:T(8,128)(2,1)}, u32[]{:S(2)}) copy-start(bf16[128,16384]{1,0:T(8,128)(2,1)} %w_ref.1) | copy-start | bytes 12582916
  131.6 8.6 %collective-permute-start.3 = (bf16[128,128]{1,0:T(8,128)(2,1)S(1)}, bf16[128,128]{1,0:T(8,128)(2,1)S(1)}, u32[]{:S(2)}, u32[]{:S(2)}) collective-permute-start(bf16[128,128]{1,0:T(8,128)(2,1)S(1)} %reduce_sum.12), channel_id=1, source_target_pairs={{0,64},{64,128},{128,192},{192,256},{256,320},{320,384},{384,448},... | collective-permute-start | bytes 98312 | tf_op jit(solution)/shard_map/ppermute | solution.py:335

commit v5 on v4

--- a/solution.py
+++ b/solution.py
@@ -22,9 +22,12 @@
 SEL = 32
 LINE = 8
 SHARE = 4
-SPAN = LINE // SHARE
+SPAN = 4
+PAIR = 2
 OWN = ROWS // SHARE
-BLOCK = 4096
+HALF = PAIR * OWN
+SMALL = HALF + 8
+BLOCK = 2048
 CHUNK = 512
 LOG2E = math.log2(math.e)
 SCALE = 1.0 / math.sqrt(HD)
@@ -67,7 +70,7 @@
 
 
 def spread_kernel(x_ref, out_ref):
-    for copy in range(LINE):
+    for copy in range(SPAN):
         out_ref[copy, :, :, :] = x_ref[...]
 
 
@@ -150,8 +153,8 @@
 def merge_kernel(r_ref, out_ref):
     kind = iota((OWN, HD), 1) % 8
     stats_of_all = []
-    for rows in range(SHARE):
-        sources = [span * SHARE + rows for span in range(SPAN)]
+    for rows in range(PAIR):
+        sources = range(rows, LINE, PAIR)
         stats = [r_ref[src, LINE * OWN : (LINE + 1) * OWN, :].astype(F32) for src in sources]
         top = functools.reduce(jnp.maximum, stats)
         factors = [jnp.exp2((s - top) * LOG2E) for s in stats]
@@ -167,35 +170,49 @@
             acc = sum(
                 f[:, head * 8 : head * 8 + 1] * r_ref[src, head * OWN : (head + 1) * OWN, :].astype(F32)
                 for f, src in zip(factors, sources)
-            )
-            out_ref[head, rows * OWN : (rows + 1) * OWN, :] = acc.astype(BF)
-    tall = jnp.concatenate(stats_of_all + [jnp.zeros((HD - ROWS, HD), F32)], axis=0).T
+            ).astype(BF)
+            out_ref[head, 0, rows * OWN : (rows + 1) * OWN, :] = acc
+            out_ref[head ^ 1, 1, rows * OWN : (rows + 1) * OWN, :] = acc
+    tall = jnp.concatenate(stats_of_all + [jnp.zeros((HD - HALF, HD), F32)], axis=0).T
     for head in range(LINE):
-        out_ref[head, ROWS:SLAB, :] = tall[head * 8 : (head + 1) * 8, :].astype(BF)
-
-
-def project_kernel(r_ref, w_ref, out_ref, att):
+        stats = tall[head * 8 : (head + 1) * 8, :].astype(BF)
+        out_ref[head, 0, HALF:SMALL, :] = stats
+        out_ref[head ^ 1, 1, HALF:SMALL, :] = stats
+
+
+def project_kernel(side_ref, r_ref, mine_ref, theirs_ref, out_ref, att):
     @pl.when(pl.program_id(0) == 0)
     def _():
-        stats = [r_ref[src, ROWS:SLAB, :].astype(F32).T[0:ROWS, :] for src in range(LINE)]
-        top = functools.reduce(jnp.maximum, [s[:, 0:1] for s in stats])
-        factors = [jnp.exp2((s[:, 0:1] - top) * LOG2E) for s in stats]
-        total = sum(f * (s[:, 1:2] + s[:, 2:3]) for f, s in zip(factors, stats))
-        acc = sum(f * r_ref[src, 0:ROWS, :].astype(F32) for src, f in enumerate(factors))
-        both = (acc / total).astype(BF)
+        heads = []
+        for head in range(PAIR):
+            halves = []
+            for rows in range(PAIR):
+                sources = range(rows, LINE, PAIR)
+                stats = [r_ref[src, head, HALF:SMALL, :].astype(F32).T[0:HALF, :] for src in sources]
+                top = functools.reduce(jnp.maximum, [s[:, 0:1] for s in stats])
+                factors = [jnp.exp2((s[:, 0:1] - top) * LOG2E) for s in stats]
+                total = sum(f * (s[:, 1:2] + s[:, 2:3]) for f, s in zip(factors, stats))
+                acc = sum(
+                    f * r_ref[src, head, 0:HALF, :].astype(F32) for src, f in zip(sources, factors)
+                )
+                halves.append((acc / total).astype(BF))
+            heads.append(jnp.concatenate(halves, axis=0))
+        both = jnp.concatenate(heads, axis=1)
         i, j = iota((ROWS, ROWS), 0), iota((ROWS, ROWS), 1)
-        came_from = (i % SHARE) * OWN + (i // LINE) * SPAN + (i % LINE) // SHARE
+        b, u = i // LINE, i % LINE
+        came_from = (b % PAIR) * HALF + (u % PAIR) * OWN + (b // PAIR) * SPAN + u // PAIR
         att[...] = dot(one_if(j == came_from), both).astype(BF)
 
-    out_ref[...] = dot(att[...], w_ref[...]).astype(BF)
+    weight = jnp.concatenate([mine_ref[...], theirs_ref[...]], axis=0)
+    out_ref[...] = dot(att[...], weight).astype(BF)
 
 
 def add_kernel(x_ref, out_ref, tmp):
     tiles = tmp.shape[0] // LINE
+    half = tiles // PAIR
     for tile in range(tiles):
-        total = x_ref[0, :, tile * 128 : (tile + 1) * 128].astype(F32)
-        for src in range(1, LINE):
-            total += x_ref[src, :, tile * 128 : (tile + 1) * 128].astype(F32)
+        lanes = slice(tile % half * 128, (tile % half + 1) * 128)
+        total = sum(x_ref[src, :, lanes].astype(F32) for src in range(tile // half, LINE, PAIR))
         tmp[pl.ds(tile, LINE, stride=tiles), :] = total
     out_ref[...] = tmp[...].reshape(LINE, tiles, 128).astype(BF)
 
@@ -225,7 +242,7 @@
 def spread(value):
     return pl.pallas_call(
         spread_kernel,
-        out_shape=jax.ShapeDtypeStruct((LINE,) + value.shape, BF),
+        out_shape=jax.ShapeDtypeStruct((SPAN,) + value.shape, BF),
         in_specs=[VMEM],
         out_specs=VMEM,
         compiler_params=PARAMS,
@@ -254,7 +271,7 @@
 def merge(parts):
     return pl.pallas_call(
         merge_kernel,
-        out_shape=jax.ShapeDtypeStruct((LINE, SLAB, HD), BF),
+        out_shape=jax.ShapeDtypeStruct((LINE, PAIR, SMALL, HD), BF),
         in_specs=[VMEM],
         out_specs=VMEM,
         compiler_params=PARAMS,
@@ -262,25 +279,30 @@
     )(parts)
 
 
-def project(parts, weight):
-    width = weight.shape[1]
+def project(side, parts, mine, theirs):
+    width = theirs.shape[1]
+    steps = width // BLOCK
     return pl.pallas_call(
         project_kernel,
         out_shape=jax.ShapeDtypeStruct((ROWS, width), BF),
-        grid=(width // BLOCK,),
-        in_specs=[
-            pl.BlockSpec((LINE, SLAB, HD), lambda n: (0, 0, 0)),
-            pl.BlockSpec((HD, BLOCK), lambda n: (0, n)),
-        ],
-        out_specs=pl.BlockSpec((ROWS, BLOCK), lambda n: (0, n)),
-        scratch_shapes=[pltpu.VMEM((ROWS, HD), BF)],
+        grid_spec=pltpu.PrefetchScalarGridSpec(
+            num_scalar_prefetch=1,
+            grid=(steps,),
+            in_specs=[
+                pl.BlockSpec(parts.shape, lambda n, side: (0, 0, 0, 0)),
+                pl.BlockSpec((HD, BLOCK), lambda n, side: (0, n + side[0] * steps)),
+                pl.BlockSpec((HD, BLOCK), lambda n, side: (0, n)),
+            ],
+            out_specs=pl.BlockSpec((ROWS, BLOCK), lambda n, side: (0, n)),
+            scratch_shapes=[pltpu.VMEM((ROWS, PAIR * HD), BF)],
+        ),
         compiler_params=PARAMS,
         name="project",
-    )(parts, weight)
+    )(side, parts, mine, theirs)
 
 
 def add(parts):
-    width = parts.shape[2]
+    width = parts.shape[2] * PAIR
     return pl.pallas_call(
         add_kernel,
         out_shape=jax.ShapeDtypeStruct((LINE, width // 128, 128), BF),
@@ -309,26 +331,48 @@
     )
 
 
+def in_hbm(value):
+    return pltpu.with_memory_space_constraint(value, pltpu.HBM)
+
+
+def neighbours(groups):
+    return [(line[k], line[k ^ 1]) for line in groups for k in range(LINE)]
+
+
 def local(queries, page_ids, key_pages, value_pages, out_weight):
     count = lax.axis_size("segment")
+    both = ("segment", "dev")
     one, other = lines(count, True), lines(count, False)
-    spread_over = [line[rows::SHARE] for line in one for rows in range(SHARE)]
+    one_rows = [line[rows::PAIR] for line in one for rows in range(PAIR)]
+    other_rows = [line[rows::PAIR] for line in other for rows in range(PAIR)]
     odd = lax.axis_index("segment") % 2
     me = lax.axis_index("dev")
-    stride = jnp.where(odd == 1, LINE, 1)
-    along = (me // stride) % LINE
-    place = [me + ((along ^ block) - along) * stride for block in range(SHARE)]
+    u = jnp.where(odd == 1, me // LINE, me % LINE)
+    b = jnp.where(odd == 1, me % LINE, me // LINE)
+    place = []
+    for block in range(SHARE):
+        block_u, block_b = u ^ (block % 2), b ^ (block // 2)
+        place.append(jnp.where(odd == 1, block_u * LINE + block_b, block_b * LINE + block_u))
     place = jnp.stack(place + [odd]).astype(jnp.int32)
+
+    near = exchange(prepare(in_hbm(queries), in_hbm(page_ids.reshape(KVH, SEL))), one_rows)
     pages = jnp.stack([key_pages.reshape(TOKENS, HD), value_pages.reshape(TOKENS, HD)])
-    shared = [pages]
-    for block in range(1, SHARE):
-        pairs = [(line[k], line[k ^ block]) for line in one for k in range(LINE)]
-        shared.append(lax.ppermute(pages, ("segment", "dev"), pairs))
-    near = exchange(prepare(queries, page_ids.reshape(KVH, SEL)), spread_over)
-    got = exchange(spread(near), other)
-    partial = attend(place, got.reshape(OWN, SLAB, HD), shared)
+    pages_u = lax.ppermute(pages, both, neighbours(one))
+    pages_b = lax.ppermute(pages, both, neighbours(other))
+    near, pages_u, pages_b = lax.optimization_barrier((near, pages_u, pages_b))
+    pages_ub = lax.ppermute(pages_u, both, neighbours(other))
+    got = exchange(spread(near), other_rows)
+
+    side = b % PAIR
+    width = out_weight.shape[1] // PAIR
+    weight, got, pages_ub = lax.optimization_barrier((out_weight, got, pages_ub))
+    given = lax.dynamic_slice_in_dim(weight, (1 - side) * width, width, axis=1)
+    theirs = lax.ppermute(given, both, neighbours(other))
+
+    partial = attend(place, got.reshape(OWN, SLAB, HD), [pages, pages_u, pages_b, pages_ub])
     joined = merge(exchange(partial, one))
-    sums = project(exchange(joined, other), out_weight)
+    gathered = exchange(joined, other)
+    sums = project(side.astype(jnp.int32).reshape(1), gathered, in_hbm(out_weight), theirs)
     added = add(exchange(sums.reshape(LINE, LINE, -1), other))
     parts = exchange(added, one)
     projected = jnp.sum(parts.astype(F32), axis=0).astype(BF)

time: 141 us -> 134 us (0.950)
  starting transfers between devices: 34.5 us -> 26.7 us
  waiting for transfers between devices: 15.1 us -> 9.55 us
  local copies, waits for them, and re-layouts: 4.39 us -> 6.77 us
  Pallas kernels: 11.5 us -> 13.2 us
    ppermute x3 -> x4, waiting for transfers between devices: 14.1 us -> 0.01 us  [the longest x1 0.01 us: local(): pages_b = lax.ppermute(pages, both, neighbours(other))]
    all_to_all x2 -> x1, starting transfers between devices: 17.7 us -> 5.91 us  [exchange(): lax.all_to_all(value, ('segment', 'dev'), split_axis=0, concat_axis=0, ax...]
    all_to_all x2 -> x1, waiting for transfers between devices: 0.01 us -> 8.51 us  [exchange(): lax.all_to_all(value, ('segment', 'dev'), split_axis=0, concat_axis=0, ax...]
    ppermute x3 -> x4, starting transfers between devices: 9.27 us -> 14.7 us  [the longest x1 4.03 us: local(): pages_b = lax.ppermute(pages, both, neighbours(other))]
    dynamic_slice x0 -> x1, local copies, waits for them, and re-layouts: none -> 3.12 us  [local(): given = lax.dynamic_slice_in_dim(weight, (1 - side) * width, width, axis=1)]
    pallas_call x1, Pallas kernels: 2.15 us -> 3.87 us  [project(): pl.pallas_call(project_kernel, out_shape=jax.ShapeDtypeStruct((ROWS, widt...]
    ppermute x1, starting transfers between devices: 7.58 us -> 6.12 us  [local(): lax.ppermute(projected, 'segment', [(s, (s + 1) % count) for s in range(c...]
    all_to_all x4 -> x5, blocking collectives: 74.1 us -> 75.5 us  [exchange(): lax.all_to_all(value, ('segment', 'dev'), split_axis=0, concat_axis=0, ax...]
  transfers between devices with their start and end apart: 6 -> 6, of which waited for: 2 -> 2; matrix products, arithmetic and copies ran while one was open for 1% -> 0% of each run, Pallas kernels for 1% -> 7%
where the time goes in v5:
time: 134 us; the launch traced here: 133 us
  blocking collectives  75.5 us (56%)
  starting transfers between devices  26.7 us (20%)
  Pallas kernels  13.2 us (10%)
  waiting for transfers between devices  9.55 us (7%)
  local copies, waits for them, and re-layouts  6.77 us (5%)
    all_to_all x5, blocking collectives, exchange(): lax.all_to_all(value, ('segment', 'dev'), split_axis=0, concat_axis=0, ax...  75.5 us
    all_to_all x1, waiting for transfers between devices, exchange(): lax.all_to_all(value, ('segment', 'dev'), split_axis=0, concat_axis=0, ax...  8.51 us
    pallas_call x1, Pallas kernels, attend(): pl.pallas_call(attend_kernel, out_shape=jax.ShapeDtypeStruct((LINE, (LINE...  7.1 us
    ppermute x1, starting transfers between devices, local(): lax.ppermute(projected, 'segment', [(s, (s + 1) % count) for s in range(c...  6.12 us
    all_to_all x1, starting transfers between devices, exchange(): lax.all_to_all(value, ('segment', 'dev'), split_axis=0, concat_axis=0, ax...  5.91 us
    ppermute x1, starting transfers between devices, local(): pages_b = lax.ppermute(pages, both, neighbours(other))  4.03 us
    ppermute x1, starting transfers between devices, local(): pages_u = lax.ppermute(pages, both, neighbours(one))  4 us
    pallas_call x1, Pallas kernels, project(): pl.pallas_call(project_kernel, out_shape=jax.ShapeDtypeStruct((ROWS, widt...  3.87 us
  transfers between devices with their start and end apart: 6, of which 2 were waited for; matrix products, arithmetic and copies ran while one was open for 0% of the time, Pallas kernels for 7%

profile of v5, /device:TPU:1, one launch (start us, length us, event | category | flops | bytes accessed | tf_op | source)
XLA Modules:
  0.0 133.0 jit_solution(18024477275594962729)
XLA Ops:
  0.0 1.1 pad_maximum_fusion.refs_0_
  1.1 4.0 %collective-permute-start.1 = (bf16[2,1024,128]{2,1,0:T(8,128)(2,1)S(1)}, bf16[2,1024,128]{2,1,0:T(8,128)(2,1)S(1)}, u32[]{:S(2)}, u32[]{:S(2)}) collective-permute-start(bf16[2,1024,128]{2,1,0:T(8,128)(2,1)S(1)} %pad_maximum_fusion.refs_0_), channel_id=1, source_target_pairs={{0,8},{8,0},{16,24},{24,16},{32,40},{40,32},{48,56},{56,48},{1,9},... | collective-permute-start | bytes 1572872 | tf_op jit(solution)/shard_map/ppermute | solution.py:361
  5.1 4.0 %collective-permute-start = (bf16[2,1024,128]{2,1,0:T(8,128)(2,1)S(1)}, bf16[2,1024,128]{2,1,0:T(8,128)(2,1)S(1)}, u32[]{:S(2)}, u32[]{:S(2)}) collective-permute-start(bf16[2,1024,128]{2,1,0:T(8,128)(2,1)S(1)} %pad_maximum_fusion.refs_0_), channel_id=1, source_target_pairs={{0,1},{1,0},{2,3},{3,2},{4,5},{5,4},{6,7},{7,6},{8,9},{9,8},{10,11... | collective-permute-start | bytes 1572872 | tf_op jit(solution)/shard_map/ppermute | solution.py:360
  9.1 0.8 prepare.1
  10.0 17.9 %all_to_all.30.x_ref = bf16[4,72,128]{2,1,0:T(8,128)(2,1)S(1)} all-to-all(bf16[4,72,128]{2,1,0:T(8,128)(2,1)S(1)} %prepare.1), channel_id=1, replica_groups={{0,2,4,6},{1,3,5,7},{8,10,12,14},{9,11,13,15},{16,18,20,22},{17,19,21,2..., dimensions={0} | all-to-all | bytes 147456 | tf_op jit(solution)/shard_map/all_to_all | solution.py:329
  27.9 0.0 collective-permute-done.1.refs_2_
  27.9 0.0 collective-permute-done.refs_1_
  27.9 0.0 copy-start
  27.9 3.2 %collective-permute-start.2 = (bf16[2,1024,128]{2,1,0:T(8,128)(2,1)S(1)}, bf16[2,1024,128]{2,1,0:T(8,128)(2,1)S(1)}, u32[]{:S(2)}, u32[]{:S(2)}) collective-permute-start(bf16[2,1024,128]{2,1,0:T(8,128)(2,1)S(1)} %collective-permute-done.refs_1_), channel_id=1, source_target_pairs={{0,8},{8,0},{16,24},{24,16},{32,40},{40,32},{48,56},{56,48},{1,9},... | collective-permute-start | bytes 1572872 | tf_op jit(solution)/shard_map/ppermute | solution.py:363
  31.1 0.8 spread.1
  31.8 5.9 %all-to-all-start.1 = ((bf16[4,4,72,128]{3,2,1,0:T(8,128)(2,1)}), bf16[4,4,72,128]{3,2,1,0:T(8,128)(2,1)S(1)}, u32[]{:S(2)}, u32[]{:S(2)}) async-start(bf16[4,4,72,128]{3,2,1,0:T(8,128)(2,1)} %spread.1), calls=%async_computation.1 | async-start | bytes 589824 | tf_op jit(solution)/shard_map/all_to_all | solution.py:329
  37.8 8.5 %all-to-all-done.1 = bf16[4,4,72,128]{3,2,1,0:T(8,128)(2,1)S(1)} async-done(((bf16[4,4,72,128]{3,2,1,0:T(8,128)(2,1)}), bf16[4,4,72,128]{3,2,1,0:T(8,128)(2,1)S(1)}, u32[]{:S(2)}, u32[]{:S(2)}) %all-to-all-start.1) | async-done | bytes 294944 | tf_op jit(solution)/shard_map/all_to_all | solution.py:329
  46.3 0.0 collective-permute-done.2.refs_3_
  46.3 0.0 copy-done
  46.3 0.0 copy-start.2
  46.3 0.8 copy-done.2
  47.1 3.1 %constant_dynamic-slice_fusion = bf16[128,8192]{1,0:T(8,128)(2,1)} fusion(bf16[128,16384]{1,0:T(8,128)(2,1)} %mine_ref.1, s32[]{:T(128)S(6)} %select_n.53), kind=kLoop, calls=%fused_computation.2 | loop fusion | bytes 4194308 | tf_op jit(solution)/shard_map/dynamic_slice | solution.py:369
  50.2 3.5 %collective-permute-start.3 = (bf16[128,8192]{1,0:T(8,128)(2,1)}, bf16[128,8192]{1,0:T(8,128)(2,1)S(1)}, u32[]{:S(2)}, u32[]{:S(2)}) collective-permute-start(bf16[128,8192]{1,0:T(8,128)(2,1)} %constant_dynamic-slice_fusion), channel_id=1, source_target_pairs={{0,8},{8,0},{16,24},{24,16},{32,40},{40,32},{48,56},{56,48},{1,9},... | collective-permute-start | bytes 6291464 | tf_op jit(solution)/shard_map/ppermute | solution.py:370
  53.7 0.1 stack.26.place_ref
  53.8 0.0 copy-start.1
  53.8 1.0 copy-done.1
  54.8 0.0 copy-start.3
  54.8 1.0 copy-done.3
  55.9 7.1 %attend.1 = bf16[8,144,128]{2,1,0:T(8,128)(2,1)S(1)} custom-call(s32[5]{0:T(128)S(1)} %stack.26.place_ref, bf16[16,72,128]{2,1,0:T(8,128)(2,1)S(1)} %bitcast.17, bf16[2,1024,128]{2,1,0:T(8,128)(2,1)S(1)} %pad_maximum_fusion.refs_0_, bf16[2,1024,128]{2,1,0:T(8,128)(2,1)S(1)} %copy-done.1, bf16[2,1024,128]{2,1,0:T(8,128)(2,1)S(1)} %collective-permute-done.1.refs_2_, ...), custom_call_target="tpu_custom_call" | custom-call | tf_op jit(solution)/shard_map/attend/pallas_call | solution.py:254
  63.0 14.8 %all_to_all.31.r_ref = bf16[8,144,128]{2,1,0:T(8,128)(2,1)S(1)} all-to-all(bf16[8,144,128]{2,1,0:T(8,128)(2,1)S(1)} %attend.1), channel_id=1, replica_groups={{0,1,2,3,4,5,6,7},{8,9,10,11,12,13,14,15},{16,17,18,19,20,21,22,23},{24..., dimensions={0} | all-to-all | bytes 589824 | tf_op jit(solution)/shard_map/all_to_all | solution.py:329
  77.7 0.3 merge.1
  78.1 10.7 %all_to_all.32.r_ref = bf16[8,2,40,128]{3,2,1,0:T(8,128)(2,1)S(1)} all-to-all(bf16[8,2,40,128]{3,2,1,0:T(8,128)(2,1)S(1)} %merge.1), channel_id=1, replica_groups={{0,8,16,24,32,40,48,56},{1,9,17,25,33,41,49,57},{2,10,18,26,34,42,50,58..., dimensions={0} | all-to-all | bytes 327680 | tf_op jit(solution)/shard_map/all_to_all | solution.py:329
  88.8 0.0 collective-permute-done.3.theirs_ref
  88.8 3.9 %project.1 = bf16[64,8192]{1,0:T(8,128)(2,1)S(1)} custom-call(s32[1]{0:T(128)} %bitcast.side_ref, bf16[8,2,40,128]{3,2,1,0:T(8,128)(2,1)S(1)} %all_to_all.32.r_ref, bf16[128,16384]{1,0:T(8,128)(2,1)} %mine_ref.1, bf16[128,8192]{1,0:T(8,128)(2,1)S(1)} %collective-permute-done.3.theirs_ref), custom_call_target="tpu_custom_call" | custom-call | tf_op jit(solution)/shard_map/project/pallas_call | solution.py:285
  92.6 20.5 %all_to_all.33.x_ref = bf16[8,8,8192]{2,1,0:T(8,128)(2,1)S(1)} all-to-all(bf16[8,8,8192]{2,1,0:T(8,128)(2,1)S(1)} %bitcast.16), channel_id=1, replica_groups={{0,8,16,24,32,40,48,56},{1,9,17,25,33,41,49,57},{2,10,18,26,34,42,50,58..., dimensions={0} | all-to-all | bytes 2097152 | tf_op jit(solution)/shard_map/all_to_all | solution.py:329
  113.1 0.3 add.52
  113.4 11.7 %all_to_all.34 = bf16[8,128,128]{2,1,0:T(8,128)(2,1)S(1)} all-to-all(bf16[8,128,128]{2,1,0:T(8,128)(2,1)S(1)} %add.52), channel_id=1, replica_groups={{0,1,2,3,4,5,6,7},{8,9,10,11,12,13,14,15},{16,17,18,19,20,21,22,23},{24..., dimensions={0} | all-to-all | bytes 524288 | tf_op jit(solution)/shard_map/all_to_all | solution.py:329
  125.2 6.1 %collective-permute-start.4 = (bf16[128,128]{1,0:T(8,128)(2,1)S(1)}, bf16[128,128]{1,0:T(8,128)(2,1)S(1)}, u32[]{:S(2)}, u32[]{:S(2)}) collective-permute-start(bf16[128,128]{1,0:T(8,128)(2,1)S(1)} %reduce_sum.12), channel_id=1, source_target_pairs={{0,64},{64,128},{128,192},{192,256},{256,320},{320,384},{384,448},... | collective-permute-start | bytes 98312 | tf_op jit(solution)/shard_map/ppermute | solution.py:379
  131.3 1.0 collective-permute-done.4
  132.4 0.7 copy.8
  (1 shorter events, 0.0 us)
Async XLA Ops:
  1.1 26.8 %collective-permute-start.1 = (bf16[2,1024,128]{2,1,0:T(8,128)(2,1)S(1)}, bf16[2,1024,128]{2,1,0:T(8,128)(2,1)S(1)}, u32[]{:S(2)}, u32[]{:S(2)}) collective-permute-start(bf16[2,1024,128]{2,1,0:T(8,128)(2,1)S(1)} %pad_maximum_fusion.refs_0_), channel_id=1, source_target_pairs={{0,8},{8,0},{16,24},{24,16},{32,40},{40,32},{48,56},{56,48},{1,9},... | collective-permute-start | bytes 1572872 | tf_op jit(solution)/shard_map/ppermute | solution.py:361
  5.1 22.7 %collective-permute-start = (bf16[2,1024,128]{2,1,0:T(8,128)(2,1)S(1)}, bf16[2,1024,128]{2,1,0:T(8,128)(2,1)S(1)}, u32[]{:S(2)}, u32[]{:S(2)}) collective-permute-start(bf16[2,1024,128]{2,1,0:T(8,128)(2,1)S(1)} %pad_maximum_fusion.refs_0_), channel_id=1, source_target_pairs={{0,1},{1,0},{2,3},{3,2},{4,5},{5,4},{6,7},{7,6},{8,9},{9,8},{10,11... | collective-permute-start | bytes 1572872 | tf_op jit(solution)/shard_map/ppermute | solution.py:360
  27.9 18.4 %copy-start = (bf16[2,1024,128]{2,1,0:T(8,128)(2,1)}, bf16[2,1024,128]{2,1,0:T(8,128)(2,1)S(1)}, u32[]{:S(2)}) copy-start(bf16[2,1024,128]{2,1,0:T(8,128)(2,1)S(1)} %collective-permute-done.refs_1_) | copy-start | bytes 1572868
  27.9 18.4 %collective-permute-start.2 = (bf16[2,1024,128]{2,1,0:T(8,128)(2,1)S(1)}, bf16[2,1024,128]{2,1,0:T(8,128)(2,1)S(1)}, u32[]{:S(2)}, u32[]{:S(2)}) collective-permute-start(bf16[2,1024,128]{2,1,0:T(8,128)(2,1)S(1)} %collective-permute-done.refs_1_), channel_id=1, source_target_pairs={{0,8},{8,0},{16,24},{24,16},{32,40},{40,32},{48,56},{56,48},{1,9},... | collective-permute-start | bytes 1572872 | tf_op jit(solution)/shard_map/ppermute | solution.py:363
  31.8 14.4 %all-to-all-start.1 = ((bf16[4,4,72,128]{3,2,1,0:T(8,128)(2,1)}), bf16[4,4,72,128]{3,2,1,0:T(8,128)(2,1)S(1)}, u32[]{:S(2)}, u32[]{:S(2)}) async-start(bf16[4,4,72,128]{3,2,1,0:T(8,128)(2,1)} %spread.1), calls=%async_computation.1 | async-start | bytes 589824 | tf_op jit(solution)/shard_map/all_to_all | solution.py:329
  46.3 0.8 copy-start.2
  50.2 38.6 %collective-permute-start.3 = (bf16[128,8192]{1,0:T(8,128)(2,1)}, bf16[128,8192]{1,0:T(8,128)(2,1)S(1)}, u32[]{:S(2)}, u32[]{:S(2)}) collective-permute-start(bf16[128,8192]{1,0:T(8,128)(2,1)} %constant_dynamic-slice_fusion), channel_id=1, source_target_pairs={{0,8},{8,0},{16,24},{24,16},{32,40},{40,32},{48,56},{56,48},{1,9},... | collective-permute-start | bytes 6291464 | tf_op jit(solution)/shard_map/ppermute | solution.py:370
  53.8 1.0 copy-start.1
  54.8 1.0 copy-start.3
  125.2 7.1 %collective-permute-start.4 = (bf16[128,128]{1,0:T(8,128)(2,1)S(1)}, bf16[128,128]{1,0:T(8,128)(2,1)S(1)}, u32[]{:S(2)}, u32[]{:S(2)}) collective-permute-start(bf16[128,128]{1,0:T(8,128)(2,1)S(1)} %reduce_sum.12), channel_id=1, source_target_pairs={{0,64},{64,128},{128,192},{192,256},{256,320},{320,384},{384,448},... | collective-permute-start | bytes 98312 | tf_op jit(solution)/shard_map/ppermute | solution.py:379

commit v6 on v5

--- a/solution.py
+++ b/solution.py
@@ -51,13 +51,17 @@
     return jnp.where(condition, 1.0, 0.0).astype(BF)
 
 
-def prepare_kernel(q_hbm, id_hbm, out_ref, q_ref, id_ref, tmp, sems):
-    q_copy = pltpu.make_async_copy(q_hbm, q_ref, sems.at[0])
-    id_copy = pltpu.make_async_copy(id_hbm, id_ref, sems.at[1])
-    q_copy.start()
-    id_copy.start()
-    q_copy.wait()
-    id_copy.wait()
+def prepare_kernel(q_hbm, id_hbm, k_hbm, v_hbm, out_ref, pages_hbm, q_ref, id_ref, tmp, sems):
+    copies = [
+        pltpu.make_async_copy(q_hbm, q_ref, sems.at[0]),
+        pltpu.make_async_copy(id_hbm, id_ref, sems.at[1]),
+        pltpu.make_async_copy(k_hbm, pages_hbm.at[0], sems.at[2]),
+        pltpu.make_async_copy(v_hbm, pages_hbm.at[1], sems.at[3]),
+    ]
+    for copy in copies:
+        copy.start()
+    copies[0].wait()
+    copies[1].wait()
     for head in range(HEADS):
         tmp[head : head + 1, :] = q_ref[:, head * HD : (head + 1) * HD].astype(F32)
     ids = id_ref[...]
@@ -67,6 +71,23 @@
     slab = tmp[...].astype(BF)
     for copy in range(SPAN):
         out_ref[copy, :, :] = slab
+    copies[2].wait()
+    copies[3].wait()
+
+
+def halves_kernel(side_ref, w_hbm, mine_ref, given_ref, sems):
+    width = mine_ref.shape[1]
+    side = side_ref[0]
+    mine = pl.ds(pl.multiple_of(side * width, width), width)
+    given = pl.ds(pl.multiple_of((1 - side) * width, width), width)
+    copies = [
+        pltpu.make_async_copy(w_hbm.at[:, given], given_ref, sems.at[0]),
+        pltpu.make_async_copy(w_hbm.at[:, mine], mine_ref, sems.at[1]),
+    ]
+    for copy in copies:
+        copy.start()
+    for copy in copies:
+        copy.wait()
 
 
 def spread_kernel(x_ref, out_ref):
@@ -75,8 +96,14 @@
 
 
 def attend_kernel(place_ref, q_ref, *refs):
-    kv_refs = refs[:SHARE]
-    out_ref, qa, point, acc, s_even, s_odd = refs[SHARE:]
+    kv_hbms = refs[:SHARE]
+    out_ref, kv_refs, sems, qa, point, acc, s_even, s_odd = refs[SHARE:]
+    copies = [
+        pltpu.make_async_copy(kv_hbms[block], kv_refs.at[block], sems.at[block])
+        for block in range(SHARE)
+    ]
+    for copy in copies:
+        copy.start()
     odd = place_ref[SHARE]
     ids = q_ref[:, HEADS:SLAB, :].astype(F32).reshape(OWN * 8, HD).astype(BF)
     i, j = iota((KVH * OWN, OWN * 8), 0), iota((KVH * OWN, OWN * 8), 1)
@@ -111,7 +138,7 @@
 
     def score(block, n):
         keys = jnp.concatenate(
-            [kv_refs[block][0], one_if(page_lane == token_page + block * POOL)], axis=1
+            [kv_refs[block, 0], one_if(page_lane == token_page + block * POOL)], axis=1
         )
         return dot_nt(qa[n * CHUNK : (n + 1) * CHUNK, :], keys)
 
@@ -123,10 +150,12 @@
         new = jnp.maximum(jnp.broadcast_to(top.astype(BF).astype(F32), old.shape), old)
         point[here, :] = new
         p = jnp.exp2(s * (SCALE * LOG2E) - new[:, 0:1] * LOG2E).astype(BF)
-        o = dot(p, jnp.concatenate([kv_refs[block][1], first_lane], axis=1))
+        o = dot(p, jnp.concatenate([kv_refs[block, 1], first_lane], axis=1))
         fade = jnp.exp2((old - new) * LOG2E)
         acc[here, :] = acc[here, :] * jnp.concatenate([fade, fade], axis=1) + o
 
+    for copy in copies:
+        copy.wait()
     chunks = HEADS * OWN // CHUNK
     steps = [(block, n) for block in range(SHARE) for n in range(chunks)]
     slots = (s_even, s_odd)
@@ -180,31 +209,31 @@
         out_ref[head ^ 1, 1, HALF:SMALL, :] = stats
 
 
-def project_kernel(side_ref, r_ref, mine_ref, theirs_ref, out_ref, att):
-    @pl.when(pl.program_id(0) == 0)
-    def _():
-        heads = []
-        for head in range(PAIR):
-            halves = []
-            for rows in range(PAIR):
-                sources = range(rows, LINE, PAIR)
-                stats = [r_ref[src, head, HALF:SMALL, :].astype(F32).T[0:HALF, :] for src in sources]
-                top = functools.reduce(jnp.maximum, [s[:, 0:1] for s in stats])
-                factors = [jnp.exp2((s[:, 0:1] - top) * LOG2E) for s in stats]
-                total = sum(f * (s[:, 1:2] + s[:, 2:3]) for f, s in zip(factors, stats))
-                acc = sum(
-                    f * r_ref[src, head, 0:HALF, :].astype(F32) for src, f in zip(sources, factors)
-                )
-                halves.append((acc / total).astype(BF))
-            heads.append(jnp.concatenate(halves, axis=0))
-        both = jnp.concatenate(heads, axis=1)
-        i, j = iota((ROWS, ROWS), 0), iota((ROWS, ROWS), 1)
-        b, u = i // LINE, i % LINE
-        came_from = (b % PAIR) * HALF + (u % PAIR) * OWN + (b // PAIR) * SPAN + u // PAIR
-        att[...] = dot(one_if(j == came_from), both).astype(BF)
-
-    weight = jnp.concatenate([mine_ref[...], theirs_ref[...]], axis=0)
-    out_ref[...] = dot(att[...], weight).astype(BF)
+def project_kernel(r_ref, mine_ref, theirs_ref, out_ref, att):
+    heads = []
+    for head in range(PAIR):
+        halves = []
+        for rows in range(PAIR):
+            sources = range(rows, LINE, PAIR)
+            stats = [r_ref[src, head, HALF:SMALL, :].astype(F32).T[0:HALF, :] for src in sources]
+            top = functools.reduce(jnp.maximum, [s[:, 0:1] for s in stats])
+            factors = [jnp.exp2((s[:, 0:1] - top) * LOG2E) for s in stats]
+            total = sum(f * (s[:, 1:2] + s[:, 2:3]) for f, s in zip(factors, stats))
+            acc = sum(
+                f * r_ref[src, head, 0:HALF, :].astype(F32) for src, f in zip(sources, factors)
+            )
+            halves.append((acc / total).astype(BF))
+        heads.append(jnp.concatenate(halves, axis=0))
+    both = jnp.concatenate(heads, axis=1)
+    i, j = iota((ROWS, ROWS), 0), iota((ROWS, ROWS), 1)
+    b, u = i // LINE, i % LINE
+    came_from = (b % PAIR) * HALF + (u % PAIR) * OWN + (b // PAIR) * SPAN + u // PAIR
+    att[...] = dot(one_if(j == came_from), both).astype(BF)
+
+    for n in range(out_ref.shape[1] // BLOCK):
+        lanes = slice(n * BLOCK, (n + 1) * BLOCK)
+        weight = jnp.concatenate([mine_ref[:, lanes], theirs_ref[:, lanes]], axis=0)
+        out_ref[:, lanes] = dot(att[...], weight).astype(BF)
 
 
 def add_kernel(x_ref, out_ref, tmp):
@@ -218,25 +247,46 @@
 
 
 VMEM = pl.BlockSpec(memory_space=pltpu.VMEM)
+ANYWHERE = pl.BlockSpec(memory_space=pl.ANY)
 SMEM = pl.BlockSpec(memory_space=pltpu.SMEM)
 PARAMS = pltpu.CompilerParams(vmem_limit_bytes=24 * 2**20)
 
 
-def prepare(queries, ids):
+def in_hbm(value):
+    return pltpu.with_memory_space_constraint(value, pltpu.HBM)
+
+
+def prepare(queries, ids, keys, values):
     return pl.pallas_call(
         prepare_kernel,
-        out_shape=jax.ShapeDtypeStruct((SPAN, SLAB, HD), BF),
-        in_specs=[pl.BlockSpec(memory_space=pltpu.HBM)] * 2,
-        out_specs=VMEM,
+        out_shape=(
+            jax.ShapeDtypeStruct((SPAN, SLAB, HD), BF),
+            pltpu.HBM((2, TOKENS, HD), BF),
+        ),
+        in_specs=[ANYWHERE] * 4,
+        out_specs=(VMEM, ANYWHERE),
         scratch_shapes=[
             pltpu.VMEM(queries.shape, BF),
             pltpu.VMEM(ids.shape, jnp.int32),
             pltpu.VMEM((SLAB, HD), F32),
-            pltpu.SemaphoreType.DMA((2,)),
+            pltpu.SemaphoreType.DMA((4,)),
         ],
         compiler_params=PARAMS,
         name="prepare",
-    )(queries, ids)
+    )(*[in_hbm(value) for value in (queries, ids, keys, values)])
+
+
+def halves(side, weight):
+    half = jax.ShapeDtypeStruct((HD, weight.shape[1] // PAIR), BF)
+    return pl.pallas_call(
+        halves_kernel,
+        out_shape=(half, half),
+        in_specs=[SMEM, ANYWHERE],
+        out_specs=(VMEM, VMEM),
+        scratch_shapes=[pltpu.SemaphoreType.DMA((2,))],
+        compiler_params=PARAMS,
+        name="halves",
+    )(side, in_hbm(weight))
 
 
 def spread(value):
@@ -254,9 +304,11 @@
     return pl.pallas_call(
         attend_kernel,
         out_shape=jax.ShapeDtypeStruct((LINE, (LINE + 1) * OWN, HD), BF),
-        in_specs=[SMEM] + [VMEM] * (1 + SHARE),
+        in_specs=[SMEM, VMEM] + [ANYWHERE] * SHARE,
         out_specs=VMEM,
         scratch_shapes=[
+            pltpu.VMEM((SHARE, 2, TOKENS, HD), BF),
+            pltpu.SemaphoreType.DMA((SHARE,)),
             pltpu.VMEM((HEADS * OWN, 2 * HD), BF),
             pltpu.VMEM((HEADS * OWN, HD), F32),
             pltpu.VMEM((HEADS * OWN, 2 * HD), F32),
@@ -265,7 +317,7 @@
         ],
         compiler_params=PARAMS,
         name="attend",
-    )(place, got, *pages)
+    )(place, got, *[in_hbm(block) for block in pages])
 
 
 def merge(parts):
@@ -279,26 +331,17 @@
     )(parts)
 
 
-def project(side, parts, mine, theirs):
+def project(parts, mine, theirs):
     width = theirs.shape[1]
-    steps = width // BLOCK
     return pl.pallas_call(
         project_kernel,
         out_shape=jax.ShapeDtypeStruct((ROWS, width), BF),
-        grid_spec=pltpu.PrefetchScalarGridSpec(
-            num_scalar_prefetch=1,
-            grid=(steps,),
-            in_specs=[
-                pl.BlockSpec(parts.shape, lambda n, side: (0, 0, 0, 0)),
-                pl.BlockSpec((HD, BLOCK), lambda n, side: (0, n + side[0] * steps)),
-                pl.BlockSpec((HD, BLOCK), lambda n, side: (0, n)),
-            ],
-            out_specs=pl.BlockSpec((ROWS, BLOCK), lambda n, side: (0, n)),
-            scratch_shapes=[pltpu.VMEM((ROWS, PAIR * HD), BF)],
-        ),
+        in_specs=[VMEM] * 3,
+        out_specs=VMEM,
+        scratch_shapes=[pltpu.VMEM((ROWS, PAIR * HD), BF)],
         compiler_params=PARAMS,
         name="project",
-    )(side, parts, mine, theirs)
+    )(parts, mine, theirs)
 
 
 def add(parts):
@@ -329,10 +372,6 @@
     return lax.all_to_all(
         value, ("segment", "dev"), split_axis=0, concat_axis=0, axis_index_groups=groups, tiled=True
     )
-
-
-def in_hbm(value):
-    return pltpu.with_memory_space_constraint(value, pltpu.HBM)
 
 
 def neighbours(groups):
@@ -355,24 +394,26 @@
         place.append(jnp.where(odd == 1, block_u * LINE + block_b, block_b * LINE + block_u))
     place = jnp.stack(place + [odd]).astype(jnp.int32)
 
-    near = exchange(prepare(in_hbm(queries), in_hbm(page_ids.reshape(KVH, SEL))), one_rows)
-    pages = jnp.stack([key_pages.reshape(TOKENS, HD), value_pages.reshape(TOKENS, HD)])
+    payload, pages = prepare(
+        queries,
+        page_ids.reshape(KVH, SEL),
+        key_pages.reshape(TOKENS, HD),
+        value_pages.reshape(TOKENS, HD),
+    )
+    mine, given = halves((b % PAIR).astype(jnp.int32).reshape(1), out_weight)
+    near = exchange(payload, one_rows)
     pages_u = lax.ppermute(pages, both, neighbours(one))
     pages_b = lax.ppermute(pages, both, neighbours(other))
-    near, pages_u, pages_b = lax.optimization_barrier((near, pages_u, pages_b))
-    pages_ub = lax.ppermute(pages_u, both, neighbours(other))
+    near, came_u, _, given = lax.optimization_barrier((near, pages_u, pages_b, given))
+    pages_ub = lax.ppermute(came_u, both, neighbours(other))
     got = exchange(spread(near), other_rows)
-
-    side = b % PAIR
-    width = out_weight.shape[1] // PAIR
-    weight, got, pages_ub = lax.optimization_barrier((out_weight, got, pages_ub))
-    given = lax.dynamic_slice_in_dim(weight, (1 - side) * width, width, axis=1)
+    given, got, _ = lax.optimization_barrier((given, got, pages_ub))
     theirs = lax.ppermute(given, both, neighbours(other))
 
     partial = attend(place, got.reshape(OWN, SLAB, HD), [pages, pages_u, pages_b, pages_ub])
     joined = merge(exchange(partial, one))
     gathered = exchange(joined, other)
-    sums = project(side.astype(jnp.int32).reshape(1), gathered, in_hbm(out_weight), theirs)
+    sums = project(gathered, mine, theirs)
     added = add(exchange(sums.reshape(LINE, LINE, -1), other))
     parts = exchange(added, one)
     projected = jnp.sum(parts.astype(F32), axis=0).astype(BF)

time: 134 us -> 145 us (1.082)
  Pallas kernels: 13.2 us -> 32.2 us
  local copies, waits for them, and re-layouts: 6.77 us -> 2.9 us
  blocking collectives: 75.5 us -> 73 us
  waiting for transfers between devices: 9.55 us -> 7.26 us
  starting transfers between devices: 26.7 us -> 28.6 us
    pallas_call x1 -> x2, Pallas kernels: 0.82 us -> 19.9 us  [the longest x1 17.6 us: prepare(): pl.pallas_call(prepare_kernel, out_shape=(jax.ShapeDtypeStruct((SPAN, SLA...]
    all_to_all x1, starting transfers between devices: 5.91 us -> 9.13 us  [exchange(): lax.all_to_all(value, ('segment', 'dev'), split_axis=0, concat_axis=0, ax...]
    dynamic_slice x1 -> x0, local copies, waits for them, and re-layouts: 3.12 us -> none  [local(): given = lax.dynamic_slice_in_dim(weight, (1 - side) * width, width, axis=1)]
    all_to_all x5, blocking collectives: 75.5 us -> 73 us  [exchange(): lax.all_to_all(value, ('segment', 'dev'), split_axis=0, concat_axis=0, ax...]
    all_to_all x1, waiting for transfers between devices: 8.51 us -> 6.22 us  [exchange(): lax.all_to_all(value, ('segment', 'dev'), split_axis=0, concat_axis=0, ax...]
    pallas_call x1, Pallas kernels: 7.1 us -> 8.65 us  [attend(): pl.pallas_call(attend_kernel, out_shape=jax.ShapeDtypeStruct((LINE, (LINE...]
  transfers between devices with their start and end apart: 6 -> 6, of which waited for: 2 -> 2; matrix products, arithmetic and copies ran while one was open for 0% -> 0% of each run, Pallas kernels for 7% -> 8%
where the time goes in v6:
time: 145 us; the launch traced here: 144 us
  blocking collectives  73 us (50%)
  Pallas kernels  32.2 us (22%)
  starting transfers between devices  28.6 us (20%)
  waiting for transfers between devices  7.26 us (5%)
  local copies, waits for them, and re-layouts  2.9 us (2%)
    all_to_all x5, blocking collectives, exchange(): lax.all_to_all(value, ('segment', 'dev'), split_axis=0, concat_axis=0, ax...  73 us
    pallas_call x1, Pallas kernels, prepare(): pl.pallas_call(prepare_kernel, out_shape=(jax.ShapeDtypeStruct((SPAN, SLA...  17.6 us
    all_to_all x1, starting transfers between devices, exchange(): lax.all_to_all(value, ('segment', 'dev'), split_axis=0, concat_axis=0, ax...  9.13 us
    pallas_call x1, Pallas kernels, attend(): pl.pallas_call(attend_kernel, out_shape=jax.ShapeDtypeStruct((LINE, (LINE...  8.65 us
    all_to_all x1, waiting for transfers between devices, exchange(): lax.all_to_all(value, ('segment', 'dev'), split_axis=0, concat_axis=0, ax...  6.22 us
    ppermute x1, starting transfers between devices, local(): lax.ppermute(projected, 'segment', [(s, (s + 1) % count) for s in range(c...  5.88 us
    ppermute x1, starting transfers between devices, local(): pages_b = lax.ppermute(pages, both, neighbours(other))  4.03 us
    ppermute x1, starting transfers between devices, local(): pages_u = lax.ppermute(pages, both, neighbours(one))  4 us
  transfers between devices with their start and end apart: 6, of which 2 were waited for; matrix products, arithmetic and copies ran while one was open for 0% of the time, Pallas kernels for 8%

profile of v6, /device:TPU:1, one launch (start us, length us, event | category | flops | bytes accessed | tf_op | source)
XLA Modules:
  0.0 144.1 jit_solution(16929409917307935569)
XLA Ops:
  0.0 17.6 %prepare.1 = (bf16[4,72,128]{2,1,0:T(8,128)(2,1)}, bf16[2,1024,128]{2,1,0:T(8,128)(2,1)}) custom-call(bf16[1,8192]{1,0:T(2,128)(2,1)} %q_hbm.1, s32[4,32]{1,0:T(4,128)} %bitcast.21, bf16[1024,128]{1,0:T(8,128)(2,1)} %bitcast.18, bf16[1024,128]{1,0:T(8,128)(2,1)} %bitcast.19), custom_call_target="tpu_custom_call" | custom-call | tf_op jit(solution)/shard_map/prepare/pallas_call | solution.py:260
  17.7 4.0 %collective-permute-start.1 = (bf16[2,1024,128]{2,1,0:T(8,128)(2,1)}, bf16[2,1024,128]{2,1,0:T(8,128)(2,1)S(1)}, u32[]{:S(2)}, u32[]{:S(2)}) collective-permute-start(bf16[2,1024,128]{2,1,0:T(8,128)(2,1)} %get-tuple-element.15.refs_0_), channel_id=1, source_target_pairs={{0,8},{8,0},{16,24},{24,16},{32,40},{40,32},{48,56},{56,48},{1,9},... | collective-permute-start | bytes 1572872 | tf_op jit(solution)/shard_map/ppermute | solution.py:406
  21.7 4.0 %collective-permute-start = (bf16[2,1024,128]{2,1,0:T(8,128)(2,1)}, bf16[2,1024,128]{2,1,0:T(8,128)(2,1)S(1)}, u32[]{:S(2)}, u32[]{:S(2)}) collective-permute-start(bf16[2,1024,128]{2,1,0:T(8,128)(2,1)} %get-tuple-element.15.refs_0_), channel_id=1, source_target_pairs={{0,1},{1,0},{2,3},{3,2},{4,5},{5,4},{6,7},{7,6},{8,9},{9,8},{10,11... | collective-permute-start | bytes 1572872 | tf_op jit(solution)/shard_map/ppermute | solution.py:405
  25.7 9.1 %all-to-all-start = ((bf16[4,72,128]{2,1,0:T(8,128)(2,1)}), bf16[4,72,128]{2,1,0:T(8,128)(2,1)S(1)}, u32[]{:S(2)}, u32[]{:S(2)}) async-start(bf16[4,72,128]{2,1,0:T(8,128)(2,1)} %get-tuple-element.14), calls=%async_computation | async-start | bytes 147456 | tf_op jit(solution)/shard_map/all_to_all | solution.py:372
  34.8 2.2 %halves.1 = (bf16[128,8192]{1,0:T(8,128)(2,1)S(1)}, bf16[128,8192]{1,0:T(8,128)(2,1)S(1)}) custom-call(s32[1]{0:T(128)} %bitcast.8.side_ref, bf16[128,16384]{1,0:T(8,128)(2,1)} %w_hbm.1), custom_call_target="tpu_custom_call" | custom-call | tf_op jit(solution)/shard_map/halves/pallas_call | solution.py:281
  37.1 0.0 copy-start
  37.1 1.3 copy-done
  38.4 6.2 %all-to-all-done.x_ref = bf16[4,72,128]{2,1,0:T(8,128)(2,1)S(1)} async-done(((bf16[4,72,128]{2,1,0:T(8,128)(2,1)}), bf16[4,72,128]{2,1,0:T(8,128)(2,1)S(1)}, u32[]{:S(2)}, u32[]{:S(2)}) %all-to-all-start) | async-done | bytes 73760 | tf_op jit(solution)/shard_map/all_to_all | solution.py:372
  44.6 0.0 collective-permute-done.1.refs_2_
  44.6 0.0 copy-start.1
  44.6 0.0 collective-permute-done.refs_1_
  44.7 0.0 copy-start.2
  44.7 3.2 %collective-permute-start.2 = (bf16[2,1024,128]{2,1,0:T(8,128)(2,1)S(1)}, bf16[2,1024,128]{2,1,0:T(8,128)(2,1)S(1)}, u32[]{:S(2)}, u32[]{:S(2)}) collective-permute-start(bf16[2,1024,128]{2,1,0:T(8,128)(2,1)S(1)} %collective-permute-done.refs_1_), channel_id=1, source_target_pairs={{0,8},{8,0},{16,24},{24,16},{32,40},{40,32},{48,56},{56,48},{1,9},... | collective-permute-start | bytes 1572872 | tf_op jit(solution)/shard_map/ppermute | solution.py:408
  47.9 15.4 %all_to_all.30 = bf16[4,4,72,128]{3,2,1,0:T(8,128)(2,1)S(1)} all-to-all(bf16[4,4,72,128]{3,2,1,0:T(8,128)(2,1)S(1)} %spread.1), channel_id=1, replica_groups={{0,16,32,48},{8,24,40,56},{1,17,33,49},{9,25,41,57},{2,18,34,50},{10,26..., dimensions={0} | all-to-all | bytes 589824 | tf_op jit(solution)/shard_map/all_to_all | solution.py:372
  63.4 0.0 collective-permute-done.2.refs_3_
  63.4 0.0 copy-start.3
  63.4 0.8 copy-done.3
  64.2 2.3 %collective-permute-start.3 = (bf16[128,8192]{1,0:T(8,128)(2,1)}, bf16[128,8192]{1,0:T(8,128)(2,1)}, u32[]{:S(2)}, u32[]{:S(2)}) collective-permute-start(bf16[128,8192]{1,0:T(8,128)(2,1)} %copy-done), channel_id=1, source_target_pairs={{0,8},{8,0},{16,24},{24,16},{32,40},{40,32},{48,56},{56,48},{1,9},... | collective-permute-start | bytes 6291464 | tf_op jit(solution)/shard_map/ppermute | solution.py:411
  66.5 0.1 stack.23.place_ref
  66.6 0.0 copy-done.1
  66.6 0.0 copy-done.2
  66.6 8.7 %attend.1 = bf16[8,144,128]{2,1,0:T(8,128)(2,1)S(1)} custom-call(s32[5]{0:T(128)S(1)} %stack.23.place_ref, bf16[16,72,128]{2,1,0:T(8,128)(2,1)S(1)} %bitcast.17, bf16[2,1024,128]{2,1,0:T(8,128)(2,1)} %get-tuple-element.15.refs_0_, bf16[2,1024,128]{2,1,0:T(8,128)(2,1)} %copy-done.2, bf16[2,1024,128]{2,1,0:T(8,128)(2,1)} %copy-done.1, ...), custom_call_target="tpu_custom_call" | custom-call | tf_op jit(solution)/shard_map/attend/pallas_call | solution.py:304
  75.3 14.7 %all_to_all.31.r_ref = bf16[8,144,128]{2,1,0:T(8,128)(2,1)S(1)} all-to-all(bf16[8,144,128]{2,1,0:T(8,128)(2,1)S(1)} %attend.1), channel_id=1, replica_groups={{0,1,2,3,4,5,6,7},{8,9,10,11,12,13,14,15},{16,17,18,19,20,21,22,23},{24..., dimensions={0} | all-to-all | bytes 589824 | tf_op jit(solution)/shard_map/all_to_all | solution.py:372
  90.0 0.3 merge.1
  90.3 10.7 %all_to_all.32.r_ref = bf16[8,2,40,128]{3,2,1,0:T(8,128)(2,1)S(1)} all-to-all(bf16[8,2,40,128]{3,2,1,0:T(8,128)(2,1)S(1)} %merge.1), channel_id=1, replica_groups={{0,8,16,24,32,40,48,56},{1,9,17,25,33,41,49,57},{2,10,18,26,34,42,50,58..., dimensions={0} | all-to-all | bytes 327680 | tf_op jit(solution)/shard_map/all_to_all | solution.py:372
  101.0 0.0 collective-permute-done.3.theirs_ref
  101.0 2.9 %project.1 = bf16[64,8192]{1,0:T(8,128)(2,1)S(1)} custom-call(bf16[8,2,40,128]{3,2,1,0:T(8,128)(2,1)S(1)} %all_to_all.32.r_ref, bf16[128,8192]{1,0:T(8,128)(2,1)S(1)} %get-tuple-element.21.mine_ref, bf16[128,8192]{1,0:T(8,128)(2,1)} %collective-permute-done.3.theirs_ref), custom_call_target="tpu_custom_call" | custom-call | tf_op jit(solution)/shard_map/project/pallas_call | solution.py:336
  103.9 20.5 %all_to_all.33.x_ref = bf16[8,8,8192]{2,1,0:T(8,128)(2,1)S(1)} all-to-all(bf16[8,8,8192]{2,1,0:T(8,128)(2,1)S(1)} %bitcast.16), channel_id=1, replica_groups={{0,8,16,24,32,40,48,56},{1,9,17,25,33,41,49,57},{2,10,18,26,34,42,50,58..., dimensions={0} | all-to-all | bytes 2097152 | tf_op jit(solution)/shard_map/all_to_all | solution.py:372
  124.4 0.3 add.48
  124.7 11.7 %all_to_all.34 = bf16[8,128,128]{2,1,0:T(8,128)(2,1)S(1)} all-to-all(bf16[8,128,128]{2,1,0:T(8,128)(2,1)S(1)} %add.48), channel_id=1, replica_groups={{0,1,2,3,4,5,6,7},{8,9,10,11,12,13,14,15},{16,17,18,19,20,21,22,23},{24..., dimensions={0} | all-to-all | bytes 524288 | tf_op jit(solution)/shard_map/all_to_all | solution.py:372
  136.5 5.9 %collective-permute-start.4 = (bf16[128,128]{1,0:T(8,128)(2,1)S(1)}, bf16[128,128]{1,0:T(8,128)(2,1)S(1)}, u32[]{:S(2)}, u32[]{:S(2)}) collective-permute-start(bf16[128,128]{1,0:T(8,128)(2,1)S(1)} %reduce_sum.12), channel_id=1, source_target_pairs={{0,64},{64,128},{128,192},{192,256},{256,320},{320,384},{384,448},... | collective-permute-start | bytes 98312 | tf_op jit(solution)/shard_map/ppermute | solution.py:420
  142.4 1.0 collective-permute-done.4
  143.4 0.7 copy.8
  (2 shorter events, 0.1 us)
Async XLA Ops:
  17.7 27.0 %collective-permute-start.1 = (bf16[2,1024,128]{2,1,0:T(8,128)(2,1)}, bf16[2,1024,128]{2,1,0:T(8,128)(2,1)S(1)}, u32[]{:S(2)}, u32[]{:S(2)}) collective-permute-start(bf16[2,1024,128]{2,1,0:T(8,128)(2,1)} %get-tuple-element.15.refs_0_), channel_id=1, source_target_pairs={{0,8},{8,0},{16,24},{24,16},{32,40},{40,32},{48,56},{56,48},{1,9},... | collective-permute-start | bytes 1572872 | tf_op jit(solution)/shard_map/ppermute | solution.py:406
  21.7 23.0 %collective-permute-start = (bf16[2,1024,128]{2,1,0:T(8,128)(2,1)}, bf16[2,1024,128]{2,1,0:T(8,128)(2,1)S(1)}, u32[]{:S(2)}, u32[]{:S(2)}) collective-permute-start(bf16[2,1024,128]{2,1,0:T(8,128)(2,1)} %get-tuple-element.15.refs_0_), channel_id=1, source_target_pairs={{0,1},{1,0},{2,3},{3,2},{4,5},{5,4},{6,7},{7,6},{8,9},{9,8},{10,11... | collective-permute-start | bytes 1572872 | tf_op jit(solution)/shard_map/ppermute | solution.py:405
  25.7 18.9 %all-to-all-start = ((bf16[4,72,128]{2,1,0:T(8,128)(2,1)}), bf16[4,72,128]{2,1,0:T(8,128)(2,1)S(1)}, u32[]{:S(2)}, u32[]{:S(2)}) async-start(bf16[4,72,128]{2,1,0:T(8,128)(2,1)} %get-tuple-element.14), calls=%async_computation | async-start | bytes 147456 | tf_op jit(solution)/shard_map/all_to_all | solution.py:372
  37.1 1.3 copy-start
  44.6 21.9 %copy-start.1 = (bf16[2,1024,128]{2,1,0:T(8,128)(2,1)}, bf16[2,1024,128]{2,1,0:T(8,128)(2,1)S(1)}, u32[]{:S(2)}) copy-start(bf16[2,1024,128]{2,1,0:T(8,128)(2,1)S(1)} %collective-permute-done.1.refs_2_) | copy-start | bytes 1572868
  44.7 21.9 %copy-start.2 = (bf16[2,1024,128]{2,1,0:T(8,128)(2,1)}, bf16[2,1024,128]{2,1,0:T(8,128)(2,1)S(1)}, u32[]{:S(2)}) copy-start(bf16[2,1024,128]{2,1,0:T(8,128)(2,1)S(1)} %collective-permute-done.refs_1_) | copy-start | bytes 1572868
  44.7 18.7 %collective-permute-start.2 = (bf16[2,1024,128]{2,1,0:T(8,128)(2,1)S(1)}, bf16[2,1024,128]{2,1,0:T(8,128)(2,1)S(1)}, u32[]{:S(2)}, u32[]{:S(2)}) collective-permute-start(bf16[2,1024,128]{2,1,0:T(8,128)(2,1)S(1)} %collective-permute-done.refs_1_), channel_id=1, source_target_pairs={{0,8},{8,0},{16,24},{24,16},{32,40},{40,32},{48,56},{56,48},{1,9},... | collective-permute-start | bytes 1572872 | tf_op jit(solution)/shard_map/ppermute | solution.py:408
  63.4 0.8 copy-start.3
  64.2 36.8 %collective-permute-start.3 = (bf16[128,8192]{1,0:T(8,128)(2,1)}, bf16[128,8192]{1,0:T(8,128)(2,1)}, u32[]{:S(2)}, u32[]{:S(2)}) collective-permute-start(bf16[128,8192]{1,0:T(8,128)(2,1)} %copy-done), channel_id=1, source_target_pairs={{0,8},{8,0},{16,24},{24,16},{32,40},{40,32},{48,56},{56,48},{1,9},... | collective-permute-start | bytes 6291464 | tf_op jit(solution)/shard_map/ppermute | solution.py:411
  136.5 6.9 %collective-permute-start.4 = (bf16[128,128]{1,0:T(8,128)(2,1)S(1)}, bf16[128,128]{1,0:T(8,128)(2,1)S(1)}, u32[]{:S(2)}, u32[]{:S(2)}) collective-permute-start(bf16[128,128]{1,0:T(8,128)(2,1)S(1)} %reduce_sum.12), channel_id=1, source_target_pairs={{0,64},{64,128},{128,192},{192,256},{256,320},{320,384},{384,448},... | collective-permute-start | bytes 98312 | tf_op jit(solution)/shard_map/ppermute | solution.py:420

commit v7 on v6

--- a/solution.py
+++ b/solution.py
@@ -51,12 +51,12 @@
     return jnp.where(condition, 1.0, 0.0).astype(BF)
 
 
-def prepare_kernel(q_hbm, id_hbm, k_hbm, v_hbm, out_ref, pages_hbm, q_ref, id_ref, tmp, sems):
+def prepare_kernel(q_hbm, id_hbm, k_hbm, v_hbm, out_ref, pages_ref, q_ref, id_ref, tmp, sems):
     copies = [
         pltpu.make_async_copy(q_hbm, q_ref, sems.at[0]),
         pltpu.make_async_copy(id_hbm, id_ref, sems.at[1]),
-        pltpu.make_async_copy(k_hbm, pages_hbm.at[0], sems.at[2]),
-        pltpu.make_async_copy(v_hbm, pages_hbm.at[1], sems.at[3]),
+        pltpu.make_async_copy(k_hbm, pages_ref.at[0], sems.at[2]),
+        pltpu.make_async_copy(v_hbm, pages_ref.at[1], sems.at[3]),
     ]
     for copy in copies:
         copy.start()
@@ -137,6 +137,8 @@
     token_page, page_lane = iota((TOKENS, HD), 0) // PAGE, iota((TOKENS, HD), 1)
 
     def score(block, n):
+        if n == 0:
+            copies[block].wait()
         keys = jnp.concatenate(
             [kv_refs[block, 0], one_if(page_lane == token_page + block * POOL)], axis=1
         )
@@ -154,8 +156,6 @@
         fade = jnp.exp2((old - new) * LOG2E)
         acc[here, :] = acc[here, :] * jnp.concatenate([fade, fade], axis=1) + o
 
-    for copy in copies:
-        copy.wait()
     chunks = HEADS * OWN // CHUNK
     steps = [(block, n) for block in range(SHARE) for n in range(chunks)]
     slots = (s_even, s_odd)
@@ -209,7 +209,9 @@
         out_ref[head ^ 1, 1, HALF:SMALL, :] = stats
 
 
-def project_kernel(r_ref, mine_ref, theirs_ref, out_ref, att):
+def project_kernel(r_ref, mine_ref, theirs_hbm, out_ref, att, theirs_ref, sem):
+    copy = pltpu.make_async_copy(theirs_hbm, theirs_ref, sem)
+    copy.start()
     heads = []
     for head in range(PAIR):
         halves = []
@@ -230,6 +232,7 @@
     came_from = (b % PAIR) * HALF + (u % PAIR) * OWN + (b // PAIR) * SPAN + u // PAIR
     att[...] = dot(one_if(j == came_from), both).astype(BF)
 
+    copy.wait()
     for n in range(out_ref.shape[1] // BLOCK):
         lanes = slice(n * BLOCK, (n + 1) * BLOCK)
         weight = jnp.concatenate([mine_ref[:, lanes], theirs_ref[:, lanes]], axis=0)
@@ -261,10 +264,10 @@
         prepare_kernel,
         out_shape=(
             jax.ShapeDtypeStruct((SPAN, SLAB, HD), BF),
-            pltpu.HBM((2, TOKENS, HD), BF),
+            jax.ShapeDtypeStruct((2, TOKENS, HD), BF),
         ),
         in_specs=[ANYWHERE] * 4,
-        out_specs=(VMEM, ANYWHERE),
+        out_specs=(VMEM, VMEM),
         scratch_shapes=[
             pltpu.VMEM(queries.shape, BF),
             pltpu.VMEM(ids.shape, jnp.int32),
@@ -317,7 +320,7 @@
         ],
         compiler_params=PARAMS,
         name="attend",
-    )(place, got, *[in_hbm(block) for block in pages])
+    )(place, got, pages[0], *[in_hbm(block) for block in pages[1:]])
 
 
 def merge(parts):
@@ -336,9 +339,13 @@
     return pl.pallas_call(
         project_kernel,
         out_shape=jax.ShapeDtypeStruct((ROWS, width), BF),
-        in_specs=[VMEM] * 3,
+        in_specs=[VMEM, VMEM, ANYWHERE],
         out_specs=VMEM,
-        scratch_shapes=[pltpu.VMEM((ROWS, PAIR * HD), BF)],
+        scratch_shapes=[
+            pltpu.VMEM((ROWS, PAIR * HD), BF),
+            pltpu.VMEM(theirs.shape, BF),
+            pltpu.SemaphoreType.DMA,
+        ],
         compiler_params=PARAMS,
         name="project",
     )(parts, mine, theirs)

time: 145 us -> 128 us (0.88)
  Pallas kernels: 32.2 us -> 16 us
    pallas_call x1, Pallas kernels: 17.6 us -> 1.73 us  [prepare(): pl.pallas_call(prepare_kernel, out_shape=(jax.ShapeDtypeStruct((SPAN, SLA...]
  transfers between devices with their start and end apart: 6 -> 6, of which waited for: 2 -> 2; matrix products, arithmetic and copies ran while one was open for 0% -> 0% of each run, Pallas kernels for 8% -> 9%
where the time goes in v7:
time: 128 us; the launch traced here: 127 us
  blocking collectives  72.4 us (57%)
  starting transfers between devices  29.5 us (23%)
  Pallas kernels  16 us (12%)
  waiting for transfers between devices  7.03 us (5%)
  local copies, waits for them, and re-layouts  2.11 us (2%)
    all_to_all x5, blocking collectives, exchange(): lax.all_to_all(value, ('segment', 'dev'), split_axis=0, concat_axis=0, ax...  72.4 us
    all_to_all x1, starting transfers between devices, exchange(): lax.all_to_all(value, ('segment', 'dev'), split_axis=0, concat_axis=0, ax...  9.13 us
    pallas_call x1, Pallas kernels, attend(): pl.pallas_call(attend_kernel, out_shape=jax.ShapeDtypeStruct((LINE, (LINE...  8.4 us
    ppermute x1, starting transfers between devices, local(): lax.ppermute(projected, 'segment', [(s, (s + 1) % count) for s in range(c...  6.7 us
    all_to_all x1, waiting for transfers between devices, exchange(): lax.all_to_all(value, ('segment', 'dev'), split_axis=0, concat_axis=0, ax...  6 us
    ppermute x1, starting transfers between devices, local(): pages_b = lax.ppermute(pages, both, neighbours(other))  4.03 us
    ppermute x1, starting transfers between devices, local(): pages_u = lax.ppermute(pages, both, neighbours(one))  4 us
    ppermute x1, starting transfers between devices, local(): pages_ub = lax.ppermute(came_u, both, neighbours(other))  3.21 us
  transfers between devices with their start and end apart: 6, of which 2 were waited for; matrix products, arithmetic and copies ran while one was open for 0% of the time, Pallas kernels for 9%

profile of v7, /device:TPU:1, one launch (start us, length us, event | category | flops | bytes accessed | tf_op | source)
XLA Modules:
  0.0 127.2 jit_solution(1352309334054015929)
XLA Ops:
  0.0 1.7 %prepare.1 = (bf16[4,72,128]{2,1,0:T(8,128)(2,1)}, bf16[2,1024,128]{2,1,0:T(8,128)(2,1)S(1)}) custom-call(bf16[1,8192]{1,0:T(2,128)(2,1)} %q_hbm.1, s32[4,32]{1,0:T(4,128)} %bitcast.21, bf16[1024,128]{1,0:T(8,128)(2,1)} %bitcast.18, bf16[1024,128]{1,0:T(8,128)(2,1)} %bitcast.19), custom_call_target="tpu_custom_call" | custom-call | tf_op jit(solution)/shard_map/prepare/pallas_call | solution.py:263
  1.7 4.0 %collective-permute-start.1 = (bf16[2,1024,128]{2,1,0:T(8,128)(2,1)S(1)}, bf16[2,1024,128]{2,1,0:T(8,128)(2,1)S(1)}, u32[]{:S(2)}, u32[]{:S(2)}) collective-permute-start(bf16[2,1024,128]{2,1,0:T(8,128)(2,1)S(1)} %get-tuple-element.15.refs_0_), channel_id=1, source_target_pairs={{0,8},{8,0},{16,24},{24,16},{32,40},{40,32},{48,56},{56,48},{1,9},... | collective-permute-start | bytes 1572872 | tf_op jit(solution)/shard_map/ppermute | solution.py:413
  5.8 4.0 %collective-permute-start = (bf16[2,1024,128]{2,1,0:T(8,128)(2,1)S(1)}, bf16[2,1024,128]{2,1,0:T(8,128)(2,1)}, u32[]{:S(2)}, u32[]{:S(2)}) collective-permute-start(bf16[2,1024,128]{2,1,0:T(8,128)(2,1)S(1)} %get-tuple-element.15.refs_0_), channel_id=1, source_target_pairs={{0,1},{1,0},{2,3},{3,2},{4,5},{5,4},{6,7},{7,6},{8,9},{9,8},{10,11... | collective-permute-start | bytes 1572872 | tf_op jit(solution)/shard_map/ppermute | solution.py:412
  9.8 9.1 %all-to-all-start = ((bf16[4,72,128]{2,1,0:T(8,128)(2,1)}), bf16[4,72,128]{2,1,0:T(8,128)(2,1)S(1)}, u32[]{:S(2)}, u32[]{:S(2)}) async-start(bf16[4,72,128]{2,1,0:T(8,128)(2,1)} %get-tuple-element.14), calls=%async_computation | async-start | bytes 147456 | tf_op jit(solution)/shard_map/all_to_all | solution.py:379
  18.9 2.2 %halves.1 = (bf16[128,8192]{1,0:T(8,128)(2,1)S(1)}, bf16[128,8192]{1,0:T(8,128)(2,1)S(1)}) custom-call(s32[1]{0:T(128)} %bitcast.8.side_ref, bf16[128,16384]{1,0:T(8,128)(2,1)} %w_hbm.1), custom_call_target="tpu_custom_call" | custom-call | tf_op jit(solution)/shard_map/halves/pallas_call | solution.py:284
  21.2 0.0 copy-start
  21.2 1.3 %copy-done = bf16[128,8192]{1,0:T(8,128)(2,1)} copy-done((bf16[128,8192]{1,0:T(8,128)(2,1)}, bf16[128,8192]{1,0:T(8,128)(2,1)S(1)}, u32[]{:S(2)}) %copy-start) | copy-done | bytes 2097176
  22.5 6.0 %all-to-all-done.x_ref = bf16[4,72,128]{2,1,0:T(8,128)(2,1)S(1)} async-done(((bf16[4,72,128]{2,1,0:T(8,128)(2,1)}), bf16[4,72,128]{2,1,0:T(8,128)(2,1)S(1)}, u32[]{:S(2)}, u32[]{:S(2)}) %all-to-all-start) | async-done | bytes 73760 | tf_op jit(solution)/shard_map/all_to_all | solution.py:379
  28.5 0.0 collective-permute-done.1.refs_2_
  28.5 0.0 copy-start.1
  28.5 0.0 collective-permute-done.refs_1_
  28.5 3.2 %collective-permute-start.2 = (bf16[2,1024,128]{2,1,0:T(8,128)(2,1)}, bf16[2,1024,128]{2,1,0:T(8,128)(2,1)}, u32[]{:S(2)}, u32[]{:S(2)}) collective-permute-start(bf16[2,1024,128]{2,1,0:T(8,128)(2,1)} %collective-permute-done.refs_1_), channel_id=1, source_target_pairs={{0,8},{8,0},{16,24},{24,16},{32,40},{40,32},{48,56},{56,48},{1,9},... | collective-permute-start | bytes 1572872 | tf_op jit(solution)/shard_map/ppermute | solution.py:415
  31.8 15.2 %all_to_all.30 = bf16[4,4,72,128]{3,2,1,0:T(8,128)(2,1)S(1)} all-to-all(bf16[4,4,72,128]{3,2,1,0:T(8,128)(2,1)S(1)} %spread.1), channel_id=1, replica_groups={{0,16,32,48},{8,24,40,56},{1,17,33,49},{9,25,41,57},{2,18,34,50},{10,26..., dimensions={0} | all-to-all | bytes 589824 | tf_op jit(solution)/shard_map/all_to_all | solution.py:379
  47.0 0.0 collective-permute-done.2.refs_3_
  47.0 2.4 %collective-permute-start.3 = (bf16[128,8192]{1,0:T(8,128)(2,1)}, bf16[128,8192]{1,0:T(8,128)(2,1)}, u32[]{:S(2)}, u32[]{:S(2)}) collective-permute-start(bf16[128,8192]{1,0:T(8,128)(2,1)} %copy-done), channel_id=1, source_target_pairs={{0,8},{8,0},{16,24},{24,16},{32,40},{40,32},{48,56},{56,48},{1,9},... | collective-permute-start | bytes 6291464 | tf_op jit(solution)/shard_map/ppermute | solution.py:418
  49.4 0.1 stack.23.place_ref
  49.5 0.0 copy-done.1
  49.5 8.4 %attend.1 = bf16[8,144,128]{2,1,0:T(8,128)(2,1)S(1)} custom-call(s32[5]{0:T(128)S(1)} %stack.23.place_ref, bf16[16,72,128]{2,1,0:T(8,128)(2,1)S(1)} %bitcast.17, bf16[2,1024,128]{2,1,0:T(8,128)(2,1)S(1)} %get-tuple-element.15.refs_0_, bf16[2,1024,128]{2,1,0:T(8,128)(2,1)} %collective-permute-done.refs_1_, bf16[2,1024,128]{2,1,0:T(8,128)(2,1)} %copy-done.1, ...), custom_call_target="tpu_custom_call" | custom-call | tf_op jit(solution)/shard_map/attend/pallas_call | solution.py:307
  57.9 14.6 %all_to_all.31.r_ref = bf16[8,144,128]{2,1,0:T(8,128)(2,1)S(1)} all-to-all(bf16[8,144,128]{2,1,0:T(8,128)(2,1)S(1)} %attend.1), channel_id=1, replica_groups={{0,1,2,3,4,5,6,7},{8,9,10,11,12,13,14,15},{16,17,18,19,20,21,22,23},{24..., dimensions={0} | all-to-all | bytes 589824 | tf_op jit(solution)/shard_map/all_to_all | solution.py:379
  72.5 0.3 merge.1
  72.9 10.7 %all_to_all.32.r_ref = bf16[8,2,40,128]{3,2,1,0:T(8,128)(2,1)S(1)} all-to-all(bf16[8,2,40,128]{3,2,1,0:T(8,128)(2,1)S(1)} %merge.1), channel_id=1, replica_groups={{0,8,16,24,32,40,48,56},{1,9,17,25,33,41,49,57},{2,10,18,26,34,42,50,58..., dimensions={0} | all-to-all | bytes 327680 | tf_op jit(solution)/shard_map/all_to_all | solution.py:379
  83.5 0.0 collective-permute-done.3.theirs_hbm
  83.5 2.9 %project.1 = bf16[64,8192]{1,0:T(8,128)(2,1)S(1)} custom-call(bf16[8,2,40,128]{3,2,1,0:T(8,128)(2,1)S(1)} %all_to_all.32.r_ref, bf16[128,8192]{1,0:T(8,128)(2,1)S(1)} %get-tuple-element.21.mine_ref, bf16[128,8192]{1,0:T(8,128)(2,1)} %collective-permute-done.3.theirs_hbm), custom_call_target="tpu_custom_call" | custom-call | tf_op jit(solution)/shard_map/project/pallas_call | solution.py:339
  86.5 20.2 %all_to_all.33.x_ref = bf16[8,8,8192]{2,1,0:T(8,128)(2,1)S(1)} all-to-all(bf16[8,8,8192]{2,1,0:T(8,128)(2,1)S(1)} %bitcast.16), channel_id=1, replica_groups={{0,8,16,24,32,40,48,56},{1,9,17,25,33,41,49,57},{2,10,18,26,34,42,50,58..., dimensions={0} | all-to-all | bytes 2097152 | tf_op jit(solution)/shard_map/all_to_all | solution.py:379
  106.7 0.3 add.48
  107.0 11.7 %all_to_all.34 = bf16[8,128,128]{2,1,0:T(8,128)(2,1)S(1)} all-to-all(bf16[8,128,128]{2,1,0:T(8,128)(2,1)S(1)} %add.48), channel_id=1, replica_groups={{0,1,2,3,4,5,6,7},{8,9,10,11,12,13,14,15},{16,17,18,19,20,21,22,23},{24..., dimensions={0} | all-to-all | bytes 524288 | tf_op jit(solution)/shard_map/all_to_all | solution.py:379
  118.8 6.7 %collective-permute-start.4 = (bf16[128,128]{1,0:T(8,128)(2,1)S(1)}, bf16[128,128]{1,0:T(8,128)(2,1)S(1)}, u32[]{:S(2)}, u32[]{:S(2)}) collective-permute-start(bf16[128,128]{1,0:T(8,128)(2,1)S(1)} %reduce_sum.12), channel_id=1, source_target_pairs={{0,64},{64,128},{128,192},{192,256},{256,320},{320,384},{384,448},... | collective-permute-start | bytes 98312 | tf_op jit(solution)/shard_map/ppermute | solution.py:427
  125.5 1.0 collective-permute-done.4
  126.5 0.7 copy.8
  (2 shorter events, 0.1 us)
Async XLA Ops:
  1.7 26.8 %collective-permute-start.1 = (bf16[2,1024,128]{2,1,0:T(8,128)(2,1)S(1)}, bf16[2,1024,128]{2,1,0:T(8,128)(2,1)S(1)}, u32[]{:S(2)}, u32[]{:S(2)}) collective-permute-start(bf16[2,1024,128]{2,1,0:T(8,128)(2,1)S(1)} %get-tuple-element.15.refs_0_), channel_id=1, source_target_pairs={{0,8},{8,0},{16,24},{24,16},{32,40},{40,32},{48,56},{56,48},{1,9},... | collective-permute-start | bytes 1572872 | tf_op jit(solution)/shard_map/ppermute | solution.py:413
  5.8 22.7 %collective-permute-start = (bf16[2,1024,128]{2,1,0:T(8,128)(2,1)S(1)}, bf16[2,1024,128]{2,1,0:T(8,128)(2,1)}, u32[]{:S(2)}, u32[]{:S(2)}) collective-permute-start(bf16[2,1024,128]{2,1,0:T(8,128)(2,1)S(1)} %get-tuple-element.15.refs_0_), channel_id=1, source_target_pairs={{0,1},{1,0},{2,3},{3,2},{4,5},{5,4},{6,7},{7,6},{8,9},{9,8},{10,11... | collective-permute-start | bytes 1572872 | tf_op jit(solution)/shard_map/ppermute | solution.py:412
  9.8 18.7 %all-to-all-start = ((bf16[4,72,128]{2,1,0:T(8,128)(2,1)}), bf16[4,72,128]{2,1,0:T(8,128)(2,1)S(1)}, u32[]{:S(2)}, u32[]{:S(2)}) async-start(bf16[4,72,128]{2,1,0:T(8,128)(2,1)} %get-tuple-element.14), calls=%async_computation | async-start | bytes 147456 | tf_op jit(solution)/shard_map/all_to_all | solution.py:379
  21.2 1.3 %copy-start = (bf16[128,8192]{1,0:T(8,128)(2,1)}, bf16[128,8192]{1,0:T(8,128)(2,1)S(1)}, u32[]{:S(2)}) copy-start(bf16[128,8192]{1,0:T(8,128)(2,1)S(1)} %get-tuple-element.22) | copy-start | bytes 6291460
  28.5 21.0 %copy-start.1 = (bf16[2,1024,128]{2,1,0:T(8,128)(2,1)}, bf16[2,1024,128]{2,1,0:T(8,128)(2,1)S(1)}, u32[]{:S(2)}) copy-start(bf16[2,1024,128]{2,1,0:T(8,128)(2,1)S(1)} %collective-permute-done.1.refs_2_) | copy-start | bytes 1572868
  28.5 18.5 %collective-permute-start.2 = (bf16[2,1024,128]{2,1,0:T(8,128)(2,1)}, bf16[2,1024,128]{2,1,0:T(8,128)(2,1)}, u32[]{:S(2)}, u32[]{:S(2)}) collective-permute-start(bf16[2,1024,128]{2,1,0:T(8,128)(2,1)} %collective-permute-done.refs_1_), channel_id=1, source_target_pairs={{0,8},{8,0},{16,24},{24,16},{32,40},{40,32},{48,56},{56,48},{1,9},... | collective-permute-start | bytes 1572872 | tf_op jit(solution)/shard_map/ppermute | solution.py:415
  47.0 36.5 %collective-permute-start.3 = (bf16[128,8192]{1,0:T(8,128)(2,1)}, bf16[128,8192]{1,0:T(8,128)(2,1)}, u32[]{:S(2)}, u32[]{:S(2)}) collective-permute-start(bf16[128,8192]{1,0:T(8,128)(2,1)} %copy-done), channel_id=1, source_target_pairs={{0,8},{8,0},{16,24},{24,16},{32,40},{40,32},{48,56},{56,48},{1,9},... | collective-permute-start | bytes 6291464 | tf_op jit(solution)/shard_map/ppermute | solution.py:418
  118.8 7.7 %collective-permute-start.4 = (bf16[128,128]{1,0:T(8,128)(2,1)S(1)}, bf16[128,128]{1,0:T(8,128)(2,1)S(1)}, u32[]{:S(2)}, u32[]{:S(2)}) collective-permute-start(bf16[128,128]{1,0:T(8,128)(2,1)S(1)} %reduce_sum.12), channel_id=1, source_target_pairs={{0,64},{64,128},{128,192},{192,256},{256,320},{320,384},{384,448},... | collective-permute-start | bytes 98312 | tf_op jit(solution)/shard_map/ppermute | solution.py:427

commit v8 on v7

--- a/solution.py
+++ b/solution.py
@@ -51,17 +51,15 @@
     return jnp.where(condition, 1.0, 0.0).astype(BF)
 
 
-def prepare_kernel(q_hbm, id_hbm, k_hbm, v_hbm, out_ref, pages_ref, q_ref, id_ref, tmp, sems):
+def prepare_kernel(q_hbm, id_hbm, out_ref, q_ref, id_ref, tmp, sems):
     copies = [
         pltpu.make_async_copy(q_hbm, q_ref, sems.at[0]),
         pltpu.make_async_copy(id_hbm, id_ref, sems.at[1]),
-        pltpu.make_async_copy(k_hbm, pages_ref.at[0], sems.at[2]),
-        pltpu.make_async_copy(v_hbm, pages_ref.at[1], sems.at[3]),
     ]
     for copy in copies:
         copy.start()
-    copies[0].wait()
-    copies[1].wait()
+    for copy in copies:
+        copy.wait()
     for head in range(HEADS):
         tmp[head : head + 1, :] = q_ref[:, head * HD : (head + 1) * HD].astype(F32)
     ids = id_ref[...]
@@ -71,8 +69,6 @@
     slab = tmp[...].astype(BF)
     for copy in range(SPAN):
         out_ref[copy, :, :] = slab
-    copies[2].wait()
-    copies[3].wait()
 
 
 def halves_kernel(side_ref, w_hbm, mine_ref, given_ref, sems):
@@ -83,6 +79,17 @@
     copies = [
         pltpu.make_async_copy(w_hbm.at[:, given], given_ref, sems.at[0]),
         pltpu.make_async_copy(w_hbm.at[:, mine], mine_ref, sems.at[1]),
+    ]
+    for copy in copies:
+        copy.start()
+    for copy in copies:
+        copy.wait()
+
+
+def pack_kernel(k_hbm, v_hbm, pages_ref, sems):
+    copies = [
+        pltpu.make_async_copy(k_hbm, pages_ref.at[0], sems.at[0]),
+        pltpu.make_async_copy(v_hbm, pages_ref.at[1], sems.at[1]),
     ]
     for copy in copies:
         copy.start()
@@ -259,24 +266,33 @@
     return pltpu.with_memory_space_constraint(value, pltpu.HBM)
 
 
-def prepare(queries, ids, keys, values):
+def prepare(queries, ids):
     return pl.pallas_call(
         prepare_kernel,
-        out_shape=(
-            jax.ShapeDtypeStruct((SPAN, SLAB, HD), BF),
-            jax.ShapeDtypeStruct((2, TOKENS, HD), BF),
-        ),
-        in_specs=[ANYWHERE] * 4,
-        out_specs=(VMEM, VMEM),
+        out_shape=jax.ShapeDtypeStruct((SPAN, SLAB, HD), BF),
+        in_specs=[ANYWHERE] * 2,
+        out_specs=VMEM,
         scratch_shapes=[
             pltpu.VMEM(queries.shape, BF),
             pltpu.VMEM(ids.shape, jnp.int32),
             pltpu.VMEM((SLAB, HD), F32),
-            pltpu.SemaphoreType.DMA((4,)),
+            pltpu.SemaphoreType.DMA((2,)),
         ],
         compiler_params=PARAMS,
         name="prepare",
-    )(*[in_hbm(value) for value in (queries, ids, keys, values)])
+    )(in_hbm(queries), in_hbm(ids))
+
+
+def pack(keys, values):
+    return pl.pallas_call(
+        pack_kernel,
+        out_shape=jax.ShapeDtypeStruct((2,) + keys.shape, BF),
+        in_specs=[ANYWHERE] * 2,
+        out_specs=VMEM,
+        scratch_shapes=[pltpu.SemaphoreType.DMA((2,))],
+        compiler_params=PARAMS,
+        name="pack",
+    )(in_hbm(keys), in_hbm(values))
 
 
 def halves(side, weight):
@@ -383,6 +399,13 @@
 
 def neighbours(groups):
     return [(line[k], line[k ^ 1]) for line in groups for k in range(LINE)]
+
+
+def diagonal(groups):
+    pairs = []
+    for number, line in enumerate(groups):
+        pairs += [(line[k], groups[number ^ 1][k ^ 1]) for k in range(LINE)]
+    return pairs
 
 
 def local(queries, page_ids, key_pages, value_pages, out_weight):
@@ -401,20 +424,17 @@
         place.append(jnp.where(odd == 1, block_u * LINE + block_b, block_b * LINE + block_u))
     place = jnp.stack(place + [odd]).astype(jnp.int32)
 
-    payload, pages = prepare(
-        queries,
-        page_ids.reshape(KVH, SEL),
-        key_pages.reshape(TOKENS, HD),
-        value_pages.reshape(TOKENS, HD),
-    )
+    payload = prepare(queries, page_ids.reshape(KVH, SEL))
+    near = exchange(payload, one_rows)
+    keys, values = key_pages.reshape(TOKENS, HD), value_pages.reshape(TOKENS, HD)
+    pages = pack(keys, values)
     mine, given = halves((b % PAIR).astype(jnp.int32).reshape(1), out_weight)
-    near = exchange(payload, one_rows)
     pages_u = lax.ppermute(pages, both, neighbours(one))
     pages_b = lax.ppermute(pages, both, neighbours(other))
-    near, came_u, _, given = lax.optimization_barrier((near, pages_u, pages_b, given))
-    pages_ub = lax.ppermute(came_u, both, neighbours(other))
+    pages_ub = lax.ppermute(pages, both, diagonal(one))
+    near, given = lax.optimization_barrier((near, given))
     got = exchange(spread(near), other_rows)
-    given, got, _ = lax.optimization_barrier((given, got, pages_ub))
+    given, got, *_ = lax.optimization_barrier((given, got, pages_u, pages_b, pages_ub))
     theirs = lax.ppermute(given, both, neighbours(other))
 
     partial = attend(place, got.reshape(OWN, SLAB, HD), [pages, pages_u, pages_b, pages_ub])

time: 128 us -> 135 us (1.055)
  blocking collectives: 72.4 us -> 63.2 us
  starting transfers between devices: 29.5 us -> 36.9 us
  waiting for transfers between devices: 7.03 us -> 14.3 us
  Pallas kernels: 16 us -> 17.5 us
    all_to_all x5 -> x4, blocking collectives: 72.4 us -> 63.2 us  [exchange(): lax.all_to_all(value, ('segment', 'dev'), split_axis=0, concat_axis=0, ax...]
    ppermute x1, waiting for transfers between devices: 0.01 us -> 9.1 us  [local(): pages_ub = lax.ppermute(pages, both, diagonal(one))]
    all_to_all x1 -> x2, starting transfers between devices: 9.13 us -> 17.7 us  [exchange(): lax.all_to_all(value, ('segment', 'dev'), split_axis=0, concat_axis=0, ax...]
    all_to_all x1 -> x2, waiting for transfers between devices: 6 us -> 4.19 us  [exchange(): lax.all_to_all(value, ('segment', 'dev'), split_axis=0, concat_axis=0, ax...]
  transfers between devices with their start and end apart: 6 -> 7, of which waited for: 2 -> 3; matrix products, arithmetic and copies ran while one was open for 0% -> 0% of each run, Pallas kernels for 9% -> 10%
where the time goes in v8:
time: 135 us; the launch traced here: 134 us
  blocking collectives  63.2 us (47%)
  starting transfers between devices  36.9 us (27%)
  Pallas kernels  17.5 us (13%)
  waiting for transfers between devices  14.3 us (11%)
  local copies, waits for them, and re-layouts  2.1 us (2%)
    all_to_all x4, blocking collectives, exchange(): lax.all_to_all(value, ('segment', 'dev'), split_axis=0, concat_axis=0, ax...  63.2 us
    all_to_all x2, starting transfers between devices, exchange(): lax.all_to_all(value, ('segment', 'dev'), split_axis=0, concat_axis=0, ax...  17.7 us
    ppermute x1, waiting for transfers between devices, local(): pages_ub = lax.ppermute(pages, both, diagonal(one))  9.1 us
    pallas_call x1, Pallas kernels, attend(): pl.pallas_call(attend_kernel, out_shape=jax.ShapeDtypeStruct((LINE, (LINE...  8.39 us
    ppermute x1, starting transfers between devices, local(): lax.ppermute(projected, 'segment', [(s, (s + 1) % count) for s in range(c...  7.26 us
    all_to_all x2, waiting for transfers between devices, exchange(): lax.all_to_all(value, ('segment', 'dev'), split_axis=0, concat_axis=0, ax...  4.19 us
    ppermute x1, starting transfers between devices, local(): theirs = lax.ppermute(given, both, neighbours(other))  3.63 us
    ppermute x1, starting transfers between devices, local(): pages_b = lax.ppermute(pages, both, neighbours(other))  3.21 us
  transfers between devices with their start and end apart: 7, of which 3 were waited for; matrix products, arithmetic and copies ran while one was open for 0% of the time, Pallas kernels for 10%

profile of v8, /device:TPU:1, one launch (start us, length us, event | category | flops | bytes accessed | tf_op | source)
XLA Modules:
  0.0 134.3 jit_solution(2028709014098657592)
XLA Ops:
  0.0 1.4 %prepare.1 = bf16[4,72,128]{2,1,0:T(8,128)(2,1)} custom-call(bf16[1,8192]{1,0:T(2,128)(2,1)} %q_hbm.1, s32[4,32]{1,0:T(4,128)} %bitcast.21), custom_call_target="tpu_custom_call" | custom-call | tf_op jit(solution)/shard_map/prepare/pallas_call | solution.py:270
  1.4 10.9 %all-to-all-start = ((bf16[4,72,128]{2,1,0:T(8,128)(2,1)}), bf16[4,72,128]{2,1,0:T(8,128)(2,1)S(1)}, u32[]{:S(2)}, u32[]{:S(2)}) async-start(bf16[4,72,128]{2,1,0:T(8,128)(2,1)} %prepare.1), calls=%async_computation | async-start | bytes 147456 | tf_op jit(solution)/shard_map/all_to_all | solution.py:395
  12.3 1.0 pack.1.refs_0_
  13.4 3.1 %collective-permute-start = (bf16[2,1024,128]{2,1,0:T(8,128)(2,1)S(1)}, bf16[2,1024,128]{2,1,0:T(8,128)(2,1)S(1)}, u32[]{:S(2)}, u32[]{:S(2)}) collective-permute-start(bf16[2,1024,128]{2,1,0:T(8,128)(2,1)S(1)} %pack.1.refs_0_), channel_id=1, source_target_pairs={{0,1},{1,0},{2,3},{3,2},{4,5},{5,4},{6,7},{7,6},{8,9},{9,8},{10,11... | collective-permute-start | bytes 1572872 | tf_op jit(solution)/shard_map/ppermute | solution.py:432
  16.5 3.2 %collective-permute-start.1 = (bf16[2,1024,128]{2,1,0:T(8,128)(2,1)S(1)}, bf16[2,1024,128]{2,1,0:T(8,128)(2,1)}, u32[]{:S(2)}, u32[]{:S(2)}) collective-permute-start(bf16[2,1024,128]{2,1,0:T(8,128)(2,1)S(1)} %pack.1.refs_0_), channel_id=1, source_target_pairs={{0,8},{8,0},{16,24},{24,16},{32,40},{40,32},{48,56},{56,48},{1,9},... | collective-permute-start | bytes 1572872 | tf_op jit(solution)/shard_map/ppermute | solution.py:433
  19.7 2.1 %collective-permute-start.2 = (bf16[2,1024,128]{2,1,0:T(8,128)(2,1)S(1)}, bf16[2,1024,128]{2,1,0:T(8,128)(2,1)}, u32[]{:S(2)}, u32[]{:S(2)}) collective-permute-start(bf16[2,1024,128]{2,1,0:T(8,128)(2,1)S(1)} %pack.1.refs_0_), channel_id=1, source_target_pairs={{0,9},{1,8},{2,11},{3,10},{4,13},{5,12},{6,15},{7,14},{8,1},{9,0},... | collective-permute-start | bytes 1572872 | tf_op jit(solution)/shard_map/ppermute | solution.py:434
  21.8 2.2 %halves.1 = (bf16[128,8192]{1,0:T(8,128)(2,1)S(1)}, bf16[128,8192]{1,0:T(8,128)(2,1)S(1)}) custom-call(s32[1]{0:T(128)} %bitcast.6.side_ref, bf16[128,16384]{1,0:T(8,128)(2,1)} %w_hbm.1), custom_call_target="tpu_custom_call" | custom-call | tf_op jit(solution)/shard_map/halves/pallas_call | solution.py:300
  24.1 0.0 copy-start
  24.1 1.3 copy-done
  25.4 0.0 all-to-all-done.x_ref
  25.4 0.7 spread.1
  26.1 6.8 %all-to-all-start.1 = ((bf16[4,4,72,128]{3,2,1,0:T(8,128)(2,1)}), bf16[4,4,72,128]{3,2,1,0:T(8,128)(2,1)S(1)}, u32[]{:S(2)}, u32[]{:S(2)}) async-start(bf16[4,4,72,128]{3,2,1,0:T(8,128)(2,1)} %spread.1), calls=%async_computation.1 | async-start | bytes 589824 | tf_op jit(solution)/shard_map/all_to_all | solution.py:395
  33.0 0.0 collective-permute-done.refs_1_
  33.0 0.0 copy-start.1
  33.0 0.0 collective-permute-done.1.refs_2_
  33.0 9.1 %collective-permute-done.2.refs_3_ = bf16[2,1024,128]{2,1,0:T(8,128)(2,1)} collective-permute-done((bf16[2,1024,128]{2,1,0:T(8,128)(2,1)S(1)}, bf16[2,1024,128]{2,1,0:T(8,128)(2,1)}, u32[]{:S(2)}, u32[]{:S(2)}) %collective-permute-start.2) | collective-permute-done | bytes 524320 | tf_op jit(solution)/shard_map/ppermute | solution.py:434
  42.1 4.2 %all-to-all-done.1 = bf16[4,4,72,128]{3,2,1,0:T(8,128)(2,1)S(1)} async-done(((bf16[4,4,72,128]{3,2,1,0:T(8,128)(2,1)}), bf16[4,4,72,128]{3,2,1,0:T(8,128)(2,1)S(1)}, u32[]{:S(2)}, u32[]{:S(2)}) %all-to-all-start.1) | async-done | bytes 294944 | tf_op jit(solution)/shard_map/all_to_all | solution.py:395
  46.3 3.6 %collective-permute-start.3 = (bf16[128,8192]{1,0:T(8,128)(2,1)}, bf16[128,8192]{1,0:T(8,128)(2,1)}, u32[]{:S(2)}, u32[]{:S(2)}) collective-permute-start(bf16[128,8192]{1,0:T(8,128)(2,1)} %copy-done), channel_id=1, source_target_pairs={{0,8},{8,0},{16,24},{24,16},{32,40},{40,32},{48,56},{56,48},{1,9},... | collective-permute-start | bytes 6291464 | tf_op jit(solution)/shard_map/ppermute | solution.py:438
  49.9 0.1 stack.23.place_ref
  50.0 0.0 copy-done.1
  50.0 8.4 %attend.1 = bf16[8,144,128]{2,1,0:T(8,128)(2,1)S(1)} custom-call(s32[5]{0:T(128)S(1)} %stack.23.place_ref, bf16[16,72,128]{2,1,0:T(8,128)(2,1)S(1)} %bitcast.17, bf16[2,1024,128]{2,1,0:T(8,128)(2,1)S(1)} %pack.1.refs_0_, bf16[2,1024,128]{2,1,0:T(8,128)(2,1)} %copy-done.1, bf16[2,1024,128]{2,1,0:T(8,128)(2,1)} %collective-permute-done.1.refs_2_, ...), custom_call_target="tpu_custom_call" | custom-call | tf_op jit(solution)/shard_map/attend/pallas_call | solution.py:323
  58.4 20.6 %all_to_all.30.r_ref = bf16[8,144,128]{2,1,0:T(8,128)(2,1)S(1)} all-to-all(bf16[8,144,128]{2,1,0:T(8,128)(2,1)S(1)} %attend.1), channel_id=1, replica_groups={{0,1,2,3,4,5,6,7},{8,9,10,11,12,13,14,15},{16,17,18,19,20,21,22,23},{24..., dimensions={0} | all-to-all | bytes 589824 | tf_op jit(solution)/shard_map/all_to_all | solution.py:395
  79.0 0.3 merge.1
  79.4 10.7 %all_to_all.31.r_ref = bf16[8,2,40,128]{3,2,1,0:T(8,128)(2,1)S(1)} all-to-all(bf16[8,2,40,128]{3,2,1,0:T(8,128)(2,1)S(1)} %merge.1), channel_id=1, replica_groups={{0,8,16,24,32,40,48,56},{1,9,17,25,33,41,49,57},{2,10,18,26,34,42,50,58..., dimensions={0} | all-to-all | bytes 327680 | tf_op jit(solution)/shard_map/all_to_all | solution.py:395
  90.1 0.0 collective-permute-done.3.theirs_hbm
  90.1 2.9 %project.1 = bf16[64,8192]{1,0:T(8,128)(2,1)S(1)} custom-call(bf16[8,2,40,128]{3,2,1,0:T(8,128)(2,1)S(1)} %all_to_all.31.r_ref, bf16[128,8192]{1,0:T(8,128)(2,1)S(1)} %get-tuple-element.15.mine_ref, bf16[128,8192]{1,0:T(8,128)(2,1)} %collective-permute-done.3.theirs_hbm), custom_call_target="tpu_custom_call" | custom-call | tf_op jit(solution)/shard_map/project/pallas_call | solution.py:355
  93.0 20.2 %all_to_all.32.x_ref = bf16[8,8,8192]{2,1,0:T(8,128)(2,1)S(1)} all-to-all(bf16[8,8,8192]{2,1,0:T(8,128)(2,1)S(1)} %bitcast.16), channel_id=1, replica_groups={{0,8,16,24,32,40,48,56},{1,9,17,25,33,41,49,57},{2,10,18,26,34,42,50,58..., dimensions={0} | all-to-all | bytes 2097152 | tf_op jit(solution)/shard_map/all_to_all | solution.py:395
  113.2 0.3 add.48
  113.5 11.7 %all_to_all.33 = bf16[8,128,128]{2,1,0:T(8,128)(2,1)S(1)} all-to-all(bf16[8,128,128]{2,1,0:T(8,128)(2,1)S(1)} %add.48), channel_id=1, replica_groups={{0,1,2,3,4,5,6,7},{8,9,10,11,12,13,14,15},{16,17,18,19,20,21,22,23},{24..., dimensions={0} | all-to-all | bytes 524288 | tf_op jit(solution)/shard_map/all_to_all | solution.py:395
  125.3 7.3 %collective-permute-start.4 = (bf16[128,128]{1,0:T(8,128)(2,1)S(1)}, bf16[128,128]{1,0:T(8,128)(2,1)S(1)}, u32[]{:S(2)}, u32[]{:S(2)}) collective-permute-start(bf16[128,128]{1,0:T(8,128)(2,1)S(1)} %reduce_sum.12), channel_id=1, source_target_pairs={{0,64},{64,128},{128,192},{192,256},{256,320},{320,384},{384,448},... | collective-permute-start | bytes 98312 | tf_op jit(solution)/shard_map/ppermute | solution.py:447
  132.6 1.0 collective-permute-done.4
  133.6 0.7 copy.8
  (1 shorter events, 0.0 us)
Async XLA Ops:
  1.4 24.0 %all-to-all-start = ((bf16[4,72,128]{2,1,0:T(8,128)(2,1)}), bf16[4,72,128]{2,1,0:T(8,128)(2,1)S(1)}, u32[]{:S(2)}, u32[]{:S(2)}) async-start(bf16[4,72,128]{2,1,0:T(8,128)(2,1)} %prepare.1), calls=%async_computation | async-start | bytes 147456 | tf_op jit(solution)/shard_map/all_to_all | solution.py:395
  13.4 19.6 %collective-permute-start = (bf16[2,1024,128]{2,1,0:T(8,128)(2,1)S(1)}, bf16[2,1024,128]{2,1,0:T(8,128)(2,1)S(1)}, u32[]{:S(2)}, u32[]{:S(2)}) collective-permute-start(bf16[2,1024,128]{2,1,0:T(8,128)(2,1)S(1)} %pack.1.refs_0_), channel_id=1, source_target_pairs={{0,1},{1,0},{2,3},{3,2},{4,5},{5,4},{6,7},{7,6},{8,9},{9,8},{10,11... | collective-permute-start | bytes 1572872 | tf_op jit(solution)/shard_map/ppermute | solution.py:432
  16.5 16.5 %collective-permute-start.1 = (bf16[2,1024,128]{2,1,0:T(8,128)(2,1)S(1)}, bf16[2,1024,128]{2,1,0:T(8,128)(2,1)}, u32[]{:S(2)}, u32[]{:S(2)}) collective-permute-start(bf16[2,1024,128]{2,1,0:T(8,128)(2,1)S(1)} %pack.1.refs_0_), channel_id=1, source_target_pairs={{0,8},{8,0},{16,24},{24,16},{32,40},{40,32},{48,56},{56,48},{1,9},... | collective-permute-start | bytes 1572872 | tf_op jit(solution)/shard_map/ppermute | solution.py:433
  19.7 22.4 %collective-permute-start.2 = (bf16[2,1024,128]{2,1,0:T(8,128)(2,1)S(1)}, bf16[2,1024,128]{2,1,0:T(8,128)(2,1)}, u32[]{:S(2)}, u32[]{:S(2)}) collective-permute-start(bf16[2,1024,128]{2,1,0:T(8,128)(2,1)S(1)} %pack.1.refs_0_), channel_id=1, source_target_pairs={{0,9},{1,8},{2,11},{3,10},{4,13},{5,12},{6,15},{7,14},{8,1},{9,0},... | collective-permute-start | bytes 1572872 | tf_op jit(solution)/shard_map/ppermute | solution.py:434
  24.1 1.3 copy-start
  26.1 20.1 %all-to-all-start.1 = ((bf16[4,4,72,128]{3,2,1,0:T(8,128)(2,1)}), bf16[4,4,72,128]{3,2,1,0:T(8,128)(2,1)S(1)}, u32[]{:S(2)}, u32[]{:S(2)}) async-start(bf16[4,4,72,128]{3,2,1,0:T(8,128)(2,1)} %spread.1), calls=%async_computation.1 | async-start | bytes 589824 | tf_op jit(solution)/shard_map/all_to_all | solution.py:395
  33.0 17.1 %copy-start.1 = (bf16[2,1024,128]{2,1,0:T(8,128)(2,1)}, bf16[2,1024,128]{2,1,0:T(8,128)(2,1)S(1)}, u32[]{:S(2)}) copy-start(bf16[2,1024,128]{2,1,0:T(8,128)(2,1)S(1)} %collective-permute-done.refs_1_) | copy-start | bytes 1572868
  46.3 43.8 %collective-permute-start.3 = (bf16[128,8192]{1,0:T(8,128)(2,1)}, bf16[128,8192]{1,0:T(8,128)(2,1)}, u32[]{:S(2)}, u32[]{:S(2)}) collective-permute-start(bf16[128,8192]{1,0:T(8,128)(2,1)} %copy-done), channel_id=1, source_target_pairs={{0,8},{8,0},{16,24},{24,16},{32,40},{40,32},{48,56},{56,48},{1,9},... | collective-permute-start | bytes 6291464 | tf_op jit(solution)/shard_map/ppermute | solution.py:438
  125.3 8.3 %collective-permute-start.4 = (bf16[128,128]{1,0:T(8,128)(2,1)S(1)}, bf16[128,128]{1,0:T(8,128)(2,1)S(1)}, u32[]{:S(2)}, u32[]{:S(2)}) collective-permute-start(bf16[128,128]{1,0:T(8,128)(2,1)S(1)} %reduce_sum.12), channel_id=1, source_target_pairs={{0,64},{64,128},{128,192},{192,256},{256,320},{320,384},{384,448},... | collective-permute-start | bytes 98312 | tf_op jit(solution)/shard_map/ppermute | solution.py:447

commit v9 on v7

--- a/solution.py
+++ b/solution.py
@@ -96,14 +96,15 @@
 
 
 def attend_kernel(place_ref, q_ref, *refs):
-    kv_hbms = refs[:SHARE]
-    out_ref, kv_refs, sems, qa, point, acc, s_even, s_odd = refs[SHARE:]
+    own_ref, kv_hbms = refs[0], refs[1:SHARE]
+    out_ref, others, sems, qa, point, acc, s_even, s_odd = refs[SHARE:]
     copies = [
-        pltpu.make_async_copy(kv_hbms[block], kv_refs.at[block], sems.at[block])
-        for block in range(SHARE)
+        pltpu.make_async_copy(kv_hbms[block], others.at[block], sems.at[block])
+        for block in range(SHARE - 1)
     ]
     for copy in copies:
         copy.start()
+    kv_refs = [own_ref] + [others.at[block] for block in range(SHARE - 1)]
     odd = place_ref[SHARE]
     ids = q_ref[:, HEADS:SLAB, :].astype(F32).reshape(OWN * 8, HD).astype(BF)
     i, j = iota((KVH * OWN, OWN * 8), 0), iota((KVH * OWN, OWN * 8), 1)
@@ -137,10 +138,11 @@
     token_page, page_lane = iota((TOKENS, HD), 0) // PAGE, iota((TOKENS, HD), 1)
 
     def score(block, n):
-        if n == 0:
-            copies[block].wait()
+        if (block, n) == (1, 0):
+            for copy in copies:
+                copy.wait()
         keys = jnp.concatenate(
-            [kv_refs[block, 0], one_if(page_lane == token_page + block * POOL)], axis=1
+            [kv_refs[block][0], one_if(page_lane == token_page + block * POOL)], axis=1
         )
         return dot_nt(qa[n * CHUNK : (n + 1) * CHUNK, :], keys)
 
@@ -152,7 +154,7 @@
         new = jnp.maximum(jnp.broadcast_to(top.astype(BF).astype(F32), old.shape), old)
         point[here, :] = new
         p = jnp.exp2(s * (SCALE * LOG2E) - new[:, 0:1] * LOG2E).astype(BF)
-        o = dot(p, jnp.concatenate([kv_refs[block, 1], first_lane], axis=1))
+        o = dot(p, jnp.concatenate([kv_refs[block][1], first_lane], axis=1))
         fade = jnp.exp2((old - new) * LOG2E)
         acc[here, :] = acc[here, :] * jnp.concatenate([fade, fade], axis=1) + o
 
@@ -307,11 +309,11 @@
     return pl.pallas_call(
         attend_kernel,
         out_shape=jax.ShapeDtypeStruct((LINE, (LINE + 1) * OWN, HD), BF),
-        in_specs=[SMEM, VMEM] + [ANYWHERE] * SHARE,
+        in_specs=[SMEM, VMEM, VMEM] + [ANYWHERE] * (SHARE - 1),
         out_specs=VMEM,
         scratch_shapes=[
-            pltpu.VMEM((SHARE, 2, TOKENS, HD), BF),
-            pltpu.SemaphoreType.DMA((SHARE,)),
+            pltpu.VMEM((SHARE - 1, 2, TOKENS, HD), BF),
+            pltpu.SemaphoreType.DMA((SHARE - 1,)),
             pltpu.VMEM((HEADS * OWN, 2 * HD), BF),
             pltpu.VMEM((HEADS * OWN, HD), F32),
             pltpu.VMEM((HEADS * OWN, 2 * HD), F32),

time: 128 us -> 127 us (level)
  transfers between devices with their start and end apart: 6 -> 6, of which waited for: 2 -> 2; matrix products, arithmetic and copies ran while one was open for 0% -> 0% of each run, Pallas kernels for 9% -> 8%
where the time goes in v9:
time: 127 us; the launch traced here: 126 us
  blocking collectives  72.6 us (57%)
  starting transfers between devices  29.2 us (23%)
  Pallas kernels  15.3 us (12%)
  waiting for transfers between devices  7.03 us (6%)
  local copies, waits for them, and re-layouts  2.11 us (2%)
    all_to_all x5, blocking collectives, exchange(): lax.all_to_all(value, ('segment', 'dev'), split_axis=0, concat_axis=0, ax...  72.6 us
    all_to_all x1, starting transfers between devices, exchange(): lax.all_to_all(value, ('segment', 'dev'), split_axis=0, concat_axis=0, ax...  9.13 us
    pallas_call x1, Pallas kernels, attend(): pl.pallas_call(attend_kernel, out_shape=jax.ShapeDtypeStruct((LINE, (LINE...  7.64 us
    ppermute x1, starting transfers between devices, local(): lax.ppermute(projected, 'segment', [(s, (s + 1) % count) for s in range(c...  6.47 us
    all_to_all x1, waiting for transfers between devices, exchange(): lax.all_to_all(value, ('segment', 'dev'), split_axis=0, concat_axis=0, ax...  6 us
    ppermute x1, starting transfers between devices, local(): pages_b = lax.ppermute(pages, both, neighbours(other))  4.03 us
    ppermute x1, starting transfers between devices, local(): pages_u = lax.ppermute(pages, both, neighbours(one))  4 us
    ppermute x1, starting transfers between devices, local(): pages_ub = lax.ppermute(came_u, both, neighbours(other))  3.21 us
  transfers between devices with their start and end apart: 6, of which 2 were waited for; matrix products, arithmetic and copies ran while one was open for 0% of the time, Pallas kernels for 8%

profile of v9, /device:TPU:1, one launch (start us, length us, event | category | flops | bytes accessed | tf_op | source)
XLA Modules:
  0.0 126.4 jit_solution(6416652347925865265)
XLA Ops:
  0.0 1.7 %prepare.1 = (bf16[4,72,128]{2,1,0:T(8,128)(2,1)}, bf16[2,1024,128]{2,1,0:T(8,128)(2,1)S(1)}) custom-call(bf16[1,8192]{1,0:T(2,128)(2,1)} %q_hbm.1, s32[4,32]{1,0:T(4,128)} %bitcast.21, bf16[1024,128]{1,0:T(8,128)(2,1)} %bitcast.18, bf16[1024,128]{1,0:T(8,128)(2,1)} %bitcast.19), custom_call_target="tpu_custom_call" | custom-call | tf_op jit(solution)/shard_map/prepare/pallas_call | solution.py:265
  1.7 4.0 %collective-permute-start.1 = (bf16[2,1024,128]{2,1,0:T(8,128)(2,1)S(1)}, bf16[2,1024,128]{2,1,0:T(8,128)(2,1)S(1)}, u32[]{:S(2)}, u32[]{:S(2)}) collective-permute-start(bf16[2,1024,128]{2,1,0:T(8,128)(2,1)S(1)} %get-tuple-element.15.refs_0_), channel_id=1, source_target_pairs={{0,8},{8,0},{16,24},{24,16},{32,40},{40,32},{48,56},{56,48},{1,9},... | collective-permute-start | bytes 1572872 | tf_op jit(solution)/shard_map/ppermute | solution.py:415
  5.8 4.0 %collective-permute-start = (bf16[2,1024,128]{2,1,0:T(8,128)(2,1)S(1)}, bf16[2,1024,128]{2,1,0:T(8,128)(2,1)}, u32[]{:S(2)}, u32[]{:S(2)}) collective-permute-start(bf16[2,1024,128]{2,1,0:T(8,128)(2,1)S(1)} %get-tuple-element.15.refs_0_), channel_id=1, source_target_pairs={{0,1},{1,0},{2,3},{3,2},{4,5},{5,4},{6,7},{7,6},{8,9},{9,8},{10,11... | collective-permute-start | bytes 1572872 | tf_op jit(solution)/shard_map/ppermute | solution.py:414
  9.8 9.1 %all-to-all-start = ((bf16[4,72,128]{2,1,0:T(8,128)(2,1)}), bf16[4,72,128]{2,1,0:T(8,128)(2,1)S(1)}, u32[]{:S(2)}, u32[]{:S(2)}) async-start(bf16[4,72,128]{2,1,0:T(8,128)(2,1)} %get-tuple-element.14), calls=%async_computation | async-start | bytes 147456 | tf_op jit(solution)/shard_map/all_to_all | solution.py:381
  18.9 2.2 %halves.1 = (bf16[128,8192]{1,0:T(8,128)(2,1)S(1)}, bf16[128,8192]{1,0:T(8,128)(2,1)S(1)}) custom-call(s32[1]{0:T(128)} %bitcast.8.side_ref, bf16[128,16384]{1,0:T(8,128)(2,1)} %w_hbm.1), custom_call_target="tpu_custom_call" | custom-call | tf_op jit(solution)/shard_map/halves/pallas_call | solution.py:286
  21.2 0.0 copy-start
  21.2 1.3 %copy-done = bf16[128,8192]{1,0:T(8,128)(2,1)} copy-done((bf16[128,8192]{1,0:T(8,128)(2,1)}, bf16[128,8192]{1,0:T(8,128)(2,1)S(1)}, u32[]{:S(2)}) %copy-start) | copy-done | bytes 2097176
  22.5 6.0 %all-to-all-done.x_ref = bf16[4,72,128]{2,1,0:T(8,128)(2,1)S(1)} async-done(((bf16[4,72,128]{2,1,0:T(8,128)(2,1)}), bf16[4,72,128]{2,1,0:T(8,128)(2,1)S(1)}, u32[]{:S(2)}, u32[]{:S(2)}) %all-to-all-start) | async-done | bytes 73760 | tf_op jit(solution)/shard_map/all_to_all | solution.py:381
  28.5 0.0 collective-permute-done.1.refs_2_
  28.5 0.0 copy-start.1
  28.5 0.0 collective-permute-done.refs_1_
  28.5 3.2 %collective-permute-start.2 = (bf16[2,1024,128]{2,1,0:T(8,128)(2,1)}, bf16[2,1024,128]{2,1,0:T(8,128)(2,1)}, u32[]{:S(2)}, u32[]{:S(2)}) collective-permute-start(bf16[2,1024,128]{2,1,0:T(8,128)(2,1)} %collective-permute-done.refs_1_), channel_id=1, source_target_pairs={{0,8},{8,0},{16,24},{24,16},{32,40},{40,32},{48,56},{56,48},{1,9},... | collective-permute-start | bytes 1572872 | tf_op jit(solution)/shard_map/ppermute | solution.py:417
  31.8 15.2 %all_to_all.30 = bf16[4,4,72,128]{3,2,1,0:T(8,128)(2,1)S(1)} all-to-all(bf16[4,4,72,128]{3,2,1,0:T(8,128)(2,1)S(1)} %spread.1), channel_id=1, replica_groups={{0,16,32,48},{8,24,40,56},{1,17,33,49},{9,25,41,57},{2,18,34,50},{10,26..., dimensions={0} | all-to-all | bytes 589824 | tf_op jit(solution)/shard_map/all_to_all | solution.py:381
  47.0 0.0 collective-permute-done.2.refs_3_
  47.0 2.4 %collective-permute-start.3 = (bf16[128,8192]{1,0:T(8,128)(2,1)}, bf16[128,8192]{1,0:T(8,128)(2,1)}, u32[]{:S(2)}, u32[]{:S(2)}) collective-permute-start(bf16[128,8192]{1,0:T(8,128)(2,1)} %copy-done), channel_id=1, source_target_pairs={{0,8},{8,0},{16,24},{24,16},{32,40},{40,32},{48,56},{56,48},{1,9},... | collective-permute-start | bytes 6291464 | tf_op jit(solution)/shard_map/ppermute | solution.py:420
  49.4 0.1 stack.23.place_ref
  49.5 0.0 copy-done.1
  49.5 7.6 %attend.1 = bf16[8,144,128]{2,1,0:T(8,128)(2,1)S(1)} custom-call(s32[5]{0:T(128)S(1)} %stack.23.place_ref, bf16[16,72,128]{2,1,0:T(8,128)(2,1)S(1)} %bitcast.17, bf16[2,1024,128]{2,1,0:T(8,128)(2,1)S(1)} %get-tuple-element.15.refs_0_, bf16[2,1024,128]{2,1,0:T(8,128)(2,1)} %collective-permute-done.refs_1_, bf16[2,1024,128]{2,1,0:T(8,128)(2,1)} %copy-done.1, ...), custom_call_target="tpu_custom_call" | custom-call | tf_op jit(solution)/shard_map/attend/pallas_call | solution.py:309
  57.1 14.6 %all_to_all.31.r_ref = bf16[8,144,128]{2,1,0:T(8,128)(2,1)S(1)} all-to-all(bf16[8,144,128]{2,1,0:T(8,128)(2,1)S(1)} %attend.1), channel_id=1, replica_groups={{0,1,2,3,4,5,6,7},{8,9,10,11,12,13,14,15},{16,17,18,19,20,21,22,23},{24..., dimensions={0} | all-to-all | bytes 589824 | tf_op jit(solution)/shard_map/all_to_all | solution.py:381
  71.8 0.3 merge.1
  72.1 10.7 %all_to_all.32.r_ref = bf16[8,2,40,128]{3,2,1,0:T(8,128)(2,1)S(1)} all-to-all(bf16[8,2,40,128]{3,2,1,0:T(8,128)(2,1)S(1)} %merge.1), channel_id=1, replica_groups={{0,8,16,24,32,40,48,56},{1,9,17,25,33,41,49,57},{2,10,18,26,34,42,50,58..., dimensions={0} | all-to-all | bytes 327680 | tf_op jit(solution)/shard_map/all_to_all | solution.py:381
  82.8 0.0 collective-permute-done.3.theirs_hbm
  82.8 3.0 %project.1 = bf16[64,8192]{1,0:T(8,128)(2,1)S(1)} custom-call(bf16[8,2,40,128]{3,2,1,0:T(8,128)(2,1)S(1)} %all_to_all.32.r_ref, bf16[128,8192]{1,0:T(8,128)(2,1)S(1)} %get-tuple-element.21.mine_ref, bf16[128,8192]{1,0:T(8,128)(2,1)} %collective-permute-done.3.theirs_hbm), custom_call_target="tpu_custom_call" | custom-call | tf_op jit(solution)/shard_map/project/pallas_call | solution.py:341
  85.8 20.2 %all_to_all.33.x_ref = bf16[8,8,8192]{2,1,0:T(8,128)(2,1)S(1)} all-to-all(bf16[8,8,8192]{2,1,0:T(8,128)(2,1)S(1)} %bitcast.16), channel_id=1, replica_groups={{0,8,16,24,32,40,48,56},{1,9,17,25,33,41,49,57},{2,10,18,26,34,42,50,58..., dimensions={0} | all-to-all | bytes 2097152 | tf_op jit(solution)/shard_map/all_to_all | solution.py:381
  105.9 0.3 add.48
  106.3 12.0 %all_to_all.34 = bf16[8,128,128]{2,1,0:T(8,128)(2,1)S(1)} all-to-all(bf16[8,128,128]{2,1,0:T(8,128)(2,1)S(1)} %add.48), channel_id=1, replica_groups={{0,1,2,3,4,5,6,7},{8,9,10,11,12,13,14,15},{16,17,18,19,20,21,22,23},{24..., dimensions={0} | all-to-all | bytes 524288 | tf_op jit(solution)/shard_map/all_to_all | solution.py:381
  118.3 6.5 %collective-permute-start.4 = (bf16[128,128]{1,0:T(8,128)(2,1)S(1)}, bf16[128,128]{1,0:T(8,128)(2,1)S(1)}, u32[]{:S(2)}, u32[]{:S(2)}) collective-permute-start(bf16[128,128]{1,0:T(8,128)(2,1)S(1)} %reduce_sum.12), channel_id=1, source_target_pairs={{0,64},{64,128},{128,192},{192,256},{256,320},{320,384},{384,448},... | collective-permute-start | bytes 98312 | tf_op jit(solution)/shard_map/ppermute | solution.py:429
  124.7 1.0 collective-permute-done.4
  125.8 0.7 copy.8
  (2 shorter events, 0.1 us)
Async XLA Ops:
  1.7 26.8 %collective-permute-start.1 = (bf16[2,1024,128]{2,1,0:T(8,128)(2,1)S(1)}, bf16[2,1024,128]{2,1,0:T(8,128)(2,1)S(1)}, u32[]{:S(2)}, u32[]{:S(2)}) collective-permute-start(bf16[2,1024,128]{2,1,0:T(8,128)(2,1)S(1)} %get-tuple-element.15.refs_0_), channel_id=1, source_target_pairs={{0,8},{8,0},{16,24},{24,16},{32,40},{40,32},{48,56},{56,48},{1,9},... | collective-permute-start | bytes 1572872 | tf_op jit(solution)/shard_map/ppermute | solution.py:415
  5.8 22.7 %collective-permute-start = (bf16[2,1024,128]{2,1,0:T(8,128)(2,1)S(1)}, bf16[2,1024,128]{2,1,0:T(8,128)(2,1)}, u32[]{:S(2)}, u32[]{:S(2)}) collective-permute-start(bf16[2,1024,128]{2,1,0:T(8,128)(2,1)S(1)} %get-tuple-element.15.refs_0_), channel_id=1, source_target_pairs={{0,1},{1,0},{2,3},{3,2},{4,5},{5,4},{6,7},{7,6},{8,9},{9,8},{10,11... | collective-permute-start | bytes 1572872 | tf_op jit(solution)/shard_map/ppermute | solution.py:414
  9.8 18.7 %all-to-all-start = ((bf16[4,72,128]{2,1,0:T(8,128)(2,1)}), bf16[4,72,128]{2,1,0:T(8,128)(2,1)S(1)}, u32[]{:S(2)}, u32[]{:S(2)}) async-start(bf16[4,72,128]{2,1,0:T(8,128)(2,1)} %get-tuple-element.14), calls=%async_computation | async-start | bytes 147456 | tf_op jit(solution)/shard_map/all_to_all | solution.py:381
  21.2 1.3 %copy-start = (bf16[128,8192]{1,0:T(8,128)(2,1)}, bf16[128,8192]{1,0:T(8,128)(2,1)S(1)}, u32[]{:S(2)}) copy-start(bf16[128,8192]{1,0:T(8,128)(2,1)S(1)} %get-tuple-element.22) | copy-start | bytes 6291460
  28.5 21.0 %copy-start.1 = (bf16[2,1024,128]{2,1,0:T(8,128)(2,1)}, bf16[2,1024,128]{2,1,0:T(8,128)(2,1)S(1)}, u32[]{:S(2)}) copy-start(bf16[2,1024,128]{2,1,0:T(8,128)(2,1)S(1)} %collective-permute-done.1.refs_2_) | copy-start | bytes 1572868
  28.5 18.5 %collective-permute-start.2 = (bf16[2,1024,128]{2,1,0:T(8,128)(2,1)}, bf16[2,1024,128]{2,1,0:T(8,128)(2,1)}, u32[]{:S(2)}, u32[]{:S(2)}) collective-permute-start(bf16[2,1024,128]{2,1,0:T(8,128)(2,1)} %collective-permute-done.refs_1_), channel_id=1, source_target_pairs={{0,8},{8,0},{16,24},{24,16},{32,40},{40,32},{48,56},{56,48},{1,9},... | collective-permute-start | bytes 1572872 | tf_op jit(solution)/shard_map/ppermute | solution.py:417
  47.0 35.8 %collective-permute-start.3 = (bf16[128,8192]{1,0:T(8,128)(2,1)}, bf16[128,8192]{1,0:T(8,128)(2,1)}, u32[]{:S(2)}, u32[]{:S(2)}) collective-permute-start(bf16[128,8192]{1,0:T(8,128)(2,1)} %copy-done), channel_id=1, source_target_pairs={{0,8},{8,0},{16,24},{24,16},{32,40},{40,32},{48,56},{56,48},{1,9},... | collective-permute-start | bytes 6291464 | tf_op jit(solution)/shard_map/ppermute | solution.py:420
  118.3 7.5 %collective-permute-start.4 = (bf16[128,128]{1,0:T(8,128)(2,1)S(1)}, bf16[128,128]{1,0:T(8,128)(2,1)S(1)}, u32[]{:S(2)}, u32[]{:S(2)}) collective-permute-start(bf16[128,128]{1,0:T(8,128)(2,1)S(1)} %reduce_sum.12), channel_id=1, source_target_pairs={{0,64},{64,128},{128,192},{192,256},{256,320},{320,384},{384,448},... | collective-permute-start | bytes 98312 | tf_op jit(solution)/shard_map/ppermute | solution.py:429

commit v10 on v9

--- a/solution.py
+++ b/solution.py
@@ -417,9 +417,10 @@
     pages_ub = lax.ppermute(came_u, both, neighbours(other))
     got = exchange(spread(near), other_rows)
     given, got, _ = lax.optimization_barrier((given, got, pages_ub))
+
+    partial = attend(place, got.reshape(OWN, SLAB, HD), [pages, pages_u, pages_b, pages_ub])
+    given, partial = lax.optimization_barrier((given, partial))
     theirs = lax.ppermute(given, both, neighbours(other))
-
-    partial = attend(place, got.reshape(OWN, SLAB, HD), [pages, pages_u, pages_b, pages_ub])
     joined = merge(exchange(partial, one))
     gathered = exchange(joined, other)
     sums = project(gathered, mine, theirs)

time: 127 us -> 132 us (1.039)
  waiting for transfers between devices: 7.03 us -> 15.5 us
  blocking collectives: 72.6 us -> 64.5 us
  starting transfers between devices: 29.2 us -> 34.5 us
    all_to_all x1 -> x2, waiting for transfers between devices: 6 us -> 14.4 us  [exchange(): lax.all_to_all(value, ('segment', 'dev'), split_axis=0, concat_axis=0, ax...]
    all_to_all x5 -> x4, blocking collectives: 72.6 us -> 64.5 us  [exchange(): lax.all_to_all(value, ('segment', 'dev'), split_axis=0, concat_axis=0, ax...]
    all_to_all x1 -> x2, starting transfers between devices: 9.13 us -> 15 us  [exchange(): lax.all_to_all(value, ('segment', 'dev'), split_axis=0, concat_axis=0, ax...]
    ppermute x1, starting transfers between devices: 6.47 us -> 4.78 us  [local(): lax.ppermute(projected, 'segment', [(s, (s + 1) % count) for s in range(c...]
  transfers between devices with their start and end apart: 6 -> 7, of which waited for: 2 -> 3; matrix products, arithmetic and copies ran while one was open for 0% -> 0% of each run, Pallas kernels for 8% -> 3%
where the time goes in v10:
time: 132 us
  blocking collectives  64.5 us (49%)
  starting transfers between devices  34.5 us (26%)
  waiting for transfers between devices  15.5 us (12%)
  Pallas kernels  14.7 us (11%)
  local copies, waits for them, and re-layouts  2.09 us (2%)
    all_to_all x4, blocking collectives, exchange(): lax.all_to_all(value, ('segment', 'dev'), split_axis=0, concat_axis=0, ax...  64.5 us
    all_to_all x2, starting transfers between devices, exchange(): lax.all_to_all(value, ('segment', 'dev'), split_axis=0, concat_axis=0, ax...  15 us
    all_to_all x2, waiting for transfers between devices, exchange(): lax.all_to_all(value, ('segment', 'dev'), split_axis=0, concat_axis=0, ax...  14.4 us
    pallas_call x1, Pallas kernels, attend(): pl.pallas_call(attend_kernel, out_shape=jax.ShapeDtypeStruct((LINE, (LINE...  7.64 us
    ppermute x1, starting transfers between devices, local(): lax.ppermute(projected, 'segment', [(s, (s + 1) % count) for s in range(c...  4.78 us
    ppermute x1, starting transfers between devices, local(): pages_b = lax.ppermute(pages, both, neighbours(other))  4.03 us
    ppermute x1, starting transfers between devices, local(): pages_u = lax.ppermute(pages, both, neighbours(one))  4 us
    ppermute x1, starting transfers between devices, local(): theirs = lax.ppermute(given, both, neighbours(other))  3.48 us
  transfers between devices with their start and end apart: 7, of which 3 were waited for; matrix products, arithmetic and copies ran while one was open for 0% of the time, Pallas kernels for 3%

profile of v10, /device:TPU:1, one launch (start us, length us, event | category | flops | bytes accessed | tf_op | source)
XLA Modules:
  0.0 131.5 jit_solution(4920140787688964006)
XLA Ops:
  0.0 1.7 %prepare.1 = (bf16[4,72,128]{2,1,0:T(8,128)(2,1)}, bf16[2,1024,128]{2,1,0:T(8,128)(2,1)S(1)}) custom-call(bf16[1,8192]{1,0:T(2,128)(2,1)} %q_hbm.1, s32[4,32]{1,0:T(4,128)} %bitcast.21, bf16[1024,128]{1,0:T(8,128)(2,1)} %bitcast.18, bf16[1024,128]{1,0:T(8,128)(2,1)} %bitcast.19), custom_call_target="tpu_custom_call" | custom-call | tf_op jit(solution)/shard_map/prepare/pallas_call | solution.py:265
  1.7 4.0 %collective-permute-start.1 = (bf16[2,1024,128]{2,1,0:T(8,128)(2,1)S(1)}, bf16[2,1024,128]{2,1,0:T(8,128)(2,1)S(1)}, u32[]{:S(2)}, u32[]{:S(2)}) collective-permute-start(bf16[2,1024,128]{2,1,0:T(8,128)(2,1)S(1)} %get-tuple-element.17.refs_0_), channel_id=1, source_target_pairs={{0,8},{8,0},{16,24},{24,16},{32,40},{40,32},{48,56},{56,48},{1,9},... | collective-permute-start | bytes 1572872 | tf_op jit(solution)/shard_map/ppermute | solution.py:415
  5.8 4.0 %collective-permute-start = (bf16[2,1024,128]{2,1,0:T(8,128)(2,1)S(1)}, bf16[2,1024,128]{2,1,0:T(8,128)(2,1)}, u32[]{:S(2)}, u32[]{:S(2)}) collective-permute-start(bf16[2,1024,128]{2,1,0:T(8,128)(2,1)S(1)} %get-tuple-element.17.refs_0_), channel_id=1, source_target_pairs={{0,1},{1,0},{2,3},{3,2},{4,5},{5,4},{6,7},{7,6},{8,9},{9,8},{10,11... | collective-permute-start | bytes 1572872 | tf_op jit(solution)/shard_map/ppermute | solution.py:414
  9.8 9.1 %all-to-all-start = ((bf16[4,72,128]{2,1,0:T(8,128)(2,1)}), bf16[4,72,128]{2,1,0:T(8,128)(2,1)S(1)}, u32[]{:S(2)}, u32[]{:S(2)}) async-start(bf16[4,72,128]{2,1,0:T(8,128)(2,1)} %get-tuple-element.16), calls=%async_computation | async-start | bytes 147456 | tf_op jit(solution)/shard_map/all_to_all | solution.py:381
  18.9 2.2 %halves.1 = (bf16[128,8192]{1,0:T(8,128)(2,1)S(1)}, bf16[128,8192]{1,0:T(8,128)(2,1)S(1)}) custom-call(s32[1]{0:T(128)} %bitcast.3.side_ref, bf16[128,16384]{1,0:T(8,128)(2,1)} %w_hbm.1), custom_call_target="tpu_custom_call" | custom-call | tf_op jit(solution)/shard_map/halves/pallas_call | solution.py:286
  21.2 0.0 copy-start
  21.2 1.3 %copy-done = bf16[128,8192]{1,0:T(8,128)(2,1)} copy-done((bf16[128,8192]{1,0:T(8,128)(2,1)}, bf16[128,8192]{1,0:T(8,128)(2,1)S(1)}, u32[]{:S(2)}) %copy-start) | copy-done | bytes 2097176
  22.5 6.0 %all-to-all-done.x_ref = bf16[4,72,128]{2,1,0:T(8,128)(2,1)S(1)} async-done(((bf16[4,72,128]{2,1,0:T(8,128)(2,1)}), bf16[4,72,128]{2,1,0:T(8,128)(2,1)S(1)}, u32[]{:S(2)}, u32[]{:S(2)}) %all-to-all-start) | async-done | bytes 73760 | tf_op jit(solution)/shard_map/all_to_all | solution.py:381
  28.5 0.0 collective-permute-done.1.refs_2_
  28.5 0.0 copy-start.2
  28.5 0.0 collective-permute-done.refs_1_
  28.5 3.2 %collective-permute-start.2 = (bf16[2,1024,128]{2,1,0:T(8,128)(2,1)}, bf16[2,1024,128]{2,1,0:T(8,128)(2,1)}, u32[]{:S(2)}, u32[]{:S(2)}) collective-permute-start(bf16[2,1024,128]{2,1,0:T(8,128)(2,1)} %collective-permute-done.refs_1_), channel_id=1, source_target_pairs={{0,8},{8,0},{16,24},{24,16},{32,40},{40,32},{48,56},{56,48},{1,9},... | collective-permute-start | bytes 1572872 | tf_op jit(solution)/shard_map/ppermute | solution.py:417
  31.7 0.8 spread.1
  32.5 5.9 %all-to-all-start.1 = ((bf16[4,4,72,128]{3,2,1,0:T(8,128)(2,1)}), bf16[4,4,72,128]{3,2,1,0:T(8,128)(2,1)S(1)}, u32[]{:S(2)}, u32[]{:S(2)}) async-start(bf16[4,4,72,128]{3,2,1,0:T(8,128)(2,1)} %spread.1), calls=%async_computation.1 | async-start | bytes 589824 | tf_op jit(solution)/shard_map/all_to_all | solution.py:381
  38.4 0.1 stack.23.place_ref
  38.5 8.4 %all-to-all-done.1 = bf16[4,4,72,128]{3,2,1,0:T(8,128)(2,1)S(1)} async-done(((bf16[4,4,72,128]{3,2,1,0:T(8,128)(2,1)}), bf16[4,4,72,128]{3,2,1,0:T(8,128)(2,1)S(1)}, u32[]{:S(2)}, u32[]{:S(2)}) %all-to-all-start.1) | async-done | bytes 294944 | tf_op jit(solution)/shard_map/all_to_all | solution.py:381
  46.9 0.0 copy-start.1
  46.9 0.0 collective-permute-done.2.refs_3_
  46.9 0.0 copy-done.2
  46.9 7.6 %attend.1 = bf16[8,144,128]{2,1,0:T(8,128)(2,1)S(1)} custom-call(s32[5]{0:T(128)S(1)} %stack.23.place_ref, bf16[16,72,128]{2,1,0:T(8,128)(2,1)S(1)} %bitcast.17, bf16[2,1024,128]{2,1,0:T(8,128)(2,1)S(1)} %get-tuple-element.17.refs_0_, bf16[2,1024,128]{2,1,0:T(8,128)(2,1)} %collective-permute-done.refs_1_, bf16[2,1024,128]{2,1,0:T(8,128)(2,1)} %copy-done.2, ...), custom_call_target="tpu_custom_call" | custom-call | tf_op jit(solution)/shard_map/attend/pallas_call | solution.py:309
  54.6 0.0 copy-done.1
  54.6 3.5 %collective-permute-start.3 = (bf16[128,8192]{1,0:T(8,128)(2,1)S(1)}, bf16[128,8192]{1,0:T(8,128)(2,1)S(1)}, u32[]{:S(2)}, u32[]{:S(2)}) collective-permute-start(bf16[128,8192]{1,0:T(8,128)(2,1)S(1)} %copy-done.1), channel_id=1, source_target_pairs={{0,8},{8,0},{16,24},{24,16},{32,40},{40,32},{48,56},{56,48},{1,9},... | collective-permute-start | bytes 6291464 | tf_op jit(solution)/shard_map/ppermute | solution.py:423
  58.1 14.5 %all_to_all.30.r_ref = bf16[8,144,128]{2,1,0:T(8,128)(2,1)S(1)} all-to-all(bf16[8,144,128]{2,1,0:T(8,128)(2,1)S(1)} %attend.1), channel_id=1, replica_groups={{0,1,2,3,4,5,6,7},{8,9,10,11,12,13,14,15},{16,17,18,19,20,21,22,23},{24..., dimensions={0} | all-to-all | bytes 589824 | tf_op jit(solution)/shard_map/all_to_all | solution.py:381
  72.6 0.3 merge.1
  72.9 14.3 %all_to_all.31.r_ref = bf16[8,2,40,128]{3,2,1,0:T(8,128)(2,1)S(1)} all-to-all(bf16[8,2,40,128]{3,2,1,0:T(8,128)(2,1)S(1)} %merge.1), channel_id=1, replica_groups={{0,8,16,24,32,40,48,56},{1,9,17,25,33,41,49,57},{2,10,18,26,34,42,50,58..., dimensions={0} | all-to-all | bytes 327680 | tf_op jit(solution)/shard_map/all_to_all | solution.py:381
  87.2 0.0 collective-permute-done.3.theirs_hbm
  87.2 1.7 %project.1 = bf16[64,8192]{1,0:T(8,128)(2,1)S(1)} custom-call(bf16[8,2,40,128]{3,2,1,0:T(8,128)(2,1)S(1)} %all_to_all.31.r_ref, bf16[128,8192]{1,0:T(8,128)(2,1)S(1)} %get-tuple-element.25.mine_ref, bf16[128,8192]{1,0:T(8,128)(2,1)S(1)} %collective-permute-done.3.theirs_hbm), custom_call_target="tpu_custom_call" | custom-call | tf_op jit(solution)/shard_map/project/pallas_call | solution.py:341
  88.9 23.4 %all_to_all.32.x_ref = bf16[8,8,8192]{2,1,0:T(8,128)(2,1)S(1)} all-to-all(bf16[8,8,8192]{2,1,0:T(8,128)(2,1)S(1)} %bitcast.16), channel_id=1, replica_groups={{0,8,16,24,32,40,48,56},{1,9,17,25,33,41,49,57},{2,10,18,26,34,42,50,58..., dimensions={0} | all-to-all | bytes 2097152 | tf_op jit(solution)/shard_map/all_to_all | solution.py:381
  112.3 0.3 add.48
  112.6 12.4 %all_to_all.33 = bf16[8,128,128]{2,1,0:T(8,128)(2,1)S(1)} all-to-all(bf16[8,128,128]{2,1,0:T(8,128)(2,1)S(1)} %add.48), channel_id=1, replica_groups={{0,1,2,3,4,5,6,7},{8,9,10,11,12,13,14,15},{16,17,18,19,20,21,22,23},{24..., dimensions={0} | all-to-all | bytes 524288 | tf_op jit(solution)/shard_map/all_to_all | solution.py:381
  125.0 4.8 %collective-permute-start.4 = (bf16[128,128]{1,0:T(8,128)(2,1)S(1)}, bf16[128,128]{1,0:T(8,128)(2,1)S(1)}, u32[]{:S(2)}, u32[]{:S(2)}) collective-permute-start(bf16[128,128]{1,0:T(8,128)(2,1)S(1)} %reduce_sum.12), channel_id=1, source_target_pairs={{0,64},{64,128},{128,192},{192,256},{256,320},{320,384},{384,448},... | collective-permute-start | bytes 98312 | tf_op jit(solution)/shard_map/ppermute | solution.py:430
  129.8 1.0 collective-permute-done.4
  130.8 0.7 copy.8
  (1 shorter events, 0.0 us)
Async XLA Ops:
  1.7 26.8 %collective-permute-start.1 = (bf16[2,1024,128]{2,1,0:T(8,128)(2,1)S(1)}, bf16[2,1024,128]{2,1,0:T(8,128)(2,1)S(1)}, u32[]{:S(2)}, u32[]{:S(2)}) collective-permute-start(bf16[2,1024,128]{2,1,0:T(8,128)(2,1)S(1)} %get-tuple-element.17.refs_0_), channel_id=1, source_target_pairs={{0,8},{8,0},{16,24},{24,16},{32,40},{40,32},{48,56},{56,48},{1,9},... | collective-permute-start | bytes 1572872 | tf_op jit(solution)/shard_map/ppermute | solution.py:415
  5.8 22.7 %collective-permute-start = (bf16[2,1024,128]{2,1,0:T(8,128)(2,1)S(1)}, bf16[2,1024,128]{2,1,0:T(8,128)(2,1)}, u32[]{:S(2)}, u32[]{:S(2)}) collective-permute-start(bf16[2,1024,128]{2,1,0:T(8,128)(2,1)S(1)} %get-tuple-element.17.refs_0_), channel_id=1, source_target_pairs={{0,1},{1,0},{2,3},{3,2},{4,5},{5,4},{6,7},{7,6},{8,9},{9,8},{10,11... | collective-permute-start | bytes 1572872 | tf_op jit(solution)/shard_map/ppermute | solution.py:414
  9.8 18.7 %all-to-all-start = ((bf16[4,72,128]{2,1,0:T(8,128)(2,1)}), bf16[4,72,128]{2,1,0:T(8,128)(2,1)S(1)}, u32[]{:S(2)}, u32[]{:S(2)}) async-start(bf16[4,72,128]{2,1,0:T(8,128)(2,1)} %get-tuple-element.16), calls=%async_computation | async-start | bytes 147456 | tf_op jit(solution)/shard_map/all_to_all | solution.py:381
  21.2 1.3 %copy-start = (bf16[128,8192]{1,0:T(8,128)(2,1)}, bf16[128,8192]{1,0:T(8,128)(2,1)S(1)}, u32[]{:S(2)}) copy-start(bf16[128,8192]{1,0:T(8,128)(2,1)S(1)} %get-tuple-element.26) | copy-start | bytes 6291460
  28.5 18.4 %copy-start.2 = (bf16[2,1024,128]{2,1,0:T(8,128)(2,1)}, bf16[2,1024,128]{2,1,0:T(8,128)(2,1)S(1)}, u32[]{:S(2)}) copy-start(bf16[2,1024,128]{2,1,0:T(8,128)(2,1)S(1)} %collective-permute-done.1.refs_2_) | copy-start | bytes 1572868
  28.5 18.4 %collective-permute-start.2 = (bf16[2,1024,128]{2,1,0:T(8,128)(2,1)}, bf16[2,1024,128]{2,1,0:T(8,128)(2,1)}, u32[]{:S(2)}, u32[]{:S(2)}) collective-permute-start(bf16[2,1024,128]{2,1,0:T(8,128)(2,1)} %collective-permute-done.refs_1_), channel_id=1, source_target_pairs={{0,8},{8,0},{16,24},{24,16},{32,40},{40,32},{48,56},{56,48},{1,9},... | collective-permute-start | bytes 1572872 | tf_op jit(solution)/shard_map/ppermute | solution.py:417
  32.5 14.4 %all-to-all-start.1 = ((bf16[4,4,72,128]{3,2,1,0:T(8,128)(2,1)}), bf16[4,4,72,128]{3,2,1,0:T(8,128)(2,1)S(1)}, u32[]{:S(2)}, u32[]{:S(2)}) async-start(bf16[4,4,72,128]{3,2,1,0:T(8,128)(2,1)} %spread.1), calls=%async_computation.1 | async-start | bytes 589824 | tf_op jit(solution)/shard_map/all_to_all | solution.py:381
  46.9 7.7 %copy-start.1 = (bf16[128,8192]{1,0:T(8,128)(2,1)S(1)}, bf16[128,8192]{1,0:T(8,128)(2,1)}, u32[]{:S(2)}) copy-start(bf16[128,8192]{1,0:T(8,128)(2,1)} %copy-done) | copy-start | bytes 6291460
  54.6 32.6 %collective-permute-start.3 = (bf16[128,8192]{1,0:T(8,128)(2,1)S(1)}, bf16[128,8192]{1,0:T(8,128)(2,1)S(1)}, u32[]{:S(2)}, u32[]{:S(2)}) collective-permute-start(bf16[128,8192]{1,0:T(8,128)(2,1)S(1)} %copy-done.1), channel_id=1, source_target_pairs={{0,8},{8,0},{16,24},{24,16},{32,40},{40,32},{48,56},{56,48},{1,9},... | collective-permute-start | bytes 6291464 | tf_op jit(solution)/shard_map/ppermute | solution.py:423
  125.0 5.8 %collective-permute-start.4 = (bf16[128,128]{1,0:T(8,128)(2,1)S(1)}, bf16[128,128]{1,0:T(8,128)(2,1)S(1)}, u32[]{:S(2)}, u32[]{:S(2)}) collective-permute-start(bf16[128,128]{1,0:T(8,128)(2,1)S(1)} %reduce_sum.12), channel_id=1, source_target_pairs={{0,64},{64,128},{128,192},{192,256},{256,320},{320,384},{384,448},... | collective-permute-start | bytes 98312 | tf_op jit(solution)/shard_map/ppermute | solution.py:430
